TPU v7x, 256 devices: a whole 4x4x8 slice. The times are simulated.
256 devices in a mesh: fsdp: 128 (over y, x_lo, z, core), seq: 2 (over x_hi).
Axes of the slice: x: 4 (x_hi: 2, x_lo: 2; x = x_hi * 2 + x_lo), y: 4, z: 8, core: 2. Of those that a mesh axis runs over, the one named last changes fastest.
Arguments:
- tokens: bfloat16 [16384, 8192], P('fsdp', 'seq'), may hold values from -6 to 6
- weight: bfloat16 [1024, 8192], P('fsdp', 'seq'), may hold values from -0.0625 to 0.0625
- bias: float32 [1024], P('seq'), may hold values from -3 to 3
- adapter_down: bfloat16 [8192, 512, 64], P('seq', 'fsdp'), may hold values from -0.0625 to 0.0625
- adapter_up: bfloat16 [512, 64, 1024], P('fsdp', None, 'seq'), may hold values from -0.75 to 0.75
- cotangent: bfloat16 [16384, 1024], P('fsdp', 'seq'), may hold values from -6 to 6
- block_task: int32 [8192], P('fsdp'), may hold values from 0 to 511, as said below
- owner_slot: int32 [512], replicated, may hold values from 0 to 511, as said below
Outputs:
- projected: bfloat16 [16384, 1024], P('fsdp', 'seq')
- grad_tokens: bfloat16 [16384, 8192], P('fsdp', 'seq')
- down_gradient: float32 [8192, 512, 64], P('seq', 'fsdp')
- up_gradient: float32 [512, 64, 1024], P('fsdp', None, 'seq')
Inputs may be any that keep to these rules, and one draw needn't show every extreme that they name: `block_task`: within one index of fsdp (aligned runs of 64 entries) the blocks name tasks whose owner devices owner_slot[task] // 4 all differ. `owner_slot`: A permutation; slot s is held by index s // 4 of fsdp.
All inputs are finite; a program needn't handle non-finite values.
Results may differ from a plain program's by a relative error of at most 0.0036.
Values may be sent and summed in bfloat16 or wider, within the bound.
No kernel may reach another device: no remote copies, remote signals or barrier semaphores. Data moves between devices by JAX's collectives and lax.ppermute only.
A program may use at most 128 MiB of HBM per device.

v0:
```python
import jax
import jax.numpy as jnp
from jax import lax
from jax.sharding import PartitionSpec as P

adapter_scale = 0.5


def contract_product(left, right, left_dim, right_dim):
    return lax.dot_general(
        left, right, (((left_dim,), (right_dim,)), ((), ())), preferred_element_type=jnp.float32
    )


def on_device(tokens, weight, bias, adapter_down, adapter_up, cotangent, block_task, owner_slot):
    tok_rows, half_width = tokens.shape
    owning_count = lax.axis_size("fsdp")
    blocks_dev = block_task.shape[0]
    rows_per_block = tok_rows // blocks_dev
    task_dev = adapter_up.shape[0]
    low_rank = adapter_up.shape[1]
    key_portion = adapter_up.shape[2]
    tasks_all = owner_slot.shape[0]
    match_task = block_task[:, None] == jnp.arange(tasks_all, dtype=jnp.int32)[None, :]
    slot_of = jnp.sum(jnp.where(match_task, owner_slot[None, :], 0), axis=1)
    owner_of = slot_of // task_dev
    inner_of = slot_of % task_dev
    match_owner = owner_of[None, :] == jnp.arange(owning_count, dtype=jnp.int32)[:, None]
    filled = jnp.any(match_owner, axis=1)
    block_pick = jnp.sum(
        jnp.where(match_owner, jnp.arange(blocks_dev, dtype=jnp.int32)[None, :], 0), axis=1
    )
    slot_table = jnp.where(filled, block_pick, blocks_dev)

    def pack_rows(rows):
        row_width = rows.shape[1]
        blocks = rows.reshape(blocks_dev, rows_per_block, row_width)
        padded = jnp.concatenate(
            [blocks, jnp.zeros((1, rows_per_block, row_width), rows.dtype)], axis=0
        )
        return padded[slot_table]

    def unpacked_rows(returned):
        return returned[owner_of].reshape(tok_rows, returned.shape[2])

    labels = jnp.concatenate([inner_of.astype(jnp.float32), jnp.full((1,), -1.0, jnp.float32)])[
        slot_table
    ]
    labels = labels.astype(jnp.bfloat16)
    down_local = adapter_down.reshape(half_width, task_dev * low_rank)
    local_up_weight = adapter_up.reshape(task_dev * low_rank, key_portion)

    def collapse(partial_value, indicator_mask):
        return jnp.sum(
            partial_value.reshape(-1, task_dev, low_rank) * indicator_mask[:, :, None], axis=1
        )

    def spread_rows(low_rows, indicator_mask):
        wide = low_rows[:, None, :].astype(jnp.float32) * indicator_mask[:, :, None]
        return wide.reshape(-1, task_dev * low_rank).astype(jnp.bfloat16)

    rows_in, labels_in = (
        lax.all_to_all(pack_rows(tokens), "fsdp", split_axis=0, concat_axis=0, tiled=True),
        lax.all_to_all(labels, "fsdp", split_axis=0, concat_axis=0, tiled=True),
    )
    label_rows = jnp.repeat(labels_in.astype(jnp.float32), rows_per_block)
    indicator_mask = (
        label_rows[:, None] == jnp.arange(task_dev, dtype=jnp.float32)[None, :]
    ).astype(jnp.float32)
    owner_rows = rows_in.reshape(-1, half_width)
    low_sum = lax.psum(
        collapse(
            jnp.dot(owner_rows, down_local, preferred_element_type=jnp.float32), indicator_mask
        ),
        "seq",
    )
    broad_reduced = spread_rows(low_sum.astype(jnp.bfloat16), indicator_mask)
    adapter_output = (
        adapter_scale * jnp.dot(broad_reduced, local_up_weight, preferred_element_type=jnp.float32)
    ).astype(jnp.bfloat16)
    adapter_backward = lax.all_to_all(
        adapter_output.reshape(owning_count, rows_per_block, key_portion),
        "fsdp",
        split_axis=0,
        concat_axis=0,
        tiled=True,
    )
    grads_in = lax.all_to_all(pack_rows(cotangent), "fsdp", split_axis=0, concat_axis=0, tiled=True)
    owning_gradient = grads_in.reshape(-1, key_portion)
    gradient_total = lax.psum(
        collapse(contract_product(owning_gradient, local_up_weight, 1, 1), indicator_mask), "seq"
    )
    broad_gradient = spread_rows(
        (adapter_scale * gradient_total).astype(jnp.bfloat16), indicator_mask
    )
    up_gradient = (adapter_scale * contract_product(broad_reduced, owning_gradient, 0, 0)).reshape(
        task_dev, low_rank, key_portion
    )
    down_gradient = contract_product(owner_rows, broad_gradient, 0, 0).reshape(
        half_width, task_dev, low_rank
    )
    returned_rows = contract_product(broad_gradient, down_local, 1, 1).astype(jnp.bfloat16)
    down_gradient, up_gradient, back_blocks = (
        down_gradient,
        up_gradient,
        returned_rows.reshape(owning_count, rows_per_block, half_width),
    )
    grads_back = lax.all_to_all(back_blocks, "fsdp", split_axis=0, concat_axis=0, tiled=True)
    full_grads = lax.all_gather(cotangent, "seq", axis=1, tiled=True)
    full_weight = lax.all_gather(weight, "fsdp", axis=0, tiled=True)
    base_part = contract_product(tokens, full_weight, 1, 1)
    base_grad = jnp.dot(full_grads, full_weight, preferred_element_type=jnp.float32)
    frozen_half = lax.psum_scatter(base_part, "seq", scatter_dimension=1, tiled=True)
    projected = (
        frozen_half + bias[None, :] + unpacked_rows(adapter_backward).astype(jnp.float32)
    ).astype(jnp.bfloat16)
    grad_tokens = (base_grad + unpacked_rows(grads_back).astype(jnp.float32)).astype(jnp.bfloat16)
    return (projected, grad_tokens, down_gradient, up_gradient)


def solution(mesh):
    return jax.shard_map(
        on_device,
        mesh=mesh,
        in_specs=(
            P("fsdp", "seq"),
            P("fsdp", "seq"),
            P("seq"),
            P("seq", "fsdp", None),
            P("fsdp", None, "seq"),
            P("fsdp", "seq"),
            P("fsdp"),
            P(),
        ),
        out_specs=(
            P("fsdp", "seq"),
            P("fsdp", "seq"),
            P("seq", "fsdp", None),
            P("fsdp", None, "seq"),
        ),
        check_vma=False,
    )
```

profile of v0, /device:TPU:32, one launch (start us, length us, event | category | flops | bytes accessed | tf_op | source)
XLA Modules:
  0.0 337.9 jit_solution(2242656082266893765)
XLA Ops:
  8.0 1.0 select_reduce_fusion
  9.1 0.1 fusion.21
  9.2 0.1 select_reduce_fusion.1
  9.3 0.1 pad_maximum_fusion
  9.4 1.2 gather_fusion.1
  10.6 0.8 copy.14
  11.4 13.5 %all-to-all-start.1 = ((bf16[128,1,1]{2,1,0:T(2,128)(2,1)}), bf16[128,1,1]{2,1,0:T(2,128)(2,1)S(1)}, u32[]{:S(2)}, u32[]{:S(2)}) async-start(bf16[128,1,1]{2,1,0:T(2,128)(2,1)} %copy.14), calls=%async_computation.2 | async-start | bytes 131072 | tf_op jit(solution)/shard_map/all_to_all | solution.py:64
  24.8 1.0 reshape.211
  25.8 0.1 concatenate.11
  25.9 1.8 gather_fusion.3
  27.7 7.0 %all-to-all-done.1 = bf16[128,1,1]{2,1,0:T(2,128)(2,1)S(1)} async-done(((bf16[128,1,1]{2,1,0:T(2,128)(2,1)}), bf16[128,1,1]{2,1,0:T(2,128)(2,1)S(1)}, u32[]{:S(2)}, u32[]{:S(2)}) %all-to-all-start.1) | async-done | bytes 288 | tf_op jit(solution)/shard_map/all_to_all | solution.py:64
  34.8 6.5 %all-to-all-start.3 = ((bf16[128,2,512]{2,1,0:T(2,128)(2,1)}), bf16[128,2,512]{2,1,0:T(2,128)(2,1)S(1)}, u32[]{:S(2)}, u32[]{:S(2)}) async-start(bf16[128,2,512]{2,1,0:T(2,128)(2,1)} %gather_fusion.3), calls=%async_computation.4 | async-start | bytes 524288 | tf_op jit(solution)/shard_map/all_to_all | solution.py:88
  41.3 1.0 convert_reduce_fusion
  42.4 0.1 broadcast_in_dim.35
  42.5 0.1 eq.53
  42.6 12.9 %all-to-all-done.3 = bf16[128,2,512]{2,1,0:T(2,128)(2,1)S(1)} async-done(((bf16[128,2,512]{2,1,0:T(2,128)(2,1)}), bf16[128,2,512]{2,1,0:T(2,128)(2,1)S(1)}, u32[]{:S(2)}, u32[]{:S(2)}) %all-to-all-start.3) | async-done | bytes 262176 | tf_op jit(solution)/shard_map/all_to_all | solution.py:88
  55.5 0.8 reshape.260
  56.3 1.9 fusion.12
  58.3 0.5 all-gather.2.cloned.1.call-update
  58.8 1.5 reshape.207
  60.3 2.4 concatenate.9
  62.8 8.0 %gather_fusion = bf16[128,2,4096]{2,1,0:T(2,128)(2,1)} fusion(bf16[65,2,4096]{2,1,0:T(2,128)(2,1)S(1)} %concatenate.9, s32[1024]{0:T(1024)S(1)} %pad_clamp_fusion.1), kind=kCustom, calls=%fused_computation | custom fusion | bytes 4194816 | tf_op jit(solution)/shard_map/gather | solution.py:41
  70.7 65.6 %all_to_all.26 = bf16[128,2,4096]{2,1,0:T(2,128)(2,1)} all-to-all(bf16[128,2,4096]{2,1,0:T(2,128)(2,1)} %gather_fusion), channel_id=1, replica_groups=mesh['fsdp'=128,'seq'=2] {'fsdp'}, dimensions={0} | all-to-all | bytes 4194304 | tf_op jit(solution)/shard_map/all_to_all | solution.py:63
  136.3 4.2 %reshape.258 = bf16[256,4096,1]{1,0,2:T(8,128)(2,1)} reshape(bf16[128,2,4096]{2,1,0:T(2,128)(2,1)} %all_to_all.26) | data formatting | bytes 4194304 | tf_op jit(solution)/shard_map/reshape | solution.py:70
  140.5 2.4 fusion.9
  142.9 11.9 %psum.14 = bf16[256,64]{0,1:T(8,128)(2,1)S(1)} all-reduce(f32[256,64]{0,1:T(8,128)S(1)} %fusion.9), channel_id=1, replica_groups=mesh['fsdp'=128,'seq'=2] {'seq'}, use_global_device_ids=true, to_apply=%region_5.6 | all-reduce | flops 16384 | bytes 98304 | tf_op jit(solution)/shard_map/psum | solution.py:71
  154.8 0.2 fusion.5
  155.0 0.8 reshape.210
  155.8 11.0 %all-to-all-start.2 = ((bf16[128,2,512]{2,1,0:T(2,128)(2,1)}), bf16[128,2,512]{2,1,0:T(2,128)(2,1)}, u32[]{:S(2)}, u32[]{:S(2)}) async-start(bf16[128,2,512]{2,1,0:T(2,128)(2,1)} %reshape.210), calls=%async_computation.3 | async-start | bytes 524288 | tf_op jit(solution)/shard_map/all_to_all | solution.py:81
  166.8 0.8 fusion.20
  167.7 2.1 fusion
  169.7 4.4 %reshape.213 = bf16[128,2,4096]{2,1,0:T(2,128)(2,1)} reshape(bf16[256,4096]{1,0:T(8,128)(2,1)} %fusion) | data formatting | bytes 4194304 | tf_op jit(solution)/shard_map/reshape | solution.py:106
  174.1 6.4 %all-to-all-done.2 = bf16[128,2,512]{2,1,0:T(2,128)(2,1)} async-done(((bf16[128,2,512]{2,1,0:T(2,128)(2,1)}), bf16[128,2,512]{2,1,0:T(2,128)(2,1)}, u32[]{:S(2)}, u32[]{:S(2)}) %all-to-all-start.2) | async-done | bytes 262176 | tf_op jit(solution)/shard_map/all_to_all | solution.py:81
  180.5 7.2 %all-to-all-start.4 = ((bf16[128,2,4096]{2,1,0:T(2,128)(2,1)}), bf16[128,2,4096]{2,1,0:T(2,128)(2,1)}, u32[]{:S(2)}, u32[]{:S(2)}) async-start(bf16[128,2,4096]{2,1,0:T(2,128)(2,1)} %reshape.213), calls=%async_computation.5 | async-start | bytes 4194304 | tf_op jit(solution)/shard_map/all_to_all | solution.py:108
  187.8 10.3 %all_gather.7 = bf16[128,1024]{1,0:T(8,128)(2,1)} all-gather(bf16[128,512]{1,0:T(8,128)(2,1)} %param.13), channel_id=1, replica_groups=mesh['fsdp'=128,'seq'=2] {'seq'}, dimensions={1}, use_global_device_ids=true | all-gather | bytes 393216 | tf_op jit(solution)/shard_map/all_gather | solution.py:109
  198.1 0.8 reshape.212
  198.9 0.7 multiply_convert_fusion.1
  199.6 96.9 %all-gather.2.cloned.1.call-done = bf16[1024,4096]{1,0:T(8,128)(2,1)} async-done(((bf16[8,4096]{1,0:T(8,128)(2,1)}), bf16[1024,4096]{1,0:T(8,128)(2,1)}) %all-gather.2.cloned.1.call-update) | async-done | bytes 8388624 | tf_op jit(solution)/shard_map/all_gather | solution.py:110
  296.5 7.1 %fusion.26 = f32[128,1024]{1,0:T(8,128)} fusion(bf16[128,4096]{1,0:T(8,128)(2,1)S(1)} %copy-done.2, bf16[1024,4096]{1,0:T(8,128)(2,1)} %all-gather.2.cloned.1.call-done), kind=kOutput, calls=%fused_computation.58 | convolution fusion | flops 1073741824 | bytes 9961472 | tf_op jit(solution)/shard_map/dot_general | solution.py:10
  303.6 1.9 convolution_multiply_fusion
  305.6 4.3 %fusion.14 = f32[4096,4,64]{0,2,1:T(8,128)} fusion(bf16[256,4096,1]{1,0,2:T(8,128)(2,1)} %reshape.258, f32[256,64]{0,1:T(8,128)S(1)} %fusion.20, f32[256,4]{0,1:T(4,128)S(1)} %fusion.22), kind=kOutput, calls=%fused_computation.23 | convolution fusion | flops 537001984 | bytes 6361088 | tf_op jit(solution)/shard_map/dot_general | solution.py:10
  309.9 1.8 gather_fusion.2
  311.7 0.7 reshape.216
  312.4 4.2 %gather_fusion.4 = bf16[64,2,4096]{2,1,0:T(2,128)(2,1)S(1)} fusion(bf16[128,2,4096]{2,1,0:T(2,128)(2,1)} %all-to-all-done.4, s32[1024]{0:T(1024)S(1)} %pad_clamp_fusion), kind=kCustom, calls=%fused_computation.4 | custom fusion | bytes 2097408 | tf_op jit(solution)/shard_map/gather | solution.py:44
  316.7 1.6 reshape.217
  318.3 6.4 %fusion.1 = bf16[128,4096]{1,0:T(8,128)(2,1)} fusion(f32[128,4096]{1,0:T(8,128)} %reshape.217, bf16[128,1024]{1,0:T(8,128)(2,1)S(1)} %copy-done.3, bf16[1024,4096]{1,0:T(8,128)(2,1)} %all-gather.2.cloned.1.call-done), kind=kOutput, calls=%fused_computation.8 | convolution fusion | flops 1074790400 | bytes 11796480 | tf_op jit(solution)/shard_map/dot_general | solution.py:112
  324.7 4.1 %reduce-scatter.2.cloned.1.call-done = f32[128,512]{1,0:T(8,128)} async-done(((f32[128,1024]{1,0:T(8,128)}), f32[128,512]{1,0:T(8,128)}) %reduce-scatter.2.cloned.1.call-update) | async-done | bytes 262160 | tf_op jit(solution)/shard_map/reduce_scatter | solution.py:113
  328.8 1.6 add_convert_fusion
  (30 shorter events, 0.3 us)
Async XLA Ops:
  8.0 132.5 %copy-start = (bf16[4096,4,64]{0,2,1:T(8,128)(2,1)S(1)}, bf16[4096,4,64]{0,2,1:T(8,128)(2,1)}, u32[]{:S(2)}) copy-start(bf16[4096,4,64]{0,2,1:T(8,128)(2,1)} %param.11) | copy-start | bytes 6291460
  8.0 50.8 %copy-start.1 = (bf16[128,4096]{1,0:T(8,128)(2,1)S(1)}, bf16[128,4096]{1,0:T(8,128)(2,1)}, u32[]{:S(2)}) copy-start(bf16[128,4096]{1,0:T(8,128)(2,1)} %param.8) | copy-start | bytes 3145732
  11.4 23.4 %all-to-all-start.1 = ((bf16[128,1,1]{2,1,0:T(2,128)(2,1)}), bf16[128,1,1]{2,1,0:T(2,128)(2,1)S(1)}, u32[]{:S(2)}, u32[]{:S(2)}) async-start(bf16[128,1,1]{2,1,0:T(2,128)(2,1)} %copy.14), calls=%async_computation.2 | async-start | bytes 131072 | tf_op jit(solution)/shard_map/all_to_all | solution.py:64
  34.8 20.8 %all-to-all-start.3 = ((bf16[128,2,512]{2,1,0:T(2,128)(2,1)}), bf16[128,2,512]{2,1,0:T(2,128)(2,1)S(1)}, u32[]{:S(2)}, u32[]{:S(2)}) async-start(bf16[128,2,512]{2,1,0:T(2,128)(2,1)} %gather_fusion.3), calls=%async_computation.4 | async-start | bytes 524288 | tf_op jit(solution)/shard_map/all_to_all | solution.py:88
  41.3 125.5 %all-reduce.4.cloned.1.call-start = ((), (), s32[]{:S(2)}) async-start(), calls=%async_computation.8 | async-start | bytes 131072 | tf_op jit(solution)/shard_map/psum | solution.py:90
  58.3 238.3 %all-gather.2.cloned.1.call-start = ((), (), s32[]{:S(2)}) async-start(), calls=%async_computation.6 | async-start | bytes 8454144 | tf_op jit(solution)/shard_map/all_gather | solution.py:110
  140.4 14.3 %copy-start.7 = (bf16[4,64,512]{2,1,0:T(8,128)(2,1)S(1)}, bf16[4,64,512]{2,1,0:T(8,128)(2,1)}, u32[]{:S(2)}) copy-start(bf16[4,64,512]{2,1,0:T(8,128)(2,1)} %param.12) | copy-start | bytes 786436
  155.8 24.7 %all-to-all-start.2 = ((bf16[128,2,512]{2,1,0:T(2,128)(2,1)}), bf16[128,2,512]{2,1,0:T(2,128)(2,1)}, u32[]{:S(2)}, u32[]{:S(2)}) async-start(bf16[128,2,512]{2,1,0:T(2,128)(2,1)} %reshape.210), calls=%async_computation.3 | async-start | bytes 524288 | tf_op jit(solution)/shard_map/all_to_all | solution.py:81
  174.1 122.4 %copy-start.2 = (bf16[128,4096]{1,0:T(8,128)(2,1)S(1)}, bf16[128,4096]{1,0:T(8,128)(2,1)}, u32[]{:S(2)}) copy-start(bf16[128,4096]{1,0:T(8,128)(2,1)} %param.8) | copy-start | bytes 3145732
  180.5 131.9 %all-to-all-start.4 = ((bf16[128,2,4096]{2,1,0:T(2,128)(2,1)}), bf16[128,2,4096]{2,1,0:T(2,128)(2,1)}, u32[]{:S(2)}, u32[]{:S(2)}) async-start(bf16[128,2,4096]{2,1,0:T(2,128)(2,1)} %reshape.213), calls=%async_computation.5 | async-start | bytes 4194304 | tf_op jit(solution)/shard_map/all_to_all | solution.py:108
  187.8 141.0 %reduce-scatter.2.cloned.1.call-start = ((), (), s32[]{:S(2)}) async-start(), calls=%async_computation.7 | async-start | bytes 786432 | tf_op jit(solution)/shard_map/reduce_scatter | solution.py:113
  199.6 104.0 %copy-start.4 = (bf16[256,512]{1,0:T(8,128)(2,1)S(1)}, bf16[256,512]{1,0:T(8,128)(2,1)}, u32[]{:S(2)}) copy-start(bf16[256,512]{1,0:T(8,128)(2,1)} %reshape.212) | copy-start | bytes 786436
  316.7 1.6 copy-start.3
  318.3 10.5 %copy-start.5 = (f32[128,512]{1,0:T(8,128)S(1)}, f32[128,512]{1,0:T(8,128)}, u32[]{:S(2)}) copy-start(f32[128,512]{1,0:T(8,128)} %reshape.216) | copy-start | bytes 786436
  318.3 10.5 %copy-start.6 = (f32[512]{0:T(512)S(1)}, f32[512]{0:T(512)}, u32[]{:S(2)}) copy-start(f32[512]{0:T(512)} %param.10) | copy-start | bytes 6148
Sparse Core Ops, SparseCore 0:
  58.4 29.0 all-reduce.3
  303.7 24.9 reduce-scatter.1
Sparse Core Ops, SparseCore 1:
  60.6 235.9 all-gather.1
where the time goes:
time: 341 us; the launch traced here: 338 us
  waiting for transfers between devices  128 us (38%)
  blocking collectives  87.7 us (26%)
  starting transfers between devices  38.3 us (11%)
  local copies, waits for them, and re-layouts  36.3 us (11%)
  matrix products  26.3 us (8%)
  between operations  15.7 us (5%)
  other arithmetic  5.54 us (2%)
    all_gather x1, waiting for transfers between devices, on_device(): full_weight = lax.all_gather(weight, 'fsdp', axis=0, tiled=True)  96.9 us
    all_to_all x1, blocking collectives, on_device(): lax.all_to_all(pack_rows(tokens), 'fsdp', split_axis=0, concat_axis=0, ti...  65.6 us
    dot_general x5, matrix products, contract_product(): lax.dot_general(left, right, (((left_dim,), (right_dim,)), ((), ())), pre...  17.3 us
    all_to_all x1, starting transfers between devices, on_device(): lax.all_to_all(labels, 'fsdp', split_axis=0, concat_axis=0, tiled=True)  13.5 us
    all_to_all x1, waiting for transfers between devices, on_device(): lax.all_to_all(pack_rows(cotangent), 'fsdp', split_axis=0, concat_axis=0,...  12.9 us
    psum x1, blocking collectives, on_device(): lax.psum(collapse(jnp.dot(owner_rows, down_local, preferred_element_type=...  11.9 us
    all_to_all x1, starting transfers between devices, on_device(): lax.all_to_all(adapter_output.reshape(owning_count, rows_per_block, key_p...  11 us
    all_gather x1, blocking collectives, on_device(): full_grads = lax.all_gather(cotangent, 'seq', axis=1, tiled=True)  10.3 us
  transfers between devices with their start and end apart: 7, of which 5 were waited for; matrix products, arithmetic and copies ran while one was open for 18% of the time, Pallas kernels for 0%

commit v1 on v0

v1 whole, which is shorter than its diff:
```python
import jax
import jax.numpy as jnp
from jax import lax
from jax.experimental import pallas as pl
from jax.experimental.pallas import tpu as pltpu
from jax.sharding import Mesh, PartitionSpec as P

adapter_scale = 0.5
GROUPS = 4
SUB = ("y", "xl", "z", "c")
SPLIT = (4, 2, 8, 2)
bf16 = jnp.bfloat16
f32 = jnp.float32
VMEM = pl.BlockSpec(memory_space=pltpu.VMEM)
PARAMS = pltpu.CompilerParams(vmem_limit_bytes=48 * 1024 * 1024)


def dot(a, b, da=1, db=0):
    return lax.dot_general(a, b, (((da,), (db,)), ((), ())), preferred_element_type=f32)


def iota(shape, dim):
    return lax.broadcasted_iota(jnp.int32, shape, dim)


def pack_kernel(key_ref, label_ref, tok_ref, cot_ref, out_ref, stack):
    rows, width = tok_ref.shape
    tw, cw = width // GROUPS, cot_ref.shape[1] // GROUPS
    for g in range(GROUPS):
        stack[g * rows:(g + 1) * rows, :tw] = tok_ref[:, g * tw:(g + 1) * tw]
        stack[g * rows:(g + 1) * rows, tw:] = cot_ref[:, g * cw:(g + 1) * cw]
    total = out_ref.shape[0]
    step = 256
    for b in range(total // step):
        part = slice(b * step, (b + 1) * step)
        pick = (key_ref[part, :] == iota((step, GROUPS * rows), 1)).astype(f32).astype(bf16)
        out_ref[part, :tw + cw] = dot(pick, stack[...]).astype(bf16)
        out_ref[part, tw + cw:] = jnp.broadcast_to(label_ref[part, :], (step, 128)).astype(bf16)


def order(chunk, groups):
    out, src = iota((chunk, chunk), 0), iota((chunk, chunk), 1)
    per = chunk // groups
    return (src == (out % per) * groups + out // per).astype(f32).astype(bf16)


def reorder(chunk, groups):
    src, out = iota((chunk, chunk), 1), iota((chunk, chunk), 0)
    per = chunk // groups
    return (out == (src % per) * groups + src // per).astype(f32).astype(bf16)


def collapse(part, label, tasks, rank):
    total = jnp.zeros((part.shape[0], rank), f32)
    for j in range(tasks):
        total = total + jnp.where(label == j, part[:, j * rank:(j + 1) * rank], 0.0)
    return total


def spread(low, label, tasks):
    return jnp.concatenate(
        [jnp.where(label == j, low, 0.0) for j in range(tasks)], axis=1
    ).astype(bf16)


def owner_in_kernel(tasks, got_ref, down_ref, up_ref, low_ref, rows_ref, cots_ref, label_ref):
    width = down_ref.shape[1]
    key_part = up_ref.shape[1]
    rank = down_ref.shape[0] // tasks
    tw, cw = width // GROUPS, key_part // GROUPS
    step = 256
    per = step // GROUPS
    to_rows = order(step, GROUPS)
    for b in range(got_ref.shape[0] // step):
        block = dot(to_rows, got_ref[b * step:(b + 1) * step, :]).astype(bf16)
        at = slice(b * per, (b + 1) * per)
        for g in range(GROUPS):
            piece = block[g * per:(g + 1) * per, :]
            rows_ref[at, g * tw:(g + 1) * tw] = piece[:, :tw]
            cots_ref[at, g * cw:(g + 1) * cw] = piece[:, tw:tw + cw]
        label_ref[at, :] = block[:per, tw + cw:]
    label = label_ref[...].astype(f32)[:, :rank]
    low_ref[:, :rank] = collapse(dot(rows_ref[...], down_ref[...], 1, 1), label, tasks, rank)
    low_ref[:, rank:] = collapse(dot(cots_ref[...], up_ref[...], 1, 1), label, tasks, rank)


def owner_out_kernel(tasks, mine_ref, other_ref, label_ref, down_ref, up_ref, out_ref, low_ref, grad_ref, back, lora):
    rank = down_ref.shape[0] // tasks
    width, key_part = down_ref.shape[1], up_ref.shape[1]
    tw, cw = width // GROUPS, key_part // GROUPS
    total = mine_ref[...] + other_ref[...]
    label = label_ref[...].astype(f32)[:, :rank]
    low = total[:, :rank].astype(bf16).astype(f32)
    grad = (adapter_scale * total[:, rank:]).astype(bf16).astype(f32)
    low_wide = spread(low, label, tasks)
    grad_wide = spread(grad, label, tasks)
    low_ref[...] = low_wide
    grad_ref[...] = grad_wide
    lora[...] = (adapter_scale * dot(low_wide, up_ref[...])).astype(bf16)
    for g in range(GROUPS):
        cols = slice(g * tw, (g + 1) * tw)
        back[:, cols] = dot(grad_wide, down_ref[:, cols]).astype(bf16)
    step = 256
    per = step // GROUPS
    to_sent = reorder(step, GROUPS)
    for b in range(out_ref.shape[0] // step):
        at = slice(b * per, (b + 1) * per)
        rows = jnp.concatenate([back[at, g * tw:(g + 1) * tw] for g in range(GROUPS)], axis=0)
        adds = jnp.concatenate([lora[at, g * cw:(g + 1) * cw] for g in range(GROUPS)], axis=0)
        where = slice(b * step, (b + 1) * step)
        out_ref[where, :tw] = dot(to_sent, rows).astype(bf16)
        out_ref[where, tw:] = dot(to_sent, adds).astype(bf16)


def finish_kernel(key_ref, got_ref, base_ref, frozen_ref, bias_ref, grad_ref, proj_ref):
    rows, width = grad_ref.shape
    key_part = proj_ref.shape[1]
    tw, cw = width // GROUPS, key_part // GROUPS
    total = got_ref.shape[0]
    for g in range(GROUPS):
        pick = (key_ref[...] + g == iota((rows, total), 1)).astype(f32).astype(bf16)
        cols, keys = slice(g * tw, (g + 1) * tw), slice(g * cw, (g + 1) * cw)
        grad_ref[:, cols] = (base_ref[:, cols] + dot(pick, got_ref[:, :tw])).astype(bf16)
        proj_ref[:, keys] = (
            frozen_ref[:, keys] + bias_ref[:, keys] + dot(pick, got_ref[:, tw:])
        ).astype(bf16)


def swap(value, axis):
    return lax.ppermute(value, axis, [(0, 1), (1, 0)])


def on_device(tokens, weight, bias, adapter_down, adapter_up, cotangent, block_task, owner_slot):
    rows_dev, half_width = tokens.shape
    owners = SPLIT[0] * SPLIT[1] * SPLIT[2] * SPLIT[3]
    blocks_dev = block_task.shape[0]
    block_rows = rows_dev // blocks_dev
    task_dev, rank, key_part = adapter_up.shape
    tasks_all = owner_slot.shape[0]
    chunk = block_rows * GROUPS
    sent_rows = owners * chunk
    tw, cw = half_width // GROUPS, key_part // GROUPS
    seq = lax.axis_index("seq")
    core = lax.axis_index("c")

    match_task = block_task[:, None] == jnp.arange(tasks_all, dtype=jnp.int32)[None, :]
    slot_of = jnp.sum(jnp.where(match_task, owner_slot[None, :], 0), axis=1)
    owner_of = slot_of // task_dev
    inner_of = slot_of % task_dev
    owner_row = jnp.arange(sent_rows, dtype=jnp.int32) // chunk
    match_owner = owner_of[None, :] == owner_row[:, None]
    block_pick = jnp.sum(
        jnp.where(match_owner, jnp.arange(blocks_dev, dtype=jnp.int32)[None, :] + 1, 0), axis=1
    )
    label = jnp.sum(jnp.where(match_owner, inner_of[None, :] + 1, 0), axis=1) - 1
    within = jnp.arange(sent_rows, dtype=jnp.int32) % chunk
    key = jnp.where(
        block_pick > 0,
        (block_pick - 1) * block_rows + within // GROUPS + (within % GROUPS) * rows_dev,
        -1,
    )
    sent = pl.pallas_call(
        pack_kernel,
        out_shape=jax.ShapeDtypeStruct((sent_rows, tw + cw + 128), bf16),
        in_specs=[VMEM] * 4,
        out_specs=VMEM,
        scratch_shapes=[pltpu.VMEM((GROUPS * rows_dev, tw + cw), bf16)],
        compiler_params=PARAMS,
        name="pack",
    )(key[:, None], label.astype(f32)[:, None], tokens, cotangent)
    got = lax.all_to_all(sent, SUB, split_axis=0, concat_axis=0, tiled=True)

    stage = lax.all_gather(weight, "xl", axis=0)
    stage = lax.all_gather(stage, "z", axis=0)
    stage = lax.all_gather(stage, "y", axis=0)
    own_weight = stage.reshape(-1, half_width)
    other_weight = swap(own_weight, "c")

    down_t = adapter_down.transpose(1, 2, 0).reshape(task_dev * rank, half_width)
    up_t = adapter_up.reshape(task_dev * rank, key_part)
    owner_rows = owners * block_rows
    low_mine, rows_in, cots_in, label_in = pl.pallas_call(
        lambda *refs: owner_in_kernel(task_dev, *refs),
        out_shape=(
            jax.ShapeDtypeStruct((owner_rows, 2 * rank), f32),
            jax.ShapeDtypeStruct((owner_rows, half_width), bf16),
            jax.ShapeDtypeStruct((owner_rows, key_part), bf16),
            jax.ShapeDtypeStruct((owner_rows, 128), bf16),
        ),
        in_specs=[VMEM] * 3,
        out_specs=(VMEM,) * 4,
        compiler_params=PARAMS,
        name="owner_in",
    )(got, down_t, up_t)
    low_other = swap(low_mine, "seq")
    to_return, low_wide, grad_wide = pl.pallas_call(
        lambda *refs: owner_out_kernel(task_dev, *refs),
        out_shape=(
            jax.ShapeDtypeStruct((sent_rows, tw + cw), bf16),
            jax.ShapeDtypeStruct((owner_rows, task_dev * rank), bf16),
            jax.ShapeDtypeStruct((owner_rows, task_dev * rank), bf16),
        ),
        in_specs=[VMEM] * 5,
        out_specs=(VMEM,) * 3,
        scratch_shapes=[
            pltpu.VMEM((owner_rows, half_width), bf16),
            pltpu.VMEM((owner_rows, key_part), bf16),
        ],
        compiler_params=PARAMS,
        name="owner_out",
    )(low_mine, low_other, label_in, down_t, up_t)
    returned = lax.all_to_all(to_return, SUB, split_axis=0, concat_axis=0, tiled=True)

    up_gradient = (adapter_scale * dot(low_wide, cots_in, 0, 0)).reshape(task_dev, rank, key_part)
    down_gradient = (
        dot(grad_wide, rows_in, 0, 0).reshape(task_dev, rank, half_width).transpose(2, 0, 1)
    )

    shard = weight.shape[0]
    held = (SPLIT[0], SPLIT[2], SPLIT[1], shard)
    natural = SPLIT + (shard,)
    other_cot = swap(cotangent, "seq")
    full_cot = jnp.where(
        seq == 0,
        jnp.concatenate([cotangent, other_cot], axis=1),
        jnp.concatenate([other_cot, cotangent], axis=1),
    )
    by_core = full_cot.reshape((rows_dev,) + natural).transpose(0, 4, 1, 3, 2, 5)
    by_core = by_core.reshape(rows_dev, 2, -1)
    cot_first, cot_second = by_core[:, 0], by_core[:, 1]
    own_cot = jnp.where(core == 0, cot_first, cot_second)
    off_cot = jnp.where(core == 0, cot_second, cot_first)
    own_part = dot(tokens, own_weight, 1, 1)
    off_part = dot(tokens, other_weight, 1, 1)
    parts = jnp.where(
        core == 0,
        jnp.stack([own_part, off_part], axis=1),
        jnp.stack([off_part, own_part], axis=1),
    )
    parts = parts.reshape((rows_dev, 2) + held).transpose(0, 2, 4, 3, 1, 5).reshape(rows_dev, -1)
    keep = jnp.where(seq == 0, parts[:, :key_part], parts[:, key_part:])
    give = jnp.where(seq == 0, parts[:, key_part:], parts[:, :key_part])
    frozen = keep + swap(give, "seq")
    base_grad = dot(own_cot, own_weight) + dot(off_cot, other_weight)

    row_key = jnp.repeat(owner_of * chunk, block_rows) + jnp.tile(
        jnp.arange(block_rows, dtype=jnp.int32) * GROUPS, blocks_dev
    )
    grad_tokens, projected = pl.pallas_call(
        finish_kernel,
        out_shape=(
            jax.ShapeDtypeStruct((rows_dev, half_width), bf16),
            jax.ShapeDtypeStruct((rows_dev, key_part), bf16),
        ),
        in_specs=[VMEM] * 5,
        out_specs=(VMEM, VMEM),
        compiler_params=PARAMS,
        name="finish",
    )(row_key[:, None], returned, base_grad, frozen, bias[None, :])
    return (projected, grad_tokens, down_gradient, up_gradient)


def solution(mesh):
    fine = Mesh(mesh.devices.reshape(SPLIT + (mesh.shape["seq"],)), SUB + ("seq",))
    return jax.shard_map(
        on_device,
        mesh=fine,
        in_specs=(
            P(SUB, "seq"),
            P(SUB, "seq"),
            P("seq"),
            P("seq", SUB, None),
            P(SUB, None, "seq"),
            P(SUB, "seq"),
            P(SUB),
            P(),
        ),
        out_specs=(
            P(SUB, "seq"),
            P(SUB, "seq"),
            P("seq", SUB, None),
            P(SUB, None, "seq"),
        ),
        check_vma=False,
    )
```

time: 341 us -> 234 us (0.69)
  blocking collectives: 87.7 us -> 6.29 us
  local copies, waits for them, and re-layouts: 36.3 us -> 12.5 us
  waiting for transfers between devices: 128 us -> 141 us
  starting transfers between devices: 38.3 us -> 26.3 us
  Pallas kernels: 0 us -> 11.3 us
  matrix products: 26.3 us -> 18.7 us
    all_to_all x1 -> x0, blocking collectives: 65.6 us -> none  [on_device(): lax.all_to_all(pack_rows(tokens), 'fsdp', split_axis=0, concat_axis=0, ti...]
    ppermute x0 -> x4, waiting for transfers between devices: none -> 23 us  [swap(): return lax.ppermute(value, axis, [(0, 1), (1, 0)])]
    all_to_all x4 -> x2, starting transfers between devices: 38.2 us -> 20.1 us  [the longest x1 10.5 us: on_device(): got = lax.all_to_all(sent, SUB, split_axis=0, concat_axis=0, tiled=True)]
    gather x5 -> x0, local copies, waits for them, and re-layouts: 17 us -> none  [the longest x2 9.76 us: pack_rows(): return padded[slot_table]]
    reshape x7 -> x0, local copies, waits for them, and re-layouts: 13.4 us -> none  [the longest x1 4.42 us: on_device(): returned_rows.reshape(owning_count, rows_per_block, half_width)]
    psum x1 -> x0, blocking collectives: 11.9 us -> none  [on_device(): lax.psum(collapse(jnp.dot(owner_rows, down_local, preferred_element_type=...]
    pallas_call x0 -> x4, Pallas kernels: none -> 11.3 us  [the longest x1 4.1 us: on_device(): pl.pallas_call(lambda *refs: owner_in_kernel(task_dev, *refs), out_shape=...]
    unnamed x16 -> x33, local copies, waits for them, and re-layouts: 0.04 us -> 10.4 us
  transfers between devices with their start and end apart: 7 -> 8, of which waited for: 5 -> 7; matrix products, arithmetic and copies ran while one was open for 18% -> 11% of each run, Pallas kernels for 0% -> 4%
where the time goes in v1:
time: 234 us; the launch traced here: 233 us
  waiting for transfers between devices  141 us (60%)
  starting transfers between devices  26.3 us (11%)
  matrix products  18.7 us (8%)
  between operations  14.3 us (6%)
  local copies, waits for them, and re-layouts  12.5 us (5%)
  Pallas kernels  11.3 us (5%)
  blocking collectives  6.29 us (3%)
  other arithmetic  2.83 us (1%)
    all_gather x1, waiting for transfers between devices, on_device(): stage = lax.all_gather(stage, 'y', axis=0)  60.8 us
    all_gather x1, waiting for transfers between devices, on_device(): stage = lax.all_gather(stage, 'z', axis=0)  40.4 us
    ppermute x4, waiting for transfers between devices, swap(): return lax.ppermute(value, axis, [(0, 1), (1, 0)])  23 us
    dot_general x6, matrix products, dot(): lax.dot_general(a, b, (((da,), (db,)), ((), ())), preferred_element_type=...  18.7 us
    all_to_all x1, waiting for transfers between devices, on_device(): lax.all_to_all(to_return, SUB, split_axis=0, concat_axis=0, tiled=True)  13.1 us
    all_to_all x1, starting transfers between devices, on_device(): got = lax.all_to_all(sent, SUB, split_axis=0, concat_axis=0, tiled=True)  10.5 us
    unnamed x33, local copies, waits for them, and re-layouts  10.4 us
    all_to_all x1, starting transfers between devices, on_device(): lax.all_to_all(to_return, SUB, split_axis=0, concat_axis=0, tiled=True)  9.64 us
  transfers between devices with their start and end apart: 8, of which 7 were waited for; matrix products, arithmetic and copies ran while one was open for 11% of the time, Pallas kernels for 4%

profile of v1, /device:TPU:32, one launch (start us, length us, event | category | flops | bytes accessed | tf_op | source)
XLA Modules:
  0.0 233.1 jit_solution(5076227916755078948)
XLA Ops:
  7.2 0.0 all-gather.6.cloned.1.call-start
  7.2 6.3 %all-gather = bf16[16,4096]{1,0:T(8,128)(2,1)} all-gather(bf16[8,4096]{1,0:T(8,128)(2,1)} %param.9), channel_id=2, replica_groups=mesh['y'=4,'xl'=2,'z'=8,'c'=2,'seq'=2] {'xl'}, dimensions={0}, use_global_device_ids=true | all-gather | bytes 196608 | tf_op jit(solution)/shard_map/all_gather | solution.py:173
  13.5 0.0 all-gather.6.cloned.1.call-update
  13.5 0.0 all-gather.8.cloned.1.call-start
  13.6 40.4 %all-gather.6.cloned.1.call-done = bf16[16,8,4096]{2,1,0:T(8,128)(2,1)} async-done(((bf16[2,8,4096]{2,1,0:T(8,128)(2,1)}), bf16[16,8,4096]{2,1,0:T(8,128)(2,1)}) %all-gather.6.cloned.1.call-update) | async-done | bytes 1048592 | tf_op jit(solution)/shard_map/all_gather | solution.py:174
  54.0 0.0 all-gather.8.cloned.1.call-update
  54.0 0.9 select_reduce_fusion
  54.9 0.1 fusion.15
  55.1 0.2 copy.41
  55.3 1.0 copy.43.label_ref
  56.3 0.3 fusion.3.key_ref
  56.7 1.0 copy-done.5
  57.7 0.9 copy-done.7
  58.6 3.1 %pack.1 = bf16[1024,1280]{1,0:T(8,128)(2,1)} custom-call(s32[1024,1]{1,0:T(8,128)S(1)} %fusion.3.key_ref, f32[1024,1]{1,0:T(8,128)S(1)} %copy-done.5, bf16[128,4096]{1,0:T(8,128)(2,1)S(1)} %copy-done.2, bf16[128,512]{1,0:T(8,128)(2,1)S(1)} %copy-done.7), custom_call_target="tpu_custom_call" | custom-call | tf_op jit(solution)/shard_map/pack/pallas_call | solution.py:162
  61.7 10.5 %all-to-all-start = ((bf16[128,8,1280]{2,1,0:T(8,128)(2,1)}), bf16[128,8,1280]{2,1,0:T(8,128)(2,1)}, u32[]{:S(2)}, u32[]{:S(2)}) async-start(bf16[128,8,1280]{2,1,0:T(8,128)(2,1)} %bitcast.2), calls=%async_computation | async-start | bytes 5242880 | tf_op jit(solution)/shard_map/all_to_all | solution.py:171
  72.2 60.8 %all-gather.8.cloned.1.call-done = bf16[32,2,8,4096]{3,2,1,0:T(8,128)(2,1)} async-done(((bf16[8,2,8,4096]{3,2,1,0:T(8,128)(2,1)}), bf16[32,2,8,4096]{3,2,1,0:T(8,128)(2,1)}) %all-gather.8.cloned.1.call-update) | async-done | bytes 4194320 | tf_op jit(solution)/shard_map/all_gather | solution.py:175
  133.0 3.5 %all-to-all-done = bf16[128,8,1280]{2,1,0:T(8,128)(2,1)} async-done(((bf16[128,8,1280]{2,1,0:T(8,128)(2,1)}), bf16[128,8,1280]{2,1,0:T(8,128)(2,1)}, u32[]{:S(2)}, u32[]{:S(2)}) %all-to-all-start) | async-done | bytes 2621472 | tf_op jit(solution)/shard_map/all_to_all | solution.py:171
  136.5 4.1 %owner_in.1 = (f32[256,128]{1,0:T(8,128)S(1)}, bf16[256,4096]{1,0:T(8,128)(2,1)S(1)}, bf16[256,512]{1,0:T(8,128)(2,1)S(1)}, bf16[256,128]{1,0:T(8,128)(2,1)S(1)}) custom-call(bf16[1024,1280]{1,0:T(8,128)(2,1)} %bitcast.3.refs_0_, bf16[256,4096]{1,0:T(8,128)(2,1)S(1)} %bitcast.53, bf16[256,512]{1,0:T(8,128)(2,1)S(1)} %bitcast.56), custom_call_target="tpu_custom_call" | custom-call | tf_op jit(solution)/shard_map/owner_in/pallas_call | solution.py:182
  140.6 1.4 copy-done.4
  142.0 0.7 copy-done.9
  142.7 2.5 %collective-permute-start = (f32[256,128]{1,0:T(8,128)S(1)}, f32[256,128]{1,0:T(8,128)S(1)}, u32[]{:S(2)}, u32[]{:S(2)}) collective-permute-start(f32[256,128]{1,0:T(8,128)S(1)} %get-tuple-element.13.refs_0_), channel_id=1, source_target_pairs={{0,1},{1,0},{2,3},{3,2},{4,5},{5,4},{6,7},{7,6},{8,9},{9,8},{10,11... | collective-permute-start | bytes 393224 | tf_op jit(solution)/shard_map/ppermute | solution.py:130
  145.2 4.0 %collective-permute-done.refs_1_ = f32[256,128]{1,0:T(8,128)S(1)} collective-permute-done((f32[256,128]{1,0:T(8,128)S(1)}, f32[256,128]{1,0:T(8,128)S(1)}, u32[]{:S(2)}, u32[]{:S(2)}) %collective-permute-start) | collective-permute-done | bytes 131104 | tf_op jit(solution)/shard_map/ppermute | solution.py:130
  149.2 1.6 owner_out.1
  150.8 1.5 copy-done.3
  152.3 0.6 copy-done.10
  152.9 0.6 copy-done.11
  153.6 9.6 %all-to-all-start.1 = ((bf16[128,8,1152]{2,1,0:T(8,128)(2,1)}), bf16[128,8,1152]{2,1,0:T(8,128)(2,1)S(1)}, u32[]{:S(2)}, u32[]{:S(2)}) async-start(bf16[128,8,1152]{2,1,0:T(8,128)(2,1)} %bitcast.55), calls=%async_computation.1 | async-start | bytes 4718592 | tf_op jit(solution)/shard_map/all_to_all | solution.py:212
  163.2 0.8 copy.44
  164.0 2.7 %collective-permute-start.1 = (bf16[128,512]{0,1:T(8,128)(2,1)}, bf16[128,512]{0,1:T(8,128)(2,1)}, u32[]{:S(2)}, u32[]{:S(2)}) collective-permute-start(bf16[128,512]{0,1:T(8,128)(2,1)} %copy.44), channel_id=1, source_target_pairs={{0,1},{1,0},{2,3},{3,2},{4,5},{5,4},{6,7},{7,6},{8,9},{9,8},{10,11... | collective-permute-start | bytes 393224 | tf_op jit(solution)/shard_map/ppermute | solution.py:130
  166.7 0.1 broadcast_add_fusion
  166.8 0.1 add.138.key_ref
  166.8 10.6 %collective-permute-done.1 = bf16[128,512]{0,1:T(8,128)(2,1)} collective-permute-done((bf16[128,512]{0,1:T(8,128)(2,1)}, bf16[128,512]{0,1:T(8,128)(2,1)}, u32[]{:S(2)}, u32[]{:S(2)}) %collective-permute-start.1) | collective-permute-done | bytes 131104 | tf_op jit(solution)/shard_map/ppermute | solution.py:130
  177.5 1.3 fusion.16
  178.8 2.3 convolution_multiply_fusion
  181.1 4.4 %fusion.34 = f32[256,4096]{1,0:T(8,128)} fusion(bf16[256,256]{1,0:T(8,128)(2,1)} %copy-done.10, bf16[256,4096]{1,0:T(8,128)(2,1)} %copy-done.4), kind=kOutput, calls=%fused_computation.69 | convolution fusion | flops 536870912 | bytes 6422528 | tf_op jit(solution)/shard_map/dot_general | solution.py:19
  185.5 1.3 convolution_bitcast_fusion
  186.8 2.1 fusion.18
  189.0 3.4 %fusion.33 = f32[128,512]{0,1:T(8,128)S(1)} fusion(bf16[128,4096]{1,0:T(8,128)(2,1)S(1)} %copy-done.2, bf16[512,4096]{1,0:T(8,128)(2,1)} %collective-permute-done.2), kind=kOutput, calls=%fused_computation.68 | convolution fusion | flops 536870912 | bytes 5505024 | tf_op jit(solution)/shard_map/dot_general | solution.py:19
  192.5 0.7 fusion.32
  193.3 0.1 copy.57
  193.4 1.1 copy.56
  194.6 0.9 collective-permute-start.3
  195.5 5.2 %convolution_add_fusion.base_ref = f32[128,4096]{1,0:T(8,128)} fusion(f32[128,4096]{1,0:T(8,128)} %fusion.18, bf16[512,4096]{1,0:T(8,128)(2,1)} %collective-permute-done.2, pred[]{:T(512)S(6)} %eq.47, bf16[128,2,512]{0,2,1:T(8,128)(2,1)} %bitcast.65), kind=kOutput, calls=%fused_computation | convolution fusion | flops 537460736 | bytes 8650753 | tf_op jit(solution)/shard_map/dot_general | solution.py:19
  200.6 8.4 %collective-permute-done.3 = f32[128,512]{1,0:T(8,128)S(1)} collective-permute-done((f32[128,512]{1,0:T(8,128)S(1)}, f32[128,512]{1,0:T(8,128)S(1)}, u32[]{:S(2)}, u32[]{:S(2)}) %collective-permute-start.3) | collective-permute-done | bytes 262176 | tf_op jit(solution)/shard_map/ppermute | solution.py:130
  209.0 0.1 select_add_fusion.frozen_ref
  209.1 13.1 %all-to-all-done.1 = bf16[128,8,1152]{2,1,0:T(8,128)(2,1)S(1)} async-done(((bf16[128,8,1152]{2,1,0:T(8,128)(2,1)}), bf16[128,8,1152]{2,1,0:T(8,128)(2,1)S(1)}, u32[]{:S(2)}, u32[]{:S(2)}) %all-to-all-start.1) | async-done | bytes 2359328 | tf_op jit(solution)/shard_map/all_to_all | solution.py:212
  222.2 1.6 copy-done.1
  223.8 2.5 %finish.1 = (bf16[128,4096]{1,0:T(8,128)(2,1)}, bf16[128,512]{1,0:T(8,128)(2,1)}) custom-call(s32[128,1]{1,0:T(8,128)S(1)} %add.138.key_ref, bf16[1024,1152]{1,0:T(8,128)(2,1)S(1)} %bitcast.52, f32[128,4096]{1,0:T(8,128)S(1)} %copy-done.1, f32[128,512]{1,0:T(8,128)S(1)} %select_add_fusion.frozen_ref, f32[1,512]{1,0:T(1,128)S(1)} %bitcast.58), custom_call_target="tpu_custom_call" | custom-call | tf_op jit(solution)/shard_map/finish/pallas_call | solution.py:249
  (34 shorter events, 0.2 us)
Async XLA Ops:
  7.2 49.5 %copy-start.2 = (bf16[128,4096]{1,0:T(8,128)(2,1)S(1)}, bf16[128,4096]{1,0:T(8,128)(2,1)}, u32[]{:S(2)}) copy-start(bf16[128,4096]{1,0:T(8,128)(2,1)} %tok_ref.1) | copy-start | bytes 3145732
  7.2 46.8 %all-gather.6.cloned.1.call-start = ((), (), s32[]{:S(2)}) async-start(), calls=%async_computation.2 | async-start | bytes 1179648 | tf_op jit(solution)/shard_map/all_gather | solution.py:174
  13.5 119.5 %all-gather.8.cloned.1.call-start = ((), (), s32[]{:S(2)}) async-start(), calls=%async_computation.3 | async-start | bytes 5242880 | tf_op jit(solution)/shard_map/all_gather | solution.py:175
  56.7 1.0 copy-start.5
  57.7 0.9 copy-start.7
  58.6 77.9 %copy-start = (bf16[4096,4,64]{0,2,1:T(8,128)(2,1)S(1)}, bf16[4096,4,64]{0,2,1:T(8,128)(2,1)}, u32[]{:S(2)}) copy-start(bf16[4096,4,64]{0,2,1:T(8,128)(2,1)} %param.11) | copy-start | bytes 6291460
  58.6 77.9 %copy-start.6 = (bf16[4,64,512]{2,1,0:T(8,128)(2,1)S(1)}, bf16[4,64,512]{2,1,0:T(8,128)(2,1)}, u32[]{:S(2)}) copy-start(bf16[4,64,512]{2,1,0:T(8,128)(2,1)} %param.12) | copy-start | bytes 786436
  61.7 74.8 %all-to-all-start = ((bf16[128,8,1280]{2,1,0:T(8,128)(2,1)}), bf16[128,8,1280]{2,1,0:T(8,128)(2,1)}, u32[]{:S(2)}, u32[]{:S(2)}) async-start(bf16[128,8,1280]{2,1,0:T(8,128)(2,1)} %bitcast.2), calls=%async_computation | async-start | bytes 5242880 | tf_op jit(solution)/shard_map/all_to_all | solution.py:171
  133.0 56.0 %collective-permute-start.2 = (bf16[512,4096]{1,0:T(8,128)(2,1)}, bf16[512,4096]{1,0:T(8,128)(2,1)}, u32[]{:S(2)}, u32[]{:S(2)}) collective-permute-start(bf16[512,4096]{1,0:T(8,128)(2,1)} %bitcast.59), channel_id=1, source_target_pairs={{0,2},{2,0},{1,3},{3,1},{4,6},{6,4},{5,7},{7,5},{8,10},{10,8},{9,1... | collective-permute-start | bytes 12582920 | tf_op jit(solution)/shard_map/ppermute | solution.py:130
  140.6 1.4 copy-start.4
  142.0 0.7 copy-start.9
  142.7 20.5 %copy-start.8 = (bf16[128,512]{1,0:T(8,128)(2,1)S(1)}, bf16[128,512]{1,0:T(8,128)(2,1)}, u32[]{:S(2)}) copy-start(bf16[128,512]{1,0:T(8,128)(2,1)} %cot_ref.1) | copy-start | bytes 393220
  142.7 6.5 %collective-permute-start = (f32[256,128]{1,0:T(8,128)S(1)}, f32[256,128]{1,0:T(8,128)S(1)}, u32[]{:S(2)}, u32[]{:S(2)}) collective-permute-start(f32[256,128]{1,0:T(8,128)S(1)} %get-tuple-element.13.refs_0_), channel_id=1, source_target_pairs={{0,1},{1,0},{2,3},{3,2},{4,5},{5,4},{6,7},{7,6},{8,9},{9,8},{10,11... | collective-permute-start | bytes 393224 | tf_op jit(solution)/shard_map/ppermute | solution.py:130
  150.8 1.5 copy-start.3
  152.3 0.6 copy-start.10
  152.9 0.6 copy-start.11
  153.6 68.6 %all-to-all-start.1 = ((bf16[128,8,1152]{2,1,0:T(8,128)(2,1)}), bf16[128,8,1152]{2,1,0:T(8,128)(2,1)S(1)}, u32[]{:S(2)}, u32[]{:S(2)}) async-start(bf16[128,8,1152]{2,1,0:T(8,128)(2,1)} %bitcast.55), calls=%async_computation.1 | async-start | bytes 4718592 | tf_op jit(solution)/shard_map/all_to_all | solution.py:212
  164.0 13.5 %collective-permute-start.1 = (bf16[128,512]{0,1:T(8,128)(2,1)}, bf16[128,512]{0,1:T(8,128)(2,1)}, u32[]{:S(2)}, u32[]{:S(2)}) collective-permute-start(bf16[128,512]{0,1:T(8,128)(2,1)} %copy.44), channel_id=1, source_target_pairs={{0,1},{1,0},{2,3},{3,2},{4,5},{5,4},{6,7},{7,6},{8,9},{9,8},{10,11... | collective-permute-start | bytes 393224 | tf_op jit(solution)/shard_map/ppermute | solution.py:130
  177.5 8.1 %copy-start.13 = (bf16[32,2,8,4096]{3,2,1,0:T(8,128)(2,1)S(1)}, bf16[32,2,8,4096]{3,2,1,0:T(8,128)(2,1)}, u32[]{:S(2)}) copy-start(bf16[32,2,8,4096]{3,2,1,0:T(8,128)(2,1)} %all-gather.8.cloned.1.call-done) | copy-start | bytes 12582916
  178.8 8.0 %copy-start.14 = (bf16[128,2,4,8,2,8]{0,5,4,3,2,1:T(8,128)(2,1)}, bf16[128,2,4,8,2,8]{0,5,4,3,2,1:T(8,128)(2,1)S(1)}, u32[]{:S(2)}) copy-start(bf16[128,2,4,8,2,8]{0,5,4,3,2,1:T(8,128)(2,1)S(1)} %copy.46) | copy-start | bytes 786436
  194.5 27.7 %copy-start.12 = (f32[512]{0:T(512)S(1)}, f32[512]{0:T(512)}, u32[]{:S(2)}) copy-start(f32[512]{0:T(512)} %param.10) | copy-start | bytes 6148
  194.6 14.5 %collective-permute-start.3 = (f32[128,512]{1,0:T(8,128)S(1)}, f32[128,512]{1,0:T(8,128)S(1)}, u32[]{:S(2)}, u32[]{:S(2)}) collective-permute-start(f32[128,512]{1,0:T(8,128)S(1)} %broadcast_select_fusion), channel_id=1, source_target_pairs={{0,1},{1,0},{2,3},{3,2},{4,5},{5,4},{6,7},{7,6},{8,9},{9,8},{10,11... | collective-permute-start | bytes 786440 | tf_op jit(solution)/shard_map/ppermute | solution.py:130
  222.2 1.6 copy-start.1
Sparse Core Ops, SparseCore 0:
  13.7 40.2 all-gather.5
  55.8 77.1 all-gather.7

commit v2 on v1

v2 whole, which is shorter than its diff:
```python
import jax
import jax.numpy as jnp
from jax import lax
from jax.experimental import pallas as pl
from jax.experimental.pallas import tpu as pltpu
from jax.sharding import Mesh, PartitionSpec as P

adapter_scale = 0.5
GROUPS = 4
SUB = ("y", "xl", "z", "c")
SPLIT = (4, 2, 8, 2)
bf16 = jnp.bfloat16
f32 = jnp.float32
OWNERS = SPLIT[0] * SPLIT[1] * SPLIT[2] * SPLIT[3]
VMEM = pl.BlockSpec(memory_space=pltpu.VMEM)
HBM = pl.BlockSpec(memory_space=pltpu.HBM)
PARAMS = pltpu.CompilerParams(vmem_limit_bytes=40 * 1024 * 1024)
WHOLE = pltpu.CompilerParams(vmem_limit_bytes=60 * 1024 * 1024)


def dot(a, b, da=1, db=0):
    return lax.dot_general(a, b, (((da,), (db,)), ((), ())), preferred_element_type=f32)


def iota(shape, dim):
    return lax.broadcasted_iota(jnp.int32, shape, dim)


def one(condition):
    return jnp.where(condition, 1.0, 0.0).astype(bf16)


def fetch(pairs, sems):
    copies = [pltpu.make_async_copy(a, b, sems.at[i]) for i, (a, b) in enumerate(pairs)]
    for copy in copies:
        copy.start()
    return copies


def pack_kernel(task_ref, slot_ref, tok_ref, cot_ref, out_ref, code_ref, stack, block, sems, out_sems):
    rows, width = tok_ref.shape
    tasks_all = slot_ref.shape[1]
    tw, cw = width // GROUPS, cot_ref.shape[1] // GROUPS
    chunk = out_ref.shape[0] // OWNERS
    task_dev = tasks_all // OWNERS
    pairs = []
    for g in range(GROUPS):
        at = pl.ds(g * rows, rows)
        pairs.append((tok_ref.at[:, pl.ds(g * tw, tw)], stack.at[at, pl.ds(0, tw)]))
        pairs.append((cot_ref.at[:, pl.ds(g * cw, cw)], stack.at[at, pl.ds(tw, cw)]))
    incoming = fetch(pairs, sems)
    slots = slot_ref[...]
    halves = jnp.concatenate([slots // task_dev, slots % task_dev] + [slots * 0] * 6, axis=0)
    blocks = task_ref.shape[1]
    picked = one(iota((tasks_all, blocks), 0) == task_ref[...])
    by_block = dot(halves.astype(f32).astype(bf16), picked).astype(bf16)
    wide = (blocks, GROUPS * rows)
    found = dot(by_block, one(iota(wide, 0) == (iota(wide, 1) % rows) // (rows // blocks)))
    owner = found[0:1, :].astype(jnp.int32)
    stack[:, tw + cw:] = dot(
        (found + 1.0).astype(bf16), one(iota((8, 128), 0) == 1), 0, 0
    ).astype(bf16)
    col = iota((1, GROUPS * rows), 1)
    code = owner * chunk + (col % (chunk // GROUPS)) * GROUPS + col // rows
    code_ref[...] = code
    step = out_ref.shape[0] // 4
    copies = []
    for copy in incoming:
        copy.wait()
    for b in range(4):
        part = slice(b * step, (b + 1) * step)
        hit = one(iota((step, GROUPS * rows), 0) + b * step == code)
        block[part, :tw + cw] = dot(hit, stack[:, :tw + cw]).astype(bf16)
        block[part, tw + cw:] = (dot(hit, stack[:, tw + cw:]) - 1.0).astype(bf16)
        copy = pltpu.make_async_copy(block.at[part], out_ref.at[part], out_sems.at[b])
        copy.start()
        copies.append(copy)
    for copy in copies:
        copy.wait()


def order(chunk, groups):
    out, src = iota((chunk, chunk), 0), iota((chunk, chunk), 1)
    per = chunk // groups
    return one(src == (out % per) * groups + out // per)


def reorder(chunk, groups):
    src, out = iota((chunk, chunk), 1), iota((chunk, chunk), 0)
    per = chunk // groups
    return one(out == (src % per) * groups + src // per)


def collapse(part, label, tasks, rank):
    total = jnp.zeros((part.shape[0], rank), f32)
    for j in range(tasks):
        total = total + jnp.where(label == j, part[:, j * rank:(j + 1) * rank], 0.0)
    return total


def spread(low, label, tasks):
    return jnp.concatenate(
        [jnp.where(label == j, low, 0.0) for j in range(tasks)], axis=1
    ).astype(bf16)


def rows_of(got_ref, rows, cots, label):
    tw, cw = rows.shape[1] // GROUPS, cots.shape[1] // GROUPS
    step = 256
    per = step // GROUPS
    to_rows = order(step, GROUPS)
    for b in range(got_ref.shape[0] // step):
        block = dot(to_rows, got_ref[b * step:(b + 1) * step, :]).astype(bf16)
        at = slice(b * per, (b + 1) * per)
        for g in range(GROUPS):
            piece = block[g * per:(g + 1) * per, :]
            rows[at, g * tw:(g + 1) * tw] = piece[:, :tw]
            cots[at, g * cw:(g + 1) * cw] = piece[:, tw:tw + cw]
        if label is not None:
            label[at, :] = block[:per, tw + cw:]


def owner_in_kernel(tasks, got_ref, down_ref, up_ref, low_ref, label_ref, rows, cots, down, sem):
    rank = down_ref.shape[0] // tasks
    copy = pltpu.make_async_copy(down_ref, down, sem)
    copy.start()
    rows_of(got_ref, rows, cots, label_ref)
    label = label_ref[...].astype(f32)[:, :rank]
    low_ref[:, rank:] = collapse(dot(cots[...], up_ref[...], 1, 1), label, tasks, rank)
    copy.wait()
    low_ref[:, :rank] = collapse(dot(rows[...], down[...], 1, 1), label, tasks, rank)


def wide_lows(tasks, rank, mine_ref, other_ref, label_ref):
    total = mine_ref[...] + other_ref[...]
    label = label_ref[...].astype(f32)[:, :rank]
    low = total[:, :rank].astype(bf16).astype(f32)
    grad = (adapter_scale * total[:, rank:]).astype(bf16).astype(f32)
    return spread(low, label, tasks), spread(grad, label, tasks)


def owner_out_kernel(
    tasks, mine_ref, other_ref, label_ref, down_ref, up_ref, out_ref, back, lora, sent, sems
):
    rank = down_ref.shape[0] // tasks
    width, key_part = down_ref.shape[1], up_ref.shape[1]
    tw, cw = width // GROUPS, key_part // GROUPS
    low_wide, grad_wide = wide_lows(tasks, rank, mine_ref, other_ref, label_ref)
    lora[...] = (adapter_scale * dot(low_wide, up_ref[...])).astype(bf16)
    for g in range(GROUPS):
        cols = slice(g * tw, (g + 1) * tw)
        back[:, cols] = dot(grad_wide, down_ref[:, cols]).astype(bf16)
    step = 256
    per = step // GROUPS
    to_sent = reorder(step, GROUPS)
    copies = []
    for b in range(out_ref.shape[0] // step):
        at = slice(b * per, (b + 1) * per)
        rows = jnp.concatenate([back[at, g * tw:(g + 1) * tw] for g in range(GROUPS)], axis=0)
        adds = jnp.concatenate([lora[at, g * cw:(g + 1) * cw] for g in range(GROUPS)], axis=0)
        part = slice(b * step, (b + 1) * step)
        sent[part, :tw] = dot(to_sent, rows).astype(bf16)
        sent[part, tw:] = dot(to_sent, adds).astype(bf16)
        copy = pltpu.make_async_copy(sent.at[part], out_ref.at[part], sems.at[b])
        copy.start()
        copies.append(copy)
    for copy in copies:
        copy.wait()


def gradients_kernel(
    tasks, got_ref, mine_ref, other_ref, label_ref, down_ref, up_ref, rows, cots
):
    rank = mine_ref.shape[1] // 2
    rows_of(got_ref, rows, cots, None)
    low_wide, grad_wide = wide_lows(tasks, rank, mine_ref, other_ref, label_ref)
    up_ref[...] = adapter_scale * dot(low_wide, cots[...], 0, 0)
    tw = rows.shape[1] // GROUPS
    for g in range(GROUPS):
        cols = slice(g * tw, (g + 1) * tw)
        down_ref[:, cols] = dot(grad_wide, rows[:, cols], 0, 0)


def base_kernel(place_ref, tok_ref, cot_ref, cot2_ref, *rest):
    held, (parts_ref, grad_ref, full, cots, sems) = rest[:-5], rest[-5:]
    y, c, seq = place_ref[0], place_ref[1], place_ref[2]
    width = tok_ref.shape[1]
    near = full.shape[0] // (2 * SPLIT[0])
    shard = near // (SPLIT[1] * SPLIT[2])
    block = 2 * near
    half = SPLIT[0] // 2
    pairs, count = [], len(held) // 2
    for i, ref in enumerate(held):
        rows, columns = ref.shape
        flip, back = i // count, i % count - 1
        if back < 0:
            at, first = 0, 0
        else:
            at, first = lax.rem(y + SPLIT[0] - back, SPLIT[0]), width - columns
        start = pl.multiple_of(flip * SPLIT[0] * near + at * near, near)
        pairs.append((ref, full.at[pl.ds(start, rows), pl.ds(first, columns)]))
    copies = fetch(pairs, sems)
    src, out = iota((near, block), 0), iota((near, block), 1)
    z, xl, k = src // (SPLIT[1] * shard), (src // shard) % SPLIT[1], src % shard
    places = []
    for flip in range(2):
        core = c if flip == 0 else 1 - c
        places.append(one(out == ((xl * SPLIT[2] + z) * SPLIT[3] + core) * shard + k))
    for at in range(SPLIT[0]):
        cols = slice((at % half) * block, (at % half + 1) * block)
        cot = jnp.where(seq == at // half, cot_ref[:, cols], cot2_ref[:, cols])
        for flip in range(2):
            first = (flip * SPLIT[0] + at) * near
            cots[:, first:first + near] = dot(cot, places[flip], 1, 1).astype(bf16)
    for copy in copies:
        copy.wait()
    part = dot(tok_ref[...], full[...], 1, 1)
    high = part.astype(bf16)
    left = part - high.astype(f32)
    mid = left.astype(bf16)
    low = (left - mid.astype(f32)).astype(bf16)
    for at in range(SPLIT[0]):
        moved = 0.0
        for flip in range(2):
            first = (flip * SPLIT[0] + at) * near
            for piece in (high, mid, low):
                moved = moved + dot(piece[:, first:first + near], places[flip])
        cols = slice((at % half) * block, (at % half + 1) * block)
        parts_ref[jnp.where(seq == at // half, 0, 1), :, cols] = moved
    tile = 1024
    for t in range(width // tile):
        cols = slice(t * tile, (t + 1) * tile)
        grad_ref[:, cols] = dot(cots[...], full[:, cols])


def finish_kernel(key_ref, got_ref, base_ref, frozen_ref, bias_ref, grad_ref, proj_ref):
    rows, width = grad_ref.shape
    key_part = proj_ref.shape[1]
    tw, cw = width // GROUPS, key_part // GROUPS
    key = jnp.concatenate([key_ref[...] + g for g in range(GROUPS)], axis=0)
    pick = one(key == iota((GROUPS * rows, got_ref.shape[0]), 1))
    step = 384
    for t in range((tw + cw) // step):
        found = dot(pick, got_ref[:, t * step:(t + 1) * step])
        keep = min(tw - t * step, step)
        for g in range(GROUPS):
            piece = found[g * rows:(g + 1) * rows, :]
            cols = slice(g * tw + t * step, g * tw + t * step + keep)
            grad_ref[:, cols] = (base_ref[:, cols] + piece[:, :keep]).astype(bf16)
            if keep < step:
                keys = slice(g * cw, (g + 1) * cw)
                proj_ref[:, keys] = (
                    frozen_ref[:, keys] + bias_ref[:, keys] + piece[:, keep:]
                ).astype(bf16)


def turn(value, shift):
    n = SPLIT[0]
    return lax.ppermute(value, "y", [(i, (i + shift) % n) for i in range(n)])


def swap(value, axis):
    return lax.ppermute(value, axis, [(0, 1), (1, 0)])


def on_device(tokens, weight, bias, adapter_down, adapter_up, cotangent, block_task, owner_slot):
    rows_dev, half_width = tokens.shape
    owners = OWNERS
    blocks_dev = block_task.shape[0]
    block_rows = rows_dev // blocks_dev
    task_dev, rank, key_part = adapter_up.shape
    chunk = block_rows * GROUPS
    sent_rows = owners * chunk
    tw, cw = half_width // GROUPS, key_part // GROUPS
    seq = lax.axis_index("seq")

    pair = swap(weight, "xl")
    first_x = lax.axis_index("xl") == 0
    pair = jnp.concatenate(
        [jnp.where(first_x, weight, pair), jnp.where(first_x, pair, weight)], axis=0
    )
    tokens_late, pair = lax.optimization_barrier((tokens, pair))
    sent, code = pl.pallas_call(
        pack_kernel,
        out_shape=(
            jax.ShapeDtypeStruct((sent_rows, tw + cw + 128), bf16),
            jax.ShapeDtypeStruct((1, GROUPS * rows_dev), jnp.int32),
        ),
        in_specs=[VMEM, VMEM, HBM, HBM],
        out_specs=(HBM, VMEM),
        scratch_shapes=[
            pltpu.VMEM((GROUPS * rows_dev, tw + cw + 128), bf16),
            pltpu.VMEM((sent_rows, tw + cw + 128), bf16),
            pltpu.SemaphoreType.DMA((2 * GROUPS,)),
            pltpu.SemaphoreType.DMA((4,)),
        ],
        compiler_params=WHOLE,
        name="pack",
    )(block_task[None, :], owner_slot[None, :], tokens_late, cotangent)
    got = lax.all_to_all(sent, SUB, split_axis=0, concat_axis=0, tiled=True)

    slab = lax.all_gather(pair, "z", axis=0, tiled=True)
    cut = half_width // 2
    whole = lax.all_gather(slab[:, :cut], "y", axis=0, tiled=True)
    own = [whole, slab[:, cut:]] + [turn(slab[:, cut:], shift) for shift in range(1, SPLIT[0])]
    weights = own + [swap(part, "c") for part in own]

    down_t = adapter_down.transpose(1, 2, 0).reshape(task_dev * rank, half_width)
    up_t = adapter_up.reshape(task_dev * rank, key_part)
    owner_rows = owners * block_rows
    low_mine, label_in = pl.pallas_call(
        lambda *refs: owner_in_kernel(task_dev, *refs),
        out_shape=(
            jax.ShapeDtypeStruct((owner_rows, 2 * rank), f32),
            jax.ShapeDtypeStruct((owner_rows, 128), bf16),
        ),
        in_specs=[VMEM, HBM, VMEM],
        out_specs=(VMEM,) * 2,
        scratch_shapes=[
            pltpu.VMEM((owner_rows, half_width), bf16),
            pltpu.VMEM((owner_rows, key_part), bf16),
            pltpu.VMEM(down_t.shape, bf16),
            pltpu.SemaphoreType.DMA,
        ],
        compiler_params=PARAMS,
        name="owner_in",
    )(got, down_t, up_t)
    low_other = swap(low_mine, "seq")
    to_return = pl.pallas_call(
        lambda *refs: owner_out_kernel(task_dev, *refs),
        out_shape=jax.ShapeDtypeStruct((sent_rows, tw + cw), bf16),
        in_specs=[VMEM] * 5,
        out_specs=HBM,
        scratch_shapes=[
            pltpu.VMEM((owner_rows, half_width), bf16),
            pltpu.VMEM((owner_rows, key_part), bf16),
            pltpu.VMEM((sent_rows, tw + cw), bf16),
            pltpu.SemaphoreType.DMA((4,)),
        ],
        compiler_params=PARAMS,
        name="owner_out",
    )(low_mine, low_other, label_in, down_t, up_t)
    to_return, _ = lax.optimization_barrier((to_return, own))
    returned = lax.all_to_all(to_return, SUB, split_axis=0, concat_axis=0, tiled=True)

    down_gradient, up_gradient = pl.pallas_call(
        lambda *refs: gradients_kernel(task_dev, *refs),
        out_shape=(
            jax.ShapeDtypeStruct((task_dev * rank, half_width), f32),
            jax.ShapeDtypeStruct((task_dev * rank, key_part), f32),
        ),
        in_specs=[VMEM] * 4,
        out_specs=(VMEM, VMEM),
        scratch_shapes=[
            pltpu.VMEM((owner_rows, half_width), bf16),
            pltpu.VMEM((owner_rows, key_part), bf16),
        ],
        compiler_params=PARAMS,
        name="gradients",
    )(got, low_mine, low_other, label_in)
    up_gradient = up_gradient.reshape(task_dev, rank, key_part)
    down_gradient = down_gradient.reshape(task_dev, rank, half_width).transpose(2, 0, 1)

    other_cot = swap(cotangent, "seq")
    places = jnp.stack([lax.axis_index("y"), lax.axis_index("c"), seq])
    parts, base_grad = pl.pallas_call(
        base_kernel,
        out_shape=(
            jax.ShapeDtypeStruct((2, rows_dev, key_part), f32),
            jax.ShapeDtypeStruct((rows_dev, half_width), f32),
        ),
        in_specs=[pl.BlockSpec(memory_space=pltpu.SMEM)] + [VMEM] * 3 + [HBM] * len(weights),
        out_specs=(VMEM, VMEM),
        scratch_shapes=[
            pltpu.VMEM((2 * key_part, half_width), bf16),
            pltpu.VMEM((rows_dev, 2 * key_part), bf16),
            pltpu.SemaphoreType.DMA((len(weights),)),
        ],
        compiler_params=PARAMS,
        name="base",
    )(places.astype(jnp.int32), tokens, cotangent, other_cot, *weights)
    frozen = parts[0] + swap(parts[1], "seq")

    row_key = code[0, :rows_dev]
    grad_tokens, projected = pl.pallas_call(
        finish_kernel,
        out_shape=(
            jax.ShapeDtypeStruct((rows_dev, half_width), bf16),
            jax.ShapeDtypeStruct((rows_dev, key_part), bf16),
        ),
        in_specs=[VMEM] * 5,
        out_specs=(VMEM, VMEM),
        compiler_params=PARAMS,
        name="finish",
    )(row_key[:, None], returned, base_grad, frozen, bias[None, :])
    return (projected, grad_tokens, down_gradient, up_gradient)


def solution(mesh):
    fine = Mesh(mesh.devices.reshape(SPLIT + (mesh.shape["seq"],)), SUB + ("seq",))
    return jax.shard_map(
        on_device,
        mesh=fine,
        in_specs=(
            P(SUB, "seq"),
            P(SUB, "seq"),
            P("seq"),
            P("seq", SUB, None),
            P(SUB, None, "seq"),
            P(SUB, "seq"),
            P(SUB),
            P(),
        ),
        out_specs=(
            P(SUB, "seq"),
            P(SUB, "seq"),
            P("seq", SUB, None),
            P(SUB, None, "seq"),
        ),
        check_vma=False,
    )
```

time: 234 us -> 206 us (0.88)
  waiting for transfers between devices: 141 us -> 109 us
  matrix products: 18.7 us -> 0 us
  Pallas kernels: 11.3 us -> 27.5 us
  starting transfers between devices: 26.3 us -> 36.7 us
  blocking collectives: 6.29 us -> 0 us
  local copies, waits for them, and re-layouts: 12.5 us -> 15.6 us
    all_gather x2, waiting for transfers between devices: 101 us -> 34 us  [the longest x1 32.6 us: on_device(): slab = lax.all_gather(pair, 'z', axis=0, tiled=True)]
    all_to_all x1, waiting for transfers between devices: 3.5 us -> 31.9 us  [on_device(): got = lax.all_to_all(sent, SUB, split_axis=0, concat_axis=0, tiled=True)]
    dot_general x6 -> x0, matrix products: 18.7 us -> none  [dot(): lax.dot_general(a, b, (((da,), (db,)), ((), ())), preferred_element_type=...]
    pallas_call x1 -> x3, Pallas kernels: 3.1 us -> 17.2 us  [the longest x1 8.3 us: on_device(): pl.pallas_call(base_kernel, out_shape=(jax.ShapeDtypeStruct((2, rows_dev,...]
    all_gather x1 -> x0, blocking collectives: 6.29 us -> none  [on_device(): stage = lax.all_gather(weight, 'xl', axis=0)]
    ppermute x4 -> x9, waiting for transfers between devices: 23 us -> 27.9 us  [swap(): return lax.ppermute(value, axis, [(0, 1), (1, 0)])]
    ppermute x0 -> x3, starting transfers between devices: none -> 4.44 us  [turn(): return lax.ppermute(value, 'y', [(i, (i + shift) % n) for i in range(n)])]
    ppermute x0 -> x3, waiting for transfers between devices: none -> 3.44 us  [turn(): return lax.ppermute(value, 'y', [(i, (i + shift) % n) for i in range(n)])]
  transfers between devices with their start and end apart: 8 -> 16, of which waited for: 7 -> 10; matrix products, arithmetic and copies ran while one was open for 11% -> 2% of each run, Pallas kernels for 4% -> 11%
where the time goes in v2:
time: 206 us; the launch traced here: 205 us
  waiting for transfers between devices  109 us (53%)
  starting transfers between devices  36.7 us (18%)
  Pallas kernels  27.5 us (13%)
  local copies, waits for them, and re-layouts  15.6 us (8%)
  between operations  14.2 us (7%)
  other arithmetic  2.58 us (1%)
    all_gather x1, waiting for transfers between devices, on_device(): slab = lax.all_gather(pair, 'z', axis=0, tiled=True)  32.6 us
    all_to_all x1, waiting for transfers between devices, on_device(): got = lax.all_to_all(sent, SUB, split_axis=0, concat_axis=0, tiled=True)  31.9 us
    ppermute x9, waiting for transfers between devices, swap(): return lax.ppermute(value, axis, [(0, 1), (1, 0)])  27.9 us
    all_to_all x1, starting transfers between devices, on_device(): got = lax.all_to_all(sent, SUB, split_axis=0, concat_axis=0, tiled=True)  13.5 us
    unnamed x36, local copies, waits for them, and re-layouts  12 us
    all_to_all x1, waiting for transfers between devices, on_device(): lax.all_to_all(to_return, SUB, split_axis=0, concat_axis=0, tiled=True)  11.3 us
    all_to_all x1, starting transfers between devices, on_device(): lax.all_to_all(to_return, SUB, split_axis=0, concat_axis=0, tiled=True)  10 us
    ppermute x9, starting transfers between devices, swap(): return lax.ppermute(value, axis, [(0, 1), (1, 0)])  8.7 us
  transfers between devices with their start and end apart: 16, of which 10 were waited for; matrix products, arithmetic and copies ran while one was open for 2% of the time, Pallas kernels for 11%

profile of v2, /device:TPU:32, one launch (start us, length us, event | category | flops | bytes accessed | tf_op | source)
XLA Modules:
  0.0 205.1 jit_solution(16689161655506217795)
XLA Ops:
  7.2 0.0 all-gather.3.cloned.1.call-start
  7.2 1.6 collective-permute-start
  8.8 3.0 %collective-permute-done = bf16[8,4096]{1,0:T(8,128)(2,1)S(1)} collective-permute-done((bf16[8,4096]{1,0:T(8,128)(2,1)}, bf16[8,4096]{1,0:T(8,128)(2,1)S(1)}, u32[]{:S(2)}, u32[]{:S(2)}) %collective-permute-start) | collective-permute-done | bytes 65568 | tf_op jit(solution)/shard_map/ppermute | solution.py:263
  11.8 0.9 broadcast_select_fusion.1
  12.6 0.7 pad_maximum_fusion
  13.3 5.3 %pack.1 = (bf16[1024,1280]{1,0:T(8,128)(2,1)}, s32[1,512]{1,0:T(1,128)}) custom-call(s32[1,64]{1,0:T(1,128)} %bitcast.34, s32[1,512]{1,0:T(1,128)} %bitcast.33, bf16[128,4096]{1,0:T(8,128)(2,1)} %tok_ref.2, bf16[128,512]{1,0:T(8,128)(2,1)} %cot_ref.3), custom_call_target="tpu_custom_call" | custom-call | tf_op jit(solution)/shard_map/pack/pallas_call | solution.py:283
  18.6 13.5 %all-to-all-start = ((bf16[128,8,1280]{2,1,0:T(8,128)(2,1)}), bf16[128,8,1280]{2,1,0:T(8,128)(2,1)S(1)}, u32[]{:S(2)}, u32[]{:S(2)}) async-start(bf16[128,8,1280]{2,1,0:T(8,128)(2,1)} %bitcast.32), calls=%async_computation | async-start | bytes 5242880 | tf_op jit(solution)/shard_map/all_to_all | solution.py:300
  32.1 0.0 all-gather.5.cloned.1.call-start
  32.1 32.6 %all-gather.3.cloned.1.call-done = bf16[128,4096]{1,0:T(8,128)(2,1)} async-done(((bf16[16,4096]{1,0:T(8,128)(2,1)}), bf16[128,4096]{1,0:T(8,128)(2,1)}) %all-gather.3.cloned.1.call-update) | async-done | bytes 1048592 | tf_op jit(solution)/shard_map/all_gather | solution.py:302
  64.8 2.1 %fusion = (bf16[128,2048]{1,0:T(8,128)(2,1)S(1)}, bf16[128,2048]{1,0:T(8,128)(2,1)}) fusion(bf16[128,4096]{1,0:T(8,128)(2,1)} %all-gather.3.cloned.1.call-done), kind=kLoop, calls=%fused_computation.7 | loop fusion | bytes 2097152 | tf_op jit(solution)/shard_map/slice | solution.py:305
  66.9 2.7 %collective-permute-start.4 = (bf16[128,2048]{1,0:T(8,128)(2,1)S(1)}, bf16[128,2048]{1,0:T(8,128)(2,1)}, u32[]{:S(2)}, u32[]{:S(2)}) collective-permute-start(bf16[128,2048]{1,0:T(8,128)(2,1)S(1)} %get-tuple-element.30.rest_1_), channel_id=1, source_target_pairs={{0,192},{64,0},{128,64},{192,128},{1,193},{65,1},{129,65},{193,129... | collective-permute-start | bytes 1572872 | tf_op jit(solution)/shard_map/ppermute | solution.py:259
  69.6 1.7 collective-permute-start.3
  71.3 31.9 %all-to-all-done = bf16[128,8,1280]{2,1,0:T(8,128)(2,1)S(1)} async-done(((bf16[128,8,1280]{2,1,0:T(8,128)(2,1)}), bf16[128,8,1280]{2,1,0:T(8,128)(2,1)S(1)}, u32[]{:S(2)}, u32[]{:S(2)}) %all-to-all-start) | async-done | bytes 2621472 | tf_op jit(solution)/shard_map/all_to_all | solution.py:300
  103.2 1.6 copy-done.1
  104.8 3.1 %owner_in.1 = (f32[256,128]{1,0:T(8,128)S(1)}, bf16[256,128]{1,0:T(8,128)(2,1)S(1)}) custom-call(bf16[1024,1280]{1,0:T(8,128)(2,1)S(1)} %bitcast.24, bf16[256,4096]{1,0:T(8,128)(2,1)S(1)} %bitcast.27, bf16[256,512]{1,0:T(8,128)(2,1)S(1)} %bitcast.29), custom_call_target="tpu_custom_call" | custom-call | tf_op jit(solution)/shard_map/owner_in/pallas_call | solution.py:311
  107.9 2.8 %collective-permute-start.1 = (f32[256,128]{1,0:T(8,128)S(1)}, f32[256,128]{1,0:T(8,128)S(1)}, u32[]{:S(2)}, u32[]{:S(2)}) collective-permute-start(f32[256,128]{1,0:T(8,128)S(1)} %get-tuple-element.20.refs_0_.refs_1_), channel_id=1, source_target_pairs={{0,1},{1,0},{2,3},{3,2},{4,5},{5,4},{6,7},{7,6},{8,9},{9,8},{10,11... | collective-permute-start | bytes 393224 | tf_op jit(solution)/shard_map/ppermute | solution.py:263
  110.7 3.8 %collective-permute-done.1.refs_1_.refs_2_ = f32[256,128]{1,0:T(8,128)S(1)} collective-permute-done((f32[256,128]{1,0:T(8,128)S(1)}, f32[256,128]{1,0:T(8,128)S(1)}, u32[]{:S(2)}, u32[]{:S(2)}) %collective-permute-start.1) | collective-permute-done | bytes 131104 | tf_op jit(solution)/shard_map/ppermute | solution.py:263
  114.5 2.8 %owner_out.1 = bf16[1024,1152]{1,0:T(8,128)(2,1)S(1)} custom-call(f32[256,128]{1,0:T(8,128)S(1)} %get-tuple-element.20.refs_0_.refs_1_, f32[256,128]{1,0:T(8,128)S(1)} %collective-permute-done.1.refs_1_.refs_2_, bf16[256,128]{1,0:T(8,128)(2,1)S(1)} %get-tuple-element.21.refs_2_.refs_3_, bf16[256,4096]{1,0:T(8,128)(2,1)S(1)} %bitcast.28, ...), custom_call_target="tpu_custom_call" | custom-call | tf_op jit(solution)/shard_map/owner_out/pallas_call | solution.py:329
  117.3 1.4 copy-done
  118.7 3.4 %collective-permute-done.3.rest_3_ = bf16[128,2048]{1,0:T(8,128)(2,1)} collective-permute-done((bf16[128,2048]{1,0:T(8,128)(2,1)S(1)}, bf16[128,2048]{1,0:T(8,128)(2,1)}, u32[]{:S(2)}, u32[]{:S(2)}) %collective-permute-start.3) | collective-permute-done | bytes 524320 | tf_op jit(solution)/shard_map/ppermute | solution.py:259
  122.2 1.3 all-gather.5.cloned.1.call-done.rest_0_
  123.5 10.0 %all-to-all-start.1 = ((bf16[128,8,1152]{2,1,0:T(8,128)(2,1)}), bf16[128,8,1152]{2,1,0:T(8,128)(2,1)}, u32[]{:S(2)}, u32[]{:S(2)}) async-start(bf16[128,8,1152]{2,1,0:T(8,128)(2,1)} %bitcast.26), calls=%async_computation.1 | async-start | bytes 4718592 | tf_op jit(solution)/shard_map/all_to_all | solution.py:344
  133.5 0.2 collective-permute-start.6
  133.8 2.8 %collective-permute-start.5 = (bf16[128,512]{1,0:T(8,128)(2,1)S(1)}, bf16[128,512]{1,0:T(8,128)(2,1)S(1)}, u32[]{:S(2)}, u32[]{:S(2)}) collective-permute-start(bf16[128,512]{1,0:T(8,128)(2,1)S(1)} %copy-done.8), channel_id=1, source_target_pairs={{0,1},{1,0},{2,3},{3,2},{4,5},{5,4},{6,7},{7,6},{8,9},{9,8},{10,11... | collective-permute-start | bytes 393224 | tf_op jit(solution)/shard_map/ppermute | solution.py:263
  136.6 0.1 collective-permute-start.7
  136.7 0.4 collective-permute-start.10
  137.1 0.1 collective-permute-start.8
  137.2 10.4 %collective-permute-done.5.cot2_ref = bf16[128,512]{1,0:T(8,128)(2,1)S(1)} collective-permute-done((bf16[128,512]{1,0:T(8,128)(2,1)S(1)}, bf16[128,512]{1,0:T(8,128)(2,1)S(1)}, u32[]{:S(2)}, u32[]{:S(2)}) %collective-permute-start.5) | collective-permute-done | bytes 131104 | tf_op jit(solution)/shard_map/ppermute | solution.py:263
  147.6 0.7 copy-done.15
  148.3 0.1 pad_add_fusion.place_ref
  148.4 2.2 %collective-permute-done.9.rest_8_ = bf16[128,2048]{1,0:T(8,128)(2,1)} collective-permute-done((bf16[128,2048]{1,0:T(8,128)(2,1)}, bf16[128,2048]{1,0:T(8,128)(2,1)}, u32[]{:S(2)}, u32[]{:S(2)}) %collective-permute-start.9) | collective-permute-done | bytes 524320 | tf_op jit(solution)/shard_map/ppermute | solution.py:263
  150.5 1.2 copy-done.3
  151.7 1.6 copy-done.4
  153.3 0.9 copy-done.16
  154.2 8.3 %base.1 = (f32[2,128,512]{2,1,0:T(8,128)S(1)}, f32[128,4096]{1,0:T(8,128)S(1)}) custom-call(s32[3]{0:T(128)S(1)} %pad_add_fusion.place_ref, bf16[128,4096]{1,0:T(8,128)(2,1)S(1)} %copy-done.3, bf16[128,512]{1,0:T(8,128)(2,1)S(1)} %copy-done.8, bf16[128,512]{1,0:T(8,128)(2,1)S(1)} %copy-done.16, bf16[512,2048]{1,0:T(8,128)(2,1)S(1)} %copy-done.4, ...), custom_call_target="tpu_custom_call" | custom-call | tf_op jit(solution)/shard_map/base/pallas_call | solution.py:366
  162.6 1.4 copy-done.5
  163.9 0.8 copy-done.11
  164.7 0.7 slice_bitcast_fusion
  165.4 0.7 collective-permute-start.11
  166.2 0.7 slice_bitcast_fusion.1
  166.8 0.1 copy.12.key_ref
  166.9 0.8 copy-done.14
  167.8 3.6 %gradients.1 = (f32[256,4096]{1,0:T(8,128)}, f32[256,512]{1,0:T(8,128)}) custom-call(bf16[1024,1280]{1,0:T(8,128)(2,1)S(1)} %bitcast.25, f32[256,128]{1,0:T(8,128)S(1)} %get-tuple-element.20.refs_0_.refs_1_, f32[256,128]{1,0:T(8,128)S(1)} %copy-done.10, bf16[256,128]{1,0:T(8,128)(2,1)S(1)} %copy-done.14), custom_call_target="tpu_custom_call" | custom-call | tf_op jit(solution)/shard_map/gradients/pallas_call | solution.py:346
  171.4 8.5 %collective-permute-done.11 = f32[128,512]{1,0:T(8,128)} collective-permute-done((f32[128,512]{1,0:T(8,128)}, f32[128,512]{1,0:T(8,128)}, u32[]{:S(2)}, u32[]{:S(2)}) %collective-permute-start.11) | collective-permute-done | bytes 262176 | tf_op jit(solution)/shard_map/ppermute | solution.py:263
  179.9 1.0 bitcast_add_fusion.frozen_ref
  180.9 11.3 %all-to-all-done.1 = bf16[128,8,1152]{2,1,0:T(8,128)(2,1)} async-done(((bf16[128,8,1152]{2,1,0:T(8,128)(2,1)}), bf16[128,8,1152]{2,1,0:T(8,128)(2,1)}, u32[]{:S(2)}, u32[]{:S(2)}) %all-to-all-start.1) | async-done | bytes 2359328 | tf_op jit(solution)/shard_map/all_to_all | solution.py:344
  192.2 1.6 copy-done.6
  193.8 4.5 %finish.1 = (bf16[128,4096]{1,0:T(8,128)(2,1)}, bf16[128,512]{1,0:T(8,128)(2,1)}) custom-call(s32[128,1]{1,0:T(8,128)S(1)} %copy.12.key_ref, bf16[1024,1152]{1,0:T(8,128)(2,1)} %bitcast.9.got_ref, f32[128,4096]{1,0:T(8,128)S(1)} %copy-done.6, f32[128,512]{1,0:T(8,128)S(1)} %bitcast_add_fusion.frozen_ref, f32[1,512]{1,0:T(1,128)S(1)} %bitcast.31), custom_call_target="tpu_custom_call" | custom-call | tf_op jit(solution)/shard_map/finish/pallas_call | solution.py:385
  (36 shorter events, 0.1 us)
Async XLA Ops:
  7.2 57.6 %all-gather.3.cloned.1.call-start = ((), (), s32[]{:S(2)}) async-start(), calls=%async_computation.2 | async-start | bytes 1179648 | tf_op jit(solution)/shard_map/all_gather | solution.py:302
  7.2 4.6 %collective-permute-start = (bf16[8,4096]{1,0:T(8,128)(2,1)}, bf16[8,4096]{1,0:T(8,128)(2,1)S(1)}, u32[]{:S(2)}, u32[]{:S(2)}) collective-permute-start(bf16[8,4096]{1,0:T(8,128)(2,1)} %param.9), channel_id=1, source_target_pairs={{0,32},{32,0},{1,33},{33,1},{2,34},{34,2},{3,35},{35,3},{4,36},{36... | collective-permute-start | bytes 196616 | tf_op jit(solution)/shard_map/ppermute | solution.py:263
  18.6 84.6 %all-to-all-start = ((bf16[128,8,1280]{2,1,0:T(8,128)(2,1)}), bf16[128,8,1280]{2,1,0:T(8,128)(2,1)S(1)}, u32[]{:S(2)}, u32[]{:S(2)}) async-start(bf16[128,8,1280]{2,1,0:T(8,128)(2,1)} %bitcast.32), calls=%async_computation | async-start | bytes 5242880 | tf_op jit(solution)/shard_map/all_to_all | solution.py:300
  32.1 71.1 %copy-start.7 = (bf16[4,64,512]{2,1,0:T(8,128)(2,1)S(1)}, bf16[4,64,512]{2,1,0:T(8,128)(2,1)}, u32[]{:S(2)}) copy-start(bf16[4,64,512]{2,1,0:T(8,128)(2,1)} %param.12) | copy-start | bytes 786436
  32.1 91.4 %all-gather.5.cloned.1.call-start = ((), (), s32[]{:S(2)}) async-start(), calls=%async_computation.3 | async-start | bytes 2621440 | tf_op jit(solution)/shard_map/all_gather | solution.py:304
  66.9 51.8 %collective-permute-start.4 = (bf16[128,2048]{1,0:T(8,128)(2,1)S(1)}, bf16[128,2048]{1,0:T(8,128)(2,1)}, u32[]{:S(2)}, u32[]{:S(2)}) collective-permute-start(bf16[128,2048]{1,0:T(8,128)(2,1)S(1)} %get-tuple-element.30.rest_1_), channel_id=1, source_target_pairs={{0,192},{64,0},{128,64},{192,128},{1,193},{65,1},{129,65},{193,129... | collective-permute-start | bytes 1572872 | tf_op jit(solution)/shard_map/ppermute | solution.py:259
  69.6 49.1 %collective-permute-start.2 = (bf16[128,2048]{1,0:T(8,128)(2,1)S(1)}, bf16[128,2048]{1,0:T(8,128)(2,1)}, u32[]{:S(2)}, u32[]{:S(2)}) collective-permute-start(bf16[128,2048]{1,0:T(8,128)(2,1)S(1)} %get-tuple-element.30.rest_1_), channel_id=1, source_target_pairs={{0,64},{64,128},{128,192},{192,0},{1,65},{65,129},{129,193},{193,1... | collective-permute-start | bytes 1572872 | tf_op jit(solution)/shard_map/ppermute | solution.py:259
  69.6 52.5 %collective-permute-start.3 = (bf16[128,2048]{1,0:T(8,128)(2,1)S(1)}, bf16[128,2048]{1,0:T(8,128)(2,1)}, u32[]{:S(2)}, u32[]{:S(2)}) collective-permute-start(bf16[128,2048]{1,0:T(8,128)(2,1)S(1)} %get-tuple-element.30.rest_1_), channel_id=1, source_target_pairs={{0,128},{64,192},{128,0},{192,64},{1,129},{65,193},{129,1},{193,65... | collective-permute-start | bytes 1572872 | tf_op jit(solution)/shard_map/ppermute | solution.py:259
  103.2 1.6 copy-start.1
  104.8 9.7 %copy-start.2 = (bf16[4096,4,64]{0,2,1:T(8,128)(2,1)S(1)}, bf16[4096,4,64]{0,2,1:T(8,128)(2,1)}, u32[]{:S(2)}) copy-start(bf16[4096,4,64]{0,2,1:T(8,128)(2,1)} %param.11) | copy-start | bytes 6291460
  107.9 9.3 %copy-start.13 = (bf16[256,128]{1,0:T(8,128)(2,1)}, bf16[256,128]{1,0:T(8,128)(2,1)S(1)}, u32[]{:S(2)}) copy-start(bf16[256,128]{1,0:T(8,128)(2,1)S(1)} %get-tuple-element.21.refs_2_.refs_3_) | copy-start | bytes 196612
  107.9 6.6 %collective-permute-start.1 = (f32[256,128]{1,0:T(8,128)S(1)}, f32[256,128]{1,0:T(8,128)S(1)}, u32[]{:S(2)}, u32[]{:S(2)}) collective-permute-start(f32[256,128]{1,0:T(8,128)S(1)} %get-tuple-element.20.refs_0_.refs_1_), channel_id=1, source_target_pairs={{0,1},{1,0},{2,3},{3,2},{4,5},{5,4},{6,7},{7,6},{8,9},{9,8},{10,11... | collective-permute-start | bytes 393224 | tf_op jit(solution)/shard_map/ppermute | solution.py:263
  114.5 2.8 %copy-start.9 = (f32[256,128]{1,0:T(8,128)}, f32[256,128]{1,0:T(8,128)S(1)}, u32[]{:S(2)}) copy-start(f32[256,128]{1,0:T(8,128)S(1)} %collective-permute-done.1.refs_1_.refs_2_) | copy-start | bytes 393220
  117.3 1.4 copy-start
  123.5 10.3 %copy-start.8 = (bf16[128,512]{1,0:T(8,128)(2,1)S(1)}, bf16[128,512]{1,0:T(8,128)(2,1)}, u32[]{:S(2)}) copy-start(bf16[128,512]{1,0:T(8,128)(2,1)} %cot_ref.3) | copy-start | bytes 393220
  123.5 68.7 %all-to-all-start.1 = ((bf16[128,8,1152]{2,1,0:T(8,128)(2,1)}), bf16[128,8,1152]{2,1,0:T(8,128)(2,1)}, u32[]{:S(2)}, u32[]{:S(2)}) async-start(bf16[128,8,1152]{2,1,0:T(8,128)(2,1)} %bitcast.26), calls=%async_computation.1 | async-start | bytes 4718592 | tf_op jit(solution)/shard_map/all_to_all | solution.py:344
  133.5 17.0 %collective-permute-start.6 = (bf16[512,2048]{1,0:T(8,128)(2,1)}, bf16[512,2048]{1,0:T(8,128)(2,1)}, u32[]{:S(2)}, u32[]{:S(2)}) collective-permute-start(bf16[512,2048]{1,0:T(8,128)(2,1)} %all-gather.5.cloned.1.call-done.rest_0_), channel_id=1, source_target_pairs={{0,2},{2,0},{1,3},{3,1},{4,6},{6,4},{5,7},{7,5},{8,10},{10,8},{9,1... | collective-permute-start | bytes 6291464 | tf_op jit(solution)/shard_map/ppermute | solution.py:263
  133.8 13.8 %collective-permute-start.5 = (bf16[128,512]{1,0:T(8,128)(2,1)S(1)}, bf16[128,512]{1,0:T(8,128)(2,1)S(1)}, u32[]{:S(2)}, u32[]{:S(2)}) collective-permute-start(bf16[128,512]{1,0:T(8,128)(2,1)S(1)} %copy-done.8), channel_id=1, source_target_pairs={{0,1},{1,0},{2,3},{3,2},{4,5},{5,4},{6,7},{7,6},{8,9},{9,8},{10,11... | collective-permute-start | bytes 393224 | tf_op jit(solution)/shard_map/ppermute | solution.py:263
  136.6 11.7 %collective-permute-start.7 = (bf16[128,2048]{1,0:T(8,128)(2,1)S(1)}, bf16[128,2048]{1,0:T(8,128)(2,1)}, u32[]{:S(2)}, u32[]{:S(2)}) collective-permute-start(bf16[128,2048]{1,0:T(8,128)(2,1)S(1)} %get-tuple-element.30.rest_1_), channel_id=1, source_target_pairs={{0,2},{2,0},{1,3},{3,1},{4,6},{6,4},{5,7},{7,5},{8,10},{10,8},{9,1... | collective-permute-start | bytes 1572872 | tf_op jit(solution)/shard_map/ppermute | solution.py:263
  136.7 11.7 %collective-permute-start.10 = (bf16[128,2048]{1,0:T(8,128)(2,1)}, bf16[128,2048]{1,0:T(8,128)(2,1)}, u32[]{:S(2)}, u32[]{:S(2)}) collective-permute-start(bf16[128,2048]{1,0:T(8,128)(2,1)} %collective-permute-done.4.rest_4_), channel_id=1, source_target_pairs={{0,2},{2,0},{1,3},{3,1},{4,6},{6,4},{5,7},{7,5},{8,10},{10,8},{9,1... | collective-permute-start | bytes 1572872 | tf_op jit(solution)/shard_map/ppermute | solution.py:263
  137.1 11.2 %collective-permute-start.8 = (bf16[128,2048]{1,0:T(8,128)(2,1)}, bf16[128,2048]{1,0:T(8,128)(2,1)}, u32[]{:S(2)}, u32[]{:S(2)}) collective-permute-start(bf16[128,2048]{1,0:T(8,128)(2,1)} %collective-permute-done.2.rest_2_), channel_id=1, source_target_pairs={{0,2},{2,0},{1,3},{3,1},{4,6},{6,4},{5,7},{7,5},{8,10},{10,8},{9,1... | collective-permute-start | bytes 1572872 | tf_op jit(solution)/shard_map/ppermute | solution.py:263
  147.6 0.7 copy-start.15
  148.3 2.3 %collective-permute-start.9 = (bf16[128,2048]{1,0:T(8,128)(2,1)}, bf16[128,2048]{1,0:T(8,128)(2,1)}, u32[]{:S(2)}, u32[]{:S(2)}) collective-permute-start(bf16[128,2048]{1,0:T(8,128)(2,1)} %collective-permute-done.3.rest_3_), channel_id=1, source_target_pairs={{0,2},{2,0},{1,3},{3,1},{4,6},{6,4},{5,7},{7,5},{8,10},{10,8},{9,1... | collective-permute-start | bytes 1572872 | tf_op jit(solution)/shard_map/ppermute | solution.py:263
  150.5 1.2 copy-start.3
  151.7 1.6 copy-start.4
  153.3 0.9 copy-start.16
  154.2 12.7 %copy-start.10 = (f32[256,128]{1,0:T(8,128)S(1)}, f32[256,128]{1,0:T(8,128)}, u32[]{:S(2)}) copy-start(f32[256,128]{1,0:T(8,128)} %copy-done.9) | copy-start | bytes 393220
  162.5 1.4 copy-start.5
  163.9 0.8 copy-start.11
  163.9 28.3 %copy-start.17 = (f32[512]{0:T(512)S(1)}, f32[512]{0:T(512)}, u32[]{:S(2)}) copy-start(f32[512]{0:T(512)} %param.10) | copy-start | bytes 6148
  165.4 14.4 %copy-start.12 = (f32[2,128,512]{2,1,0:T(8,128)S(1)}, f32[2,128,512]{2,1,0:T(8,128)}, u32[]{:S(2)}) copy-start(f32[2,128,512]{2,1,0:T(8,128)} %copy-done.11) | copy-start | bytes 1572868
  165.4 14.4 %collective-permute-start.11 = (f32[128,512]{1,0:T(8,128)}, f32[128,512]{1,0:T(8,128)}, u32[]{:S(2)}, u32[]{:S(2)}) collective-permute-start(f32[128,512]{1,0:T(8,128)} %slice_bitcast_fusion), channel_id=1, source_target_pairs={{0,1},{1,0},{2,3},{3,2},{4,5},{5,4},{6,7},{7,6},{8,9},{9,8},{10,11... | collective-permute-start | bytes 786440 | tf_op jit(solution)/shard_map/ppermute | solution.py:263
  166.9 0.8 copy-start.14
  192.2 1.6 copy-start.6
Sparse Core Ops, SparseCore 0:
  13.4 51.3 all-gather.2
  67.2 56.2 all-gather.4

commit v3 on v2

--- a/solution.py
+++ b/solution.py
@@ -1,3 +1,5 @@
+import functools
+
 import jax
 import jax.numpy as jnp
 from jax import lax
@@ -181,37 +183,34 @@
         down_ref[:, cols] = dot(grad_wide, rows[:, cols], 0, 0)
 
 
-def base_kernel(place_ref, tok_ref, cot_ref, cot2_ref, *rest):
-    held, (parts_ref, grad_ref, full, cots, sems) = rest[:-5], rest[-5:]
-    y, c, seq = place_ref[0], place_ref[1], place_ref[2]
+def base_kernel(flip, place_ref, tok_ref, cot_ref, cot2_ref, *rest):
+    held, rest = rest[:1 + SPLIT[0]], rest[1 + SPLIT[0]:]
+    before, (parts_ref, grad_ref, full, cots, sems) = rest[:-5], rest[-5:]
+    y, xl, c, seq = (place_ref[i] for i in range(4))
     width = tok_ref.shape[1]
-    near = full.shape[0] // (2 * SPLIT[0])
+    near = full.shape[0] // SPLIT[0]
     shard = near // (SPLIT[1] * SPLIT[2])
     block = 2 * near
     half = SPLIT[0] // 2
-    pairs, count = [], len(held) // 2
-    for i, ref in enumerate(held):
+    pairs = []
+    for back, ref in enumerate(held, -1):
         rows, columns = ref.shape
-        flip, back = i // count, i % count - 1
         if back < 0:
             at, first = 0, 0
         else:
             at, first = lax.rem(y + SPLIT[0] - back, SPLIT[0]), width - columns
-        start = pl.multiple_of(flip * SPLIT[0] * near + at * near, near)
+        start = pl.multiple_of(at * near, near)
         pairs.append((ref, full.at[pl.ds(start, rows), pl.ds(first, columns)]))
     copies = fetch(pairs, sems)
     src, out = iota((near, block), 0), iota((near, block), 1)
-    z, xl, k = src // (SPLIT[1] * shard), (src // shard) % SPLIT[1], src % shard
-    places = []
-    for flip in range(2):
-        core = c if flip == 0 else 1 - c
-        places.append(one(out == ((xl * SPLIT[2] + z) * SPLIT[3] + core) * shard + k))
+    xl_of = (src // (SPLIT[2] * shard) + xl) % SPLIT[1]
+    z, k = (src // shard) % SPLIT[2], src % shard
+    core = c if flip == 0 else 1 - c
+    place = one(out == ((xl_of * SPLIT[2] + z) * SPLIT[3] + core) * shard + k)
     for at in range(SPLIT[0]):
         cols = slice((at % half) * block, (at % half + 1) * block)
         cot = jnp.where(seq == at // half, cot_ref[:, cols], cot2_ref[:, cols])
-        for flip in range(2):
-            first = (flip * SPLIT[0] + at) * near
-            cots[:, first:first + near] = dot(cot, places[flip], 1, 1).astype(bf16)
+        cots[:, at * near:(at + 1) * near] = dot(cot, place, 1, 1).astype(bf16)
     for copy in copies:
         copy.wait()
     part = dot(tok_ref[...], full[...], 1, 1)
@@ -221,16 +220,20 @@
     low = (left - mid.astype(f32)).astype(bf16)
     for at in range(SPLIT[0]):
         moved = 0.0
-        for flip in range(2):
-            first = (flip * SPLIT[0] + at) * near
-            for piece in (high, mid, low):
-                moved = moved + dot(piece[:, first:first + near], places[flip])
+        for piece in (high, mid, low):
+            moved = moved + dot(piece[:, at * near:(at + 1) * near], place)
         cols = slice((at % half) * block, (at % half + 1) * block)
-        parts_ref[jnp.where(seq == at // half, 0, 1), :, cols] = moved
+        which = jnp.where(seq == at // half, 0, 1)
+        if before:
+            moved = moved + before[0][which, :, cols]
+        parts_ref[which, :, cols] = moved
     tile = 1024
     for t in range(width // tile):
         cols = slice(t * tile, (t + 1) * tile)
-        grad_ref[:, cols] = dot(cots[...], full[:, cols])
+        total = dot(cots[...], full[:, cols])
+        if before:
+            total = total + before[1][:, cols]
+        grad_ref[:, cols] = total
 
 
 def finish_kernel(key_ref, got_ref, base_ref, frozen_ref, bias_ref, grad_ref, proj_ref):
@@ -274,12 +277,6 @@
     tw, cw = half_width // GROUPS, key_part // GROUPS
     seq = lax.axis_index("seq")
 
-    pair = swap(weight, "xl")
-    first_x = lax.axis_index("xl") == 0
-    pair = jnp.concatenate(
-        [jnp.where(first_x, weight, pair), jnp.where(first_x, pair, weight)], axis=0
-    )
-    tokens_late, pair = lax.optimization_barrier((tokens, pair))
     sent, code = pl.pallas_call(
         pack_kernel,
         out_shape=(
@@ -296,14 +293,17 @@
         ],
         compiler_params=WHOLE,
         name="pack",
-    )(block_task[None, :], owner_slot[None, :], tokens_late, cotangent)
+    )(block_task[None, :], owner_slot[None, :], tokens, cotangent)
+    sent, other_cot = lax.optimization_barrier((sent, swap(cotangent, "seq")))
     got = lax.all_to_all(sent, SUB, split_axis=0, concat_axis=0, tiled=True)
 
-    slab = lax.all_gather(pair, "z", axis=0, tiled=True)
-    cut = half_width // 2
+    slab = lax.all_gather(weight, ("z", "c"), axis=0).reshape(SPLIT[2], 2, -1, half_width)
+    slab = lax.dynamic_index_in_dim(slab, lax.axis_index("c"), 1, keepdims=False)
+    slab = slab.reshape(-1, half_width)
+    slab = jnp.concatenate([slab, swap(slab, "xl")], axis=0)
+    cut = half_width * 3 // 4
     whole = lax.all_gather(slab[:, :cut], "y", axis=0, tiled=True)
     own = [whole, slab[:, cut:]] + [turn(slab[:, cut:], shift) for shift in range(1, SPLIT[0])]
-    weights = own + [swap(part, "c") for part in own]
 
     down_t = adapter_down.transpose(1, 2, 0).reshape(task_dev * rank, half_width)
     up_t = adapter_up.reshape(task_dev * rank, key_part)
@@ -340,7 +340,7 @@
         compiler_params=PARAMS,
         name="owner_out",
     )(low_mine, low_other, label_in, down_t, up_t)
-    to_return, _ = lax.optimization_barrier((to_return, own))
+    to_return, _ = lax.optimization_barrier((to_return, own[1:]))
     returned = lax.all_to_all(to_return, SUB, split_axis=0, concat_axis=0, tiled=True)
 
     down_gradient, up_gradient = pl.pallas_call(
@@ -361,24 +361,27 @@
     up_gradient = up_gradient.reshape(task_dev, rank, key_part)
     down_gradient = down_gradient.reshape(task_dev, rank, half_width).transpose(2, 0, 1)
 
-    other_cot = swap(cotangent, "seq")
-    places = jnp.stack([lax.axis_index("y"), lax.axis_index("c"), seq])
-    parts, base_grad = pl.pallas_call(
-        base_kernel,
-        out_shape=(
-            jax.ShapeDtypeStruct((2, rows_dev, key_part), f32),
-            jax.ShapeDtypeStruct((rows_dev, half_width), f32),
-        ),
-        in_specs=[pl.BlockSpec(memory_space=pltpu.SMEM)] + [VMEM] * 3 + [HBM] * len(weights),
-        out_specs=(VMEM, VMEM),
-        scratch_shapes=[
-            pltpu.VMEM((2 * key_part, half_width), bf16),
-            pltpu.VMEM((rows_dev, 2 * key_part), bf16),
-            pltpu.SemaphoreType.DMA((len(weights),)),
-        ],
-        compiler_params=PARAMS,
-        name="base",
-    )(places.astype(jnp.int32), tokens, cotangent, other_cot, *weights)
+    places = jnp.stack([lax.axis_index("y"), lax.axis_index("xl"), lax.axis_index("c"), seq])
+    before = ()
+    for flip, held in enumerate((own, [swap(part, "c") for part in own])):
+        before = pl.pallas_call(
+            functools.partial(base_kernel, flip),
+            out_shape=(
+                jax.ShapeDtypeStruct((2, rows_dev, key_part), f32),
+                jax.ShapeDtypeStruct((rows_dev, half_width), f32),
+            ),
+            in_specs=[pl.BlockSpec(memory_space=pltpu.SMEM)]
+            + [VMEM] * 3 + [HBM] * len(held) + [VMEM] * len(before),
+            out_specs=(VMEM, VMEM),
+            scratch_shapes=[
+                pltpu.VMEM((key_part, half_width), bf16),
+                pltpu.VMEM((rows_dev, key_part), bf16),
+                pltpu.SemaphoreType.DMA((len(held),)),
+            ],
+            compiler_params=PARAMS,
+            name=("base_own", "base_other")[flip],
+        )(places.astype(jnp.int32), tokens, cotangent, other_cot, *held, *before)
+    parts, base_grad = before
     frozen = parts[0] + swap(parts[1], "seq")
 
     row_key = code[0, :rows_dev]

time: 206 us -> 191 us (0.927)
  waiting for transfers between devices: 109 us -> 93.4 us
    all_to_all x1, waiting for transfers between devices: 31.9 us -> 7.3 us  [on_device(): got = lax.all_to_all(sent, SUB, split_axis=0, concat_axis=0, tiled=True)]
    all_gather x1, waiting for transfers between devices: 1.34 us -> 16.7 us  [on_device(): whole = lax.all_gather(slab[:, :cut], 'y', axis=0, tiled=True)]
    all_gather x1, waiting for transfers between devices: 32.6 us -> 25.8 us  [on_device(): lax.all_gather(weight, ('z', 'c'), axis=0)]
    ppermute x9, waiting for transfers between devices: 27.9 us -> 32.9 us  [swap(): return lax.ppermute(value, axis, [(0, 1), (1, 0)])]
    all_to_all x1, starting transfers between devices: 10 us -> 6.56 us  [on_device(): lax.all_to_all(to_return, SUB, split_axis=0, concat_axis=0, tiled=True)]
    ppermute x3, waiting for transfers between devices: 3.44 us -> 0.01 us  [turn(): return lax.ppermute(value, 'y', [(i, (i + shift) % n) for i in range(n)])]
    ppermute x9, starting transfers between devices: 8.7 us -> 11 us  [swap(): return lax.ppermute(value, axis, [(0, 1), (1, 0)])]
    slice x1 -> x0, local copies, waits for them, and re-layouts: 2.08 us -> none  [on_device(): slab[:, cut:]]
  transfers between devices with their start and end apart: 16 -> 16, of which waited for: 10 -> 7; matrix products, arithmetic and copies ran while one was open for 2% -> 3% of each run, Pallas kernels for 11% -> 13%
where the time goes in v3:
time: 191 us; the launch traced here: 190 us
  waiting for transfers between devices  93.4 us (49%)
  starting transfers between devices  36.5 us (19%)
  Pallas kernels  29.1 us (15%)
  between operations  14.2 us (7%)
  local copies, waits for them, and re-layouts  14.1 us (7%)
  other arithmetic  2.99 us (2%)
    ppermute x9, waiting for transfers between devices, swap(): return lax.ppermute(value, axis, [(0, 1), (1, 0)])  32.9 us
    all_gather x1, waiting for transfers between devices, on_device(): lax.all_gather(weight, ('z', 'c'), axis=0)  25.8 us
    all_gather x1, waiting for transfers between devices, on_device(): whole = lax.all_gather(slab[:, :cut], 'y', axis=0, tiled=True)  16.7 us
    all_to_all x1, starting transfers between devices, on_device(): got = lax.all_to_all(sent, SUB, split_axis=0, concat_axis=0, tiled=True)  12.6 us
    unnamed x34, local copies, waits for them, and re-layouts  11.5 us
    ppermute x9, starting transfers between devices, swap(): return lax.ppermute(value, axis, [(0, 1), (1, 0)])  11 us
    all_to_all x1, waiting for transfers between devices, on_device(): lax.all_to_all(to_return, SUB, split_axis=0, concat_axis=0, tiled=True)  9.95 us
    pallas_call x2, Pallas kernels, on_device(): pl.pallas_call(functools.partial(base_kernel, flip), out_shape=(jax.Shape...  9.94 us
  transfers between devices with their start and end apart: 16, of which 7 were waited for; matrix products, arithmetic and copies ran while one was open for 3% of the time, Pallas kernels for 13%

profile of v3, /device:TPU:32, one launch (start us, length us, event | category | flops | bytes accessed | tf_op | source)
XLA Modules:
  0.0 190.3 jit_solution(12450021104302890778)
XLA Ops:
  7.2 0.0 all-gather.6.cloned.1.call-start
  7.2 0.7 all-gather.6.cloned.1.call-update
  7.9 3.1 %collective-permute-start = (bf16[128,512]{1,0:T(8,128)(2,1)}, bf16[128,512]{1,0:T(8,128)(2,1)S(1)}, u32[]{:S(2)}, u32[]{:S(2)}) collective-permute-start(bf16[128,512]{1,0:T(8,128)(2,1)} %cot_ref.5), channel_id=1, source_target_pairs={{0,1},{1,0},{2,3},{3,2},{4,5},{5,4},{6,7},{7,6},{8,9},{9,8},{10,11... | collective-permute-start | bytes 393224 | tf_op jit(solution)/shard_map/ppermute | solution.py:266
  11.0 5.2 %pack.1 = (bf16[1024,1280]{1,0:T(8,128)(2,1)}, s32[1,512]{1,0:T(1,128)}) custom-call(s32[1,64]{1,0:T(1,128)} %bitcast.41, s32[1,512]{1,0:T(1,128)} %bitcast.40, bf16[128,4096]{1,0:T(8,128)(2,1)} %tok_ref.5, bf16[128,512]{1,0:T(8,128)(2,1)} %cot_ref.5), custom_call_target="tpu_custom_call" | custom-call | tf_op jit(solution)/shard_map/pack/pallas_call | solution.py:280
  16.3 12.6 %all-to-all-start = ((bf16[128,8,1280]{2,1,0:T(8,128)(2,1)}), bf16[128,8,1280]{2,1,0:T(8,128)(2,1)S(1)}, u32[]{:S(2)}, u32[]{:S(2)}) async-start(bf16[128,8,1280]{2,1,0:T(8,128)(2,1)} %bitcast.38), calls=%async_computation | async-start | bytes 5242880 | tf_op jit(solution)/shard_map/all_to_all | solution.py:298
  28.8 0.0 all-gather.4.cloned.1.call-start
  28.9 25.8 %all-gather.6.cloned.1.call-done = bf16[128,4096]{1,0:T(8,128)(2,1)} async-done(((bf16[8,4096]{1,0:T(8,128)(2,1)}), bf16[128,4096]{1,0:T(8,128)(2,1)}) %all-gather.6.cloned.1.call-update) | async-done | bytes 1048592 | tf_op jit(solution)/shard_map/all_gather | solution.py:300
  54.7 1.1 dynamic-slice_bitcast_fusion
  55.8 1.7 collective-permute-start.2
  57.6 23.0 %collective-permute-done.2 = bf16[64,4096]{1,0:T(8,128)(2,1)S(1)} collective-permute-done((bf16[64,4096]{1,0:T(8,128)(2,1)S(1)}, bf16[64,4096]{1,0:T(8,128)(2,1)S(1)}, u32[]{:S(2)}, u32[]{:S(2)}) %collective-permute-start.2) | collective-permute-done | bytes 524320 | tf_op jit(solution)/shard_map/ppermute | solution.py:266
  80.6 0.8 copy-done.16
  81.3 0.9 pad_maximum_fusion
  82.3 1.0 pad_maximum_fusion.1.rest_1_
  83.3 2.3 %collective-permute-start.3 = (bf16[128,1024]{1,0:T(8,128)(2,1)S(1)}, bf16[128,1024]{1,0:T(8,128)(2,1)}, u32[]{:S(2)}, u32[]{:S(2)}) collective-permute-start(bf16[128,1024]{1,0:T(8,128)(2,1)S(1)} %pad_maximum_fusion.1.rest_1_), channel_id=1, source_target_pairs={{0,64},{64,128},{128,192},{192,0},{1,65},{65,129},{129,193},{193,1... | collective-permute-start | bytes 786440 | tf_op jit(solution)/shard_map/ppermute | solution.py:262
  85.6 1.5 collective-permute-start.4
  87.1 2.5 %collective-permute-start.5 = (bf16[128,1024]{1,0:T(8,128)(2,1)S(1)}, bf16[128,1024]{1,0:T(8,128)(2,1)}, u32[]{:S(2)}, u32[]{:S(2)}) collective-permute-start(bf16[128,1024]{1,0:T(8,128)(2,1)S(1)} %pad_maximum_fusion.1.rest_1_), channel_id=1, source_target_pairs={{0,192},{64,0},{128,64},{192,128},{1,193},{65,1},{129,65},{193,129... | collective-permute-start | bytes 786440 | tf_op jit(solution)/shard_map/ppermute | solution.py:262
  89.6 7.3 %all-to-all-done = bf16[128,8,1280]{2,1,0:T(8,128)(2,1)S(1)} async-done(((bf16[128,8,1280]{2,1,0:T(8,128)(2,1)}), bf16[128,8,1280]{2,1,0:T(8,128)(2,1)S(1)}, u32[]{:S(2)}, u32[]{:S(2)}) %all-to-all-start) | async-done | bytes 2621472 | tf_op jit(solution)/shard_map/all_to_all | solution.py:298
  96.9 1.6 copy-done.3
  98.5 3.1 %owner_in.1 = (f32[256,128]{1,0:T(8,128)S(1)}, bf16[256,128]{1,0:T(8,128)(2,1)S(1)}) custom-call(bf16[1024,1280]{1,0:T(8,128)(2,1)S(1)} %bitcast.30, bf16[256,4096]{1,0:T(8,128)(2,1)S(1)} %bitcast.33, bf16[256,512]{1,0:T(8,128)(2,1)S(1)} %bitcast.35), custom_call_target="tpu_custom_call" | custom-call | tf_op jit(solution)/shard_map/owner_in/pallas_call | solution.py:311
  101.6 2.5 %collective-permute-start.1 = (f32[256,128]{1,0:T(8,128)S(1)}, f32[256,128]{1,0:T(8,128)S(1)}, u32[]{:S(2)}, u32[]{:S(2)}) collective-permute-start(f32[256,128]{1,0:T(8,128)S(1)} %get-tuple-element.22.refs_0_.refs_1_), channel_id=1, source_target_pairs={{0,1},{1,0},{2,3},{3,2},{4,5},{5,4},{6,7},{7,6},{8,9},{9,8},{10,11... | collective-permute-start | bytes 393224 | tf_op jit(solution)/shard_map/ppermute | solution.py:266
  104.1 4.2 %collective-permute-done.1.refs_1_.refs_2_ = f32[256,128]{1,0:T(8,128)S(1)} collective-permute-done((f32[256,128]{1,0:T(8,128)S(1)}, f32[256,128]{1,0:T(8,128)S(1)}, u32[]{:S(2)}, u32[]{:S(2)}) %collective-permute-start.1) | collective-permute-done | bytes 131104 | tf_op jit(solution)/shard_map/ppermute | solution.py:266
  108.3 2.7 %owner_out.1 = bf16[1024,1152]{1,0:T(8,128)(2,1)S(1)} custom-call(f32[256,128]{1,0:T(8,128)S(1)} %get-tuple-element.22.refs_0_.refs_1_, f32[256,128]{1,0:T(8,128)S(1)} %collective-permute-done.1.refs_1_.refs_2_, bf16[256,128]{1,0:T(8,128)(2,1)S(1)} %get-tuple-element.23.refs_2_.refs_3_, bf16[256,4096]{1,0:T(8,128)(2,1)S(1)} %bitcast.34, ...), custom_call_target="tpu_custom_call" | custom-call | tf_op jit(solution)/shard_map/owner_out/pallas_call | solution.py:329
  111.1 1.4 copy-done
  112.5 6.6 %all-to-all-start.1 = ((bf16[128,8,1152]{2,1,0:T(8,128)(2,1)}), bf16[128,8,1152]{2,1,0:T(8,128)(2,1)}, u32[]{:S(2)}, u32[]{:S(2)}) async-start(bf16[128,8,1152]{2,1,0:T(8,128)(2,1)} %bitcast.32), calls=%async_computation.1 | async-start | bytes 4718592 | tf_op jit(solution)/shard_map/all_to_all | solution.py:344
  119.1 16.7 %all-gather.4.cloned.1.call-done.rest_0_ = bf16[512,3072]{1,0:T(8,128)(2,1)} async-done(((bf16[128,3072]{1,0:T(8,128)(2,1)}), bf16[512,3072]{1,0:T(8,128)(2,1)}) %all-gather.4.cloned.1.call-update) | async-done | bytes 3145744 | tf_op jit(solution)/shard_map/all_gather | solution.py:305
  135.8 0.1 collective-permute-start.6
  135.8 0.5 collective-permute-start.7
  136.3 0.1 collective-permute-start.10
  136.3 0.5 collective-permute-start.8
  136.8 0.1 collective-permute-start.9
  136.9 0.1 pad_add_fusion.place_ref
  136.9 1.2 copy-done.1
  138.2 1.9 copy-done.5
  140.1 4.6 %base_own.1 = (f32[2,128,512]{2,1,0:T(8,128)S(1)}, f32[128,4096]{1,0:T(8,128)S(1)}) custom-call(s32[4]{0:T(128)S(1)} %pad_add_fusion.place_ref, bf16[128,4096]{1,0:T(8,128)(2,1)S(1)} %copy-done.1, bf16[128,512]{1,0:T(8,128)(2,1)S(1)} %copy-done.8, bf16[128,512]{1,0:T(8,128)(2,1)S(1)} %collective-permute-done.cot2_ref, bf16[512,3072]{1,0:T(8,128)(2,1)S(1)} %copy-done.5, ...), custom_call_target="tpu_custom_call" | custom-call | tf_op jit(solution)/shard_map/base_own/pallas_call | solution.py:367
  144.8 5.3 %base_other.1 = (f32[2,128,512]{2,1,0:T(8,128)S(1)}, f32[128,4096]{1,0:T(8,128)S(1)}) custom-call(s32[4]{0:T(128)S(1)} %pad_add_fusion.place_ref, bf16[128,4096]{1,0:T(8,128)(2,1)S(1)} %copy-done.2, bf16[128,512]{1,0:T(8,128)(2,1)S(1)} %copy-done.8, bf16[128,512]{1,0:T(8,128)(2,1)S(1)} %collective-permute-done.cot2_ref, ...), custom_call_target="tpu_custom_call" | custom-call | tf_op jit(solution)/shard_map/base_other/pallas_call | solution.py:367
  150.1 1.3 copy-done.6
  151.4 0.8 copy-done.10
  152.2 0.7 slice_bitcast_fusion
  153.0 2.5 %collective-permute-start.11 = (f32[128,512]{1,0:T(8,128)}, f32[128,512]{1,0:T(8,128)}, u32[]{:S(2)}, u32[]{:S(2)}) collective-permute-start(f32[128,512]{1,0:T(8,128)} %slice_bitcast_fusion), channel_id=1, source_target_pairs={{0,1},{1,0},{2,3},{3,2},{4,5},{5,4},{6,7},{7,6},{8,9},{9,8},{10,11... | collective-permute-start | bytes 786440 | tf_op jit(solution)/shard_map/ppermute | solution.py:266
  155.5 0.6 slice_bitcast_fusion.1
  156.1 0.1 copy.13.key_ref
  156.2 0.8 copy-done.13
  157.0 3.6 %gradients.1 = (f32[256,4096]{1,0:T(8,128)}, f32[256,512]{1,0:T(8,128)}) custom-call(bf16[1024,1280]{1,0:T(8,128)(2,1)S(1)} %bitcast.31, f32[256,128]{1,0:T(8,128)S(1)} %get-tuple-element.22.refs_0_.refs_1_, f32[256,128]{1,0:T(8,128)S(1)} %collective-permute-done.1.refs_1_.refs_2_, bf16[256,128]{1,0:T(8,128)(2,1)S(1)} %copy-done.13), custom_call_target="tpu_custom_call" | custom-call | tf_op jit(solution)/shard_map/gradients/pallas_call | solution.py:346
  160.7 5.7 %collective-permute-done.11 = f32[128,512]{1,0:T(8,128)} collective-permute-done((f32[128,512]{1,0:T(8,128)}, f32[128,512]{1,0:T(8,128)}, u32[]{:S(2)}, u32[]{:S(2)}) %collective-permute-start.11) | collective-permute-done | bytes 262176 | tf_op jit(solution)/shard_map/ppermute | solution.py:266
  166.4 1.0 bitcast_add_fusion.frozen_ref
  167.4 10.0 %all-to-all-done.1 = bf16[128,8,1152]{2,1,0:T(8,128)(2,1)} async-done(((bf16[128,8,1152]{2,1,0:T(8,128)(2,1)}), bf16[128,8,1152]{2,1,0:T(8,128)(2,1)}, u32[]{:S(2)}, u32[]{:S(2)}) %all-to-all-start.1) | async-done | bytes 2359328 | tf_op jit(solution)/shard_map/all_to_all | solution.py:344
  177.3 1.6 copy-done.7
  178.9 4.5 %finish.1 = (bf16[128,4096]{1,0:T(8,128)(2,1)}, bf16[128,512]{1,0:T(8,128)(2,1)}) custom-call(s32[128,1]{1,0:T(8,128)S(1)} %copy.13.key_ref, bf16[1024,1152]{1,0:T(8,128)(2,1)} %bitcast.11.got_ref, f32[128,4096]{1,0:T(8,128)S(1)} %copy-done.7, f32[128,512]{1,0:T(8,128)S(1)} %bitcast_add_fusion.frozen_ref, f32[1,512]{1,0:T(1,128)S(1)} %bitcast.37), custom_call_target="tpu_custom_call" | custom-call | tf_op jit(solution)/shard_map/finish/pallas_call | solution.py:388
  (35 shorter events, 0.1 us)
Async XLA Ops:
  7.2 47.5 %all-gather.6.cloned.1.call-start = ((), (), s32[]{:S(2)}) async-start(), calls=%async_computation.3 | async-start | bytes 1114112 | tf_op jit(solution)/shard_map/all_gather | solution.py:300
  7.9 8.3 %collective-permute-start = (bf16[128,512]{1,0:T(8,128)(2,1)}, bf16[128,512]{1,0:T(8,128)(2,1)S(1)}, u32[]{:S(2)}, u32[]{:S(2)}) collective-permute-start(bf16[128,512]{1,0:T(8,128)(2,1)} %cot_ref.5), channel_id=1, source_target_pairs={{0,1},{1,0},{2,3},{3,2},{4,5},{5,4},{6,7},{7,6},{8,9},{9,8},{10,11... | collective-permute-start | bytes 393224 | tf_op jit(solution)/shard_map/ppermute | solution.py:266
  16.3 80.7 %all-to-all-start = ((bf16[128,8,1280]{2,1,0:T(8,128)(2,1)}), bf16[128,8,1280]{2,1,0:T(8,128)(2,1)S(1)}, u32[]{:S(2)}, u32[]{:S(2)}) async-start(bf16[128,8,1280]{2,1,0:T(8,128)(2,1)} %bitcast.38), calls=%async_computation | async-start | bytes 5242880 | tf_op jit(solution)/shard_map/all_to_all | solution.py:298
  28.8 106.9 %all-gather.4.cloned.1.call-start = ((), (), s32[]{:S(2)}) async-start(), calls=%async_computation.2 | async-start | bytes 3932160 | tf_op jit(solution)/shard_map/all_gather | solution.py:305
  54.7 42.2 %copy-start.9 = (bf16[4,64,512]{2,1,0:T(8,128)(2,1)S(1)}, bf16[4,64,512]{2,1,0:T(8,128)(2,1)}, u32[]{:S(2)}) copy-start(bf16[4,64,512]{2,1,0:T(8,128)(2,1)} %param.12) | copy-start | bytes 786436
  55.8 26.5 %copy-start.15 = (bf16[64,4096]{1,0:T(8,128)(2,1)}, bf16[64,4096]{1,0:T(8,128)(2,1)S(1)}, u32[]{:S(2)}) copy-start(bf16[64,4096]{1,0:T(8,128)(2,1)S(1)} %dynamic-slice_bitcast_fusion) | copy-start | bytes 1572868
  55.8 24.7 %collective-permute-start.2 = (bf16[64,4096]{1,0:T(8,128)(2,1)S(1)}, bf16[64,4096]{1,0:T(8,128)(2,1)S(1)}, u32[]{:S(2)}, u32[]{:S(2)}) collective-permute-start(bf16[64,4096]{1,0:T(8,128)(2,1)S(1)} %dynamic-slice_bitcast_fusion), channel_id=1, source_target_pairs={{0,32},{32,0},{1,33},{33,1},{2,34},{34,2},{3,35},{35,3},{4,36},{36... | collective-permute-start | bytes 1572872 | tf_op jit(solution)/shard_map/ppermute | solution.py:266
  80.5 0.8 copy-start.16
  83.3 29.2 %collective-permute-start.3 = (bf16[128,1024]{1,0:T(8,128)(2,1)S(1)}, bf16[128,1024]{1,0:T(8,128)(2,1)}, u32[]{:S(2)}, u32[]{:S(2)}) collective-permute-start(bf16[128,1024]{1,0:T(8,128)(2,1)S(1)} %pad_maximum_fusion.1.rest_1_), channel_id=1, source_target_pairs={{0,64},{64,128},{128,192},{192,0},{1,65},{65,129},{129,193},{193,1... | collective-permute-start | bytes 786440 | tf_op jit(solution)/shard_map/ppermute | solution.py:262
  85.6 26.9 %collective-permute-start.4 = (bf16[128,1024]{1,0:T(8,128)(2,1)S(1)}, bf16[128,1024]{1,0:T(8,128)(2,1)}, u32[]{:S(2)}, u32[]{:S(2)}) collective-permute-start(bf16[128,1024]{1,0:T(8,128)(2,1)S(1)} %pad_maximum_fusion.1.rest_1_), channel_id=1, source_target_pairs={{0,128},{64,192},{128,0},{192,64},{1,129},{65,193},{129,1},{193,65... | collective-permute-start | bytes 786440 | tf_op jit(solution)/shard_map/ppermute | solution.py:262
  87.1 25.4 %collective-permute-start.5 = (bf16[128,1024]{1,0:T(8,128)(2,1)S(1)}, bf16[128,1024]{1,0:T(8,128)(2,1)}, u32[]{:S(2)}, u32[]{:S(2)}) collective-permute-start(bf16[128,1024]{1,0:T(8,128)(2,1)S(1)} %pad_maximum_fusion.1.rest_1_), channel_id=1, source_target_pairs={{0,192},{64,0},{128,64},{192,128},{1,193},{65,1},{129,65},{193,129... | collective-permute-start | bytes 786440 | tf_op jit(solution)/shard_map/ppermute | solution.py:262
  96.9 1.6 copy-start.3
  98.5 9.8 %copy-start.4 = (bf16[4096,4,64]{0,2,1:T(8,128)(2,1)S(1)}, bf16[4096,4,64]{0,2,1:T(8,128)(2,1)}, u32[]{:S(2)}) copy-start(bf16[4096,4,64]{0,2,1:T(8,128)(2,1)} %param.11) | copy-start | bytes 6291460
  101.6 9.5 %copy-start.12 = (bf16[256,128]{1,0:T(8,128)(2,1)}, bf16[256,128]{1,0:T(8,128)(2,1)S(1)}, u32[]{:S(2)}) copy-start(bf16[256,128]{1,0:T(8,128)(2,1)S(1)} %get-tuple-element.23.refs_2_.refs_3_) | copy-start | bytes 196612
  101.6 6.7 %collective-permute-start.1 = (f32[256,128]{1,0:T(8,128)S(1)}, f32[256,128]{1,0:T(8,128)S(1)}, u32[]{:S(2)}, u32[]{:S(2)}) collective-permute-start(f32[256,128]{1,0:T(8,128)S(1)} %get-tuple-element.22.refs_0_.refs_1_), channel_id=1, source_target_pairs={{0,1},{1,0},{2,3},{3,2},{4,5},{5,4},{6,7},{7,6},{8,9},{9,8},{10,11... | collective-permute-start | bytes 393224 | tf_op jit(solution)/shard_map/ppermute | solution.py:266
  111.1 1.4 copy-start
  112.5 24.4 %copy-start.8 = (bf16[128,512]{1,0:T(8,128)(2,1)S(1)}, bf16[128,512]{1,0:T(8,128)(2,1)}, u32[]{:S(2)}) copy-start(bf16[128,512]{1,0:T(8,128)(2,1)} %cot_ref.5) | copy-start | bytes 393220
  112.5 64.8 %all-to-all-start.1 = ((bf16[128,8,1152]{2,1,0:T(8,128)(2,1)}), bf16[128,8,1152]{2,1,0:T(8,128)(2,1)}, u32[]{:S(2)}, u32[]{:S(2)}) async-start(bf16[128,8,1152]{2,1,0:T(8,128)(2,1)} %bitcast.32), calls=%async_computation.1 | async-start | bytes 4718592 | tf_op jit(solution)/shard_map/all_to_all | solution.py:344
  135.8 9.0 %collective-permute-start.6 = (bf16[512,3072]{1,0:T(8,128)(2,1)}, bf16[512,3072]{1,0:T(8,128)(2,1)}, u32[]{:S(2)}, u32[]{:S(2)}) collective-permute-start(bf16[512,3072]{1,0:T(8,128)(2,1)} %all-gather.4.cloned.1.call-done.rest_0_), channel_id=1, source_target_pairs={{0,2},{2,0},{1,3},{3,1},{4,6},{6,4},{5,7},{7,5},{8,10},{10,8},{9,1... | collective-permute-start | bytes 9437192 | tf_op jit(solution)/shard_map/ppermute | solution.py:266
  135.8 8.9 %collective-permute-start.7 = (bf16[128,1024]{1,0:T(8,128)(2,1)S(1)}, bf16[128,1024]{1,0:T(8,128)(2,1)}, u32[]{:S(2)}, u32[]{:S(2)}) collective-permute-start(bf16[128,1024]{1,0:T(8,128)(2,1)S(1)} %pad_maximum_fusion.1.rest_1_), channel_id=1, source_target_pairs={{0,2},{2,0},{1,3},{3,1},{4,6},{6,4},{5,7},{7,5},{8,10},{10,8},{9,1... | collective-permute-start | bytes 786440 | tf_op jit(solution)/shard_map/ppermute | solution.py:266
  136.3 8.4 %collective-permute-start.10 = (bf16[128,1024]{1,0:T(8,128)(2,1)}, bf16[128,1024]{1,0:T(8,128)(2,1)}, u32[]{:S(2)}, u32[]{:S(2)}) collective-permute-start(bf16[128,1024]{1,0:T(8,128)(2,1)} %collective-permute-done.5.rest_4_), channel_id=1, source_target_pairs={{0,2},{2,0},{1,3},{3,1},{4,6},{6,4},{5,7},{7,5},{8,10},{10,8},{9,1... | collective-permute-start | bytes 786440 | tf_op jit(solution)/shard_map/ppermute | solution.py:266
  136.3 8.4 %collective-permute-start.8 = (bf16[128,1024]{1,0:T(8,128)(2,1)}, bf16[128,1024]{1,0:T(8,128)(2,1)}, u32[]{:S(2)}, u32[]{:S(2)}) collective-permute-start(bf16[128,1024]{1,0:T(8,128)(2,1)} %collective-permute-done.3.rest_2_), channel_id=1, source_target_pairs={{0,2},{2,0},{1,3},{3,1},{4,6},{6,4},{5,7},{7,5},{8,10},{10,8},{9,1... | collective-permute-start | bytes 786440 | tf_op jit(solution)/shard_map/ppermute | solution.py:266
  136.8 7.9 %collective-permute-start.9 = (bf16[128,1024]{1,0:T(8,128)(2,1)}, bf16[128,1024]{1,0:T(8,128)(2,1)}, u32[]{:S(2)}, u32[]{:S(2)}) collective-permute-start(bf16[128,1024]{1,0:T(8,128)(2,1)} %collective-permute-done.4.rest_3_), channel_id=1, source_target_pairs={{0,2},{2,0},{1,3},{3,1},{4,6},{6,4},{5,7},{7,5},{8,10},{10,8},{9,1... | collective-permute-start | bytes 786440 | tf_op jit(solution)/shard_map/ppermute | solution.py:266
  136.9 1.2 copy-start.1
  138.2 1.9 copy-start.5
  140.1 4.7 %copy-start.2 = (bf16[128,4096]{1,0:T(8,128)(2,1)S(1)}, bf16[128,4096]{1,0:T(8,128)(2,1)}, u32[]{:S(2)}) copy-start(bf16[128,4096]{1,0:T(8,128)(2,1)} %tok_ref.5) | copy-start | bytes 3145732
  150.1 1.4 copy-start.6
  151.4 0.8 copy-start.10
  151.4 25.9 %copy-start.14 = (f32[512]{0:T(512)S(1)}, f32[512]{0:T(512)}, u32[]{:S(2)}) copy-start(f32[512]{0:T(512)} %param.10) | copy-start | bytes 6148
  153.0 13.4 %copy-start.11 = (f32[2,128,512]{2,1,0:T(8,128)S(1)}, f32[2,128,512]{2,1,0:T(8,128)}, u32[]{:S(2)}) copy-start(f32[2,128,512]{2,1,0:T(8,128)} %copy-done.10) | copy-start | bytes 1572868
  153.0 13.4 %collective-permute-start.11 = (f32[128,512]{1,0:T(8,128)}, f32[128,512]{1,0:T(8,128)}, u32[]{:S(2)}, u32[]{:S(2)}) collective-permute-start(f32[128,512]{1,0:T(8,128)} %slice_bitcast_fusion), channel_id=1, source_target_pairs={{0,1},{1,0},{2,3},{3,2},{4,5},{5,4},{6,7},{7,6},{8,9},{9,8},{10,11... | collective-permute-start | bytes 786440 | tf_op jit(solution)/shard_map/ppermute | solution.py:266
  156.2 0.8 copy-start.13
  177.3 1.6 copy-start.7
Sparse Core Ops, SparseCore 0:
  9.8 44.8 all-gather.5
  82.4 53.2 all-gather.3

commit v4 on v3

--- a/solution.py
+++ b/solution.py
@@ -16,7 +16,7 @@
 OWNERS = SPLIT[0] * SPLIT[1] * SPLIT[2] * SPLIT[3]
 VMEM = pl.BlockSpec(memory_space=pltpu.VMEM)
 HBM = pl.BlockSpec(memory_space=pltpu.HBM)
-PARAMS = pltpu.CompilerParams(vmem_limit_bytes=40 * 1024 * 1024)
+PARAMS = pltpu.CompilerParams(vmem_limit_bytes=20 * 1024 * 1024)
 WHOLE = pltpu.CompilerParams(vmem_limit_bytes=60 * 1024 * 1024)
 
 
@@ -39,18 +39,16 @@
     return copies
 
 
-def pack_kernel(task_ref, slot_ref, tok_ref, cot_ref, out_ref, code_ref, stack, block, sems, out_sems):
+def pack_kernel(task_ref, slot_ref, tok_ref, cot_ref, out_ref, code_ref, stack, block, out_sems):
     rows, width = tok_ref.shape
     tasks_all = slot_ref.shape[1]
     tw, cw = width // GROUPS, cot_ref.shape[1] // GROUPS
     chunk = out_ref.shape[0] // OWNERS
     task_dev = tasks_all // OWNERS
-    pairs = []
     for g in range(GROUPS):
-        at = pl.ds(g * rows, rows)
-        pairs.append((tok_ref.at[:, pl.ds(g * tw, tw)], stack.at[at, pl.ds(0, tw)]))
-        pairs.append((cot_ref.at[:, pl.ds(g * cw, cw)], stack.at[at, pl.ds(tw, cw)]))
-    incoming = fetch(pairs, sems)
+        at = slice(g * rows, (g + 1) * rows)
+        stack[at, :tw] = tok_ref[:, g * tw:(g + 1) * tw]
+        stack[at, tw:tw + cw] = cot_ref[:, g * cw:(g + 1) * cw]
     slots = slot_ref[...]
     halves = jnp.concatenate([slots // task_dev, slots % task_dev] + [slots * 0] * 6, axis=0)
     blocks = task_ref.shape[1]
@@ -67,8 +65,6 @@
     code_ref[...] = code
     step = out_ref.shape[0] // 4
     copies = []
-    for copy in incoming:
-        copy.wait()
     for b in range(4):
         part = slice(b * step, (b + 1) * step)
         hit = one(iota((step, GROUPS * rows), 0) + b * step == code)
@@ -122,15 +118,15 @@
             label[at, :] = block[:per, tw + cw:]
 
 
-def owner_in_kernel(tasks, got_ref, down_ref, up_ref, low_ref, label_ref, rows, cots, down, sem):
+def rows_kernel(got_ref, rows_ref, cots_ref, label_ref):
+    rows_of(got_ref, rows_ref, cots_ref, label_ref)
+
+
+def low_kernel(tasks, rows_ref, cots_ref, label_ref, down_ref, up_ref, low_ref):
     rank = down_ref.shape[0] // tasks
-    copy = pltpu.make_async_copy(down_ref, down, sem)
-    copy.start()
-    rows_of(got_ref, rows, cots, label_ref)
     label = label_ref[...].astype(f32)[:, :rank]
-    low_ref[:, rank:] = collapse(dot(cots[...], up_ref[...], 1, 1), label, tasks, rank)
-    copy.wait()
-    low_ref[:, :rank] = collapse(dot(rows[...], down[...], 1, 1), label, tasks, rank)
+    low_ref[:, rank:] = collapse(dot(cots_ref[...], up_ref[...], 1, 1), label, tasks, rank)
+    low_ref[:, :rank] = collapse(dot(rows_ref[...], down_ref[...], 1, 1), label, tasks, rank)
 
 
 def wide_lows(tasks, rank, mine_ref, other_ref, label_ref):
@@ -236,25 +232,20 @@
         grad_ref[:, cols] = total
 
 
-def finish_kernel(key_ref, got_ref, base_ref, frozen_ref, bias_ref, grad_ref, proj_ref):
-    rows, width = grad_ref.shape
-    key_part = proj_ref.shape[1]
-    tw, cw = width // GROUPS, key_part // GROUPS
+def pick_kernel(key_ref, got_ref, found_ref):
+    rows = key_ref.shape[0]
     key = jnp.concatenate([key_ref[...] + g for g in range(GROUPS)], axis=0)
     pick = one(key == iota((GROUPS * rows, got_ref.shape[0]), 1))
     step = 384
-    for t in range((tw + cw) // step):
-        found = dot(pick, got_ref[:, t * step:(t + 1) * step])
-        keep = min(tw - t * step, step)
-        for g in range(GROUPS):
-            piece = found[g * rows:(g + 1) * rows, :]
-            cols = slice(g * tw + t * step, g * tw + t * step + keep)
-            grad_ref[:, cols] = (base_ref[:, cols] + piece[:, :keep]).astype(bf16)
-            if keep < step:
-                keys = slice(g * cw, (g + 1) * cw)
-                proj_ref[:, keys] = (
-                    frozen_ref[:, keys] + bias_ref[:, keys] + piece[:, keep:]
-                ).astype(bf16)
+    for t in range(found_ref.shape[1] // step):
+        cols = slice(t * step, (t + 1) * step)
+        found_ref[:, cols] = dot(pick, got_ref[:, cols])
+
+
+def finish_kernel(found_ref, base_ref, frozen_ref, bias_ref, grad_ref, proj_ref):
+    tw = grad_ref.shape[1]
+    grad_ref[...] = (base_ref[...] + found_ref[:, :tw]).astype(bf16)
+    proj_ref[...] = (frozen_ref[...] + bias_ref[...] + found_ref[:, tw:]).astype(bf16)
 
 
 def turn(value, shift):
@@ -283,18 +274,17 @@
             jax.ShapeDtypeStruct((sent_rows, tw + cw + 128), bf16),
             jax.ShapeDtypeStruct((1, GROUPS * rows_dev), jnp.int32),
         ),
-        in_specs=[VMEM, VMEM, HBM, HBM],
+        in_specs=[VMEM] * 4,
         out_specs=(HBM, VMEM),
         scratch_shapes=[
             pltpu.VMEM((GROUPS * rows_dev, tw + cw + 128), bf16),
             pltpu.VMEM((sent_rows, tw + cw + 128), bf16),
-            pltpu.SemaphoreType.DMA((2 * GROUPS,)),
             pltpu.SemaphoreType.DMA((4,)),
         ],
         compiler_params=WHOLE,
         name="pack",
     )(block_task[None, :], owner_slot[None, :], tokens, cotangent)
-    sent, other_cot = lax.optimization_barrier((sent, swap(cotangent, "seq")))
+    other_cot = swap(cotangent, "seq")
     got = lax.all_to_all(sent, SUB, split_axis=0, concat_axis=0, tiled=True)
 
     slab = lax.all_gather(weight, ("z", "c"), axis=0).reshape(SPLIT[2], 2, -1, half_width)
@@ -308,23 +298,26 @@
     down_t = adapter_down.transpose(1, 2, 0).reshape(task_dev * rank, half_width)
     up_t = adapter_up.reshape(task_dev * rank, key_part)
     owner_rows = owners * block_rows
-    low_mine, label_in = pl.pallas_call(
-        lambda *refs: owner_in_kernel(task_dev, *refs),
+    rows_in, cots_in, label_in = pl.pallas_call(
+        rows_kernel,
         out_shape=(
-            jax.ShapeDtypeStruct((owner_rows, 2 * rank), f32),
+            jax.ShapeDtypeStruct((owner_rows, half_width), bf16),
+            jax.ShapeDtypeStruct((owner_rows, key_part), bf16),
             jax.ShapeDtypeStruct((owner_rows, 128), bf16),
         ),
-        in_specs=[VMEM, HBM, VMEM],
-        out_specs=(VMEM,) * 2,
-        scratch_shapes=[
-            pltpu.VMEM((owner_rows, half_width), bf16),
-            pltpu.VMEM((owner_rows, key_part), bf16),
-            pltpu.VMEM(down_t.shape, bf16),
-            pltpu.SemaphoreType.DMA,
-        ],
+        in_specs=[VMEM],
+        out_specs=(VMEM,) * 3,
+        compiler_params=PARAMS,
+        name="owner_rows",
+    )(got)
+    low_mine = pl.pallas_call(
+        functools.partial(low_kernel, task_dev),
+        out_shape=jax.ShapeDtypeStruct((owner_rows, 2 * rank), f32),
+        in_specs=[VMEM] * 5,
+        out_specs=VMEM,
         compiler_params=PARAMS,
         name="owner_in",
-    )(got, down_t, up_t)
+    )(rows_in, cots_in, label_in, down_t, up_t)
     low_other = swap(low_mine, "seq")
     to_return = pl.pallas_call(
         lambda *refs: owner_out_kernel(task_dev, *refs),
@@ -337,7 +330,7 @@
             pltpu.VMEM((sent_rows, tw + cw), bf16),
             pltpu.SemaphoreType.DMA((4,)),
         ],
-        compiler_params=PARAMS,
+        compiler_params=pltpu.CompilerParams(vmem_limit_bytes=50 * 1024 * 1024),
         name="owner_out",
     )(low_mine, low_other, label_in, down_t, up_t)
     to_return, _ = lax.optimization_barrier((to_return, own[1:]))
@@ -385,17 +378,34 @@
     frozen = parts[0] + swap(parts[1], "seq")
 
     row_key = code[0, :rows_dev]
+    found = pl.pallas_call(
+        pick_kernel,
+        out_shape=jax.ShapeDtypeStruct((GROUPS * rows_dev, tw + cw), f32),
+        in_specs=[VMEM, VMEM],
+        out_specs=VMEM,
+        compiler_params=PARAMS,
+        name="pick",
+    )(row_key[:, None], returned)
     grad_tokens, projected = pl.pallas_call(
         finish_kernel,
         out_shape=(
             jax.ShapeDtypeStruct((rows_dev, half_width), bf16),
             jax.ShapeDtypeStruct((rows_dev, key_part), bf16),
         ),
-        in_specs=[VMEM] * 5,
-        out_specs=(VMEM, VMEM),
+        grid=(GROUPS,),
+        in_specs=[
+            pl.BlockSpec((rows_dev, tw + cw), lambda g: (g, 0)),
+            pl.BlockSpec((rows_dev, tw), lambda g: (0, g)),
+            pl.BlockSpec((rows_dev, cw), lambda g: (0, g)),
+            pl.BlockSpec((1, cw), lambda g: (0, g)),
+        ],
+        out_specs=(
+            pl.BlockSpec((rows_dev, tw), lambda g: (0, g)),
+            pl.BlockSpec((rows_dev, cw), lambda g: (0, g)),
+        ),
         compiler_params=PARAMS,
         name="finish",
-    )(row_key[:, None], returned, base_grad, frozen, bias[None, :])
+    )(found, base_grad, frozen, bias[None, :])
     return (projected, grad_tokens, down_gradient, up_gradient)
 
 

time: 191 us -> 186 us (0.974)
  local copies, waits for them, and re-layouts: 14.1 us -> 8.73 us
  starting transfers between devices: 36.5 us -> 39.4 us
    all_to_all x1, waiting for transfers between devices: 9.95 us -> 0.01 us  [on_device(): lax.all_to_all(to_return, SUB, split_axis=0, concat_axis=0, tiled=True)]
    all_gather x1, waiting for transfers between devices: 16.7 us -> 24.8 us  [on_device(): whole = lax.all_gather(slab[:, :cut], 'y', axis=0, tiled=True)]
    unnamed x34 -> x28, local copies, waits for them, and re-layouts: 11.5 us -> 6.92 us
    all_gather x1, waiting for transfers between devices: 25.8 us -> 29.1 us  [on_device(): lax.all_gather(weight, ('z', 'c'), axis=0)]
    pallas_call x1, Pallas kernels: 4.52 us -> 1.78 us  [on_device(): pl.pallas_call(finish_kernel, out_shape=(jax.ShapeDtypeStruct((rows_dev,...]
    pallas_call x1 -> x3, Pallas kernels: 3.07 us -> 5.37 us  [the longest x1 3.64 us: on_device(): pl.pallas_call(pick_kernel, out_shape=jax.ShapeDtypeStruct((GROUPS * rows...]
    ppermute x9, starting transfers between devices: 11 us -> 13.1 us  [swap(): return lax.ppermute(value, axis, [(0, 1), (1, 0)])]
    all_to_all x1, waiting for transfers between devices: 7.3 us -> 5.19 us  [on_device(): got = lax.all_to_all(sent, SUB, split_axis=0, concat_axis=0, tiled=True)]
  transfers between devices with their start and end apart: 16 -> 16, of which waited for: 7 -> 6; matrix products, arithmetic and copies ran while one was open for 3% -> 2% of each run, Pallas kernels for 13% -> 14%
where the time goes in v4:
time: 186 us; the launch traced here: 185 us
  waiting for transfers between devices  92.5 us (50%)
  starting transfers between devices  39.4 us (21%)
  Pallas kernels  28.1 us (15%)
  between operations  14.3 us (8%)
  local copies, waits for them, and re-layouts  8.73 us (5%)
  other arithmetic  2.09 us (1%)
    ppermute x9, waiting for transfers between devices, swap(): return lax.ppermute(value, axis, [(0, 1), (1, 0)])  32.8 us
    all_gather x1, waiting for transfers between devices, on_device(): lax.all_gather(weight, ('z', 'c'), axis=0)  29.1 us
    all_gather x1, waiting for transfers between devices, on_device(): whole = lax.all_gather(slab[:, :cut], 'y', axis=0, tiled=True)  24.8 us
    all_to_all x1, starting transfers between devices, on_device(): got = lax.all_to_all(sent, SUB, split_axis=0, concat_axis=0, tiled=True)  13.5 us
    ppermute x9, starting transfers between devices, swap(): return lax.ppermute(value, axis, [(0, 1), (1, 0)])  13.1 us
    pallas_call x2, Pallas kernels, on_device(): pl.pallas_call(functools.partial(base_kernel, flip), out_shape=(jax.Shape...  9.94 us
    unnamed x28, local copies, waits for them, and re-layouts  6.92 us
    all_to_all x1, starting transfers between devices, on_device(): lax.all_to_all(to_return, SUB, split_axis=0, concat_axis=0, tiled=True)  6.74 us
  transfers between devices with their start and end apart: 16, of which 6 were waited for; matrix products, arithmetic and copies ran while one was open for 2% of the time, Pallas kernels for 14%

profile of v4, /device:TPU:32, one launch (start us, length us, event | category | flops | bytes accessed | tf_op | source)
XLA Modules:
  0.0 185.1 jit_solution(11804343110420304635)
XLA Ops:
  7.2 0.0 all-gather.6.cloned.1.call-start
  7.2 0.7 all-gather.6.cloned.1.call-update
  7.9 4.8 %pack.1 = (bf16[1024,1280]{1,0:T(8,128)(2,1)}, s32[1,512]{1,0:T(1,128)}) custom-call(s32[1,64]{1,0:T(1,128)} %bitcast.41, s32[1,512]{1,0:T(1,128)} %bitcast.40, bf16[128,4096]{1,0:T(8,128)(2,1)} %tok_ref.5, bf16[128,512]{1,0:T(8,128)(2,1)} %cot_ref.5), custom_call_target="tpu_custom_call" | custom-call | tf_op jit(solution)/shard_map/pack/pallas_call | solution.py:271
  12.7 13.5 %all-to-all-start = ((bf16[128,8,1280]{2,1,0:T(8,128)(2,1)}), bf16[128,8,1280]{2,1,0:T(8,128)(2,1)S(1)}, u32[]{:S(2)}, u32[]{:S(2)}) async-start(bf16[128,8,1280]{2,1,0:T(8,128)(2,1)} %bitcast.38), calls=%async_computation | async-start | bytes 5242880 | tf_op jit(solution)/shard_map/all_to_all | solution.py:288
  26.2 0.0 all-gather.4.cloned.1.call-start
  26.3 29.1 %all-gather.6.cloned.1.call-done = bf16[128,4096]{1,0:T(8,128)(2,1)} async-done(((bf16[8,4096]{1,0:T(8,128)(2,1)}), bf16[128,4096]{1,0:T(8,128)(2,1)}) %all-gather.6.cloned.1.call-update) | async-done | bytes 1048592 | tf_op jit(solution)/shard_map/all_gather | solution.py:290
  55.4 1.1 dynamic-slice_bitcast_fusion
  56.5 1.6 collective-permute-start.1
  58.0 22.6 %collective-permute-done.1 = bf16[64,4096]{1,0:T(8,128)(2,1)S(1)} collective-permute-done((bf16[64,4096]{1,0:T(8,128)(2,1)S(1)}, bf16[64,4096]{1,0:T(8,128)(2,1)S(1)}, u32[]{:S(2)}, u32[]{:S(2)}) %collective-permute-start.1) | collective-permute-done | bytes 524320 | tf_op jit(solution)/shard_map/ppermute | solution.py:257
  80.7 0.8 copy-done.13
  81.5 0.9 pad_maximum_fusion
  82.4 0.0 all-gather.4.cloned.1.call-update
  82.4 1.0 pad_maximum_fusion.1.rest_1_
  83.5 1.6 collective-permute-start.2
  85.1 1.9 %collective-permute-start.3 = (bf16[128,1024]{1,0:T(8,128)(2,1)S(1)}, bf16[128,1024]{1,0:T(8,128)(2,1)}, u32[]{:S(2)}, u32[]{:S(2)}) collective-permute-start(bf16[128,1024]{1,0:T(8,128)(2,1)S(1)} %pad_maximum_fusion.1.rest_1_), channel_id=1, source_target_pairs={{0,128},{64,192},{128,0},{192,64},{1,129},{65,193},{129,1},{193,65... | collective-permute-start | bytes 786440 | tf_op jit(solution)/shard_map/ppermute | solution.py:253
  87.0 2.4 %collective-permute-start.4 = (bf16[128,1024]{1,0:T(8,128)(2,1)S(1)}, bf16[128,1024]{1,0:T(8,128)(2,1)}, u32[]{:S(2)}, u32[]{:S(2)}) collective-permute-start(bf16[128,1024]{1,0:T(8,128)(2,1)S(1)} %pad_maximum_fusion.1.rest_1_), channel_id=1, source_target_pairs={{0,192},{64,0},{128,64},{192,128},{1,193},{65,1},{129,65},{193,129... | collective-permute-start | bytes 786440 | tf_op jit(solution)/shard_map/ppermute | solution.py:253
  89.4 5.2 %all-to-all-done = bf16[128,8,1280]{2,1,0:T(8,128)(2,1)S(1)} async-done(((bf16[128,8,1280]{2,1,0:T(8,128)(2,1)}), bf16[128,8,1280]{2,1,0:T(8,128)(2,1)S(1)}, u32[]{:S(2)}, u32[]{:S(2)}) %all-to-all-start) | async-done | bytes 2621472 | tf_op jit(solution)/shard_map/all_to_all | solution.py:288
  94.6 0.8 owner_rows.1
  95.4 0.8 copy-done.1
  96.3 0.9 owner_in.1.refs_0_.refs_1_
  97.1 2.9 %collective-permute-start = (f32[256,128]{1,0:T(8,128)S(1)}, f32[256,128]{1,0:T(8,128)S(1)}, u32[]{:S(2)}, u32[]{:S(2)}) collective-permute-start(f32[256,128]{1,0:T(8,128)S(1)} %owner_in.1.refs_0_.refs_1_), channel_id=1, source_target_pairs={{0,1},{1,0},{2,3},{3,2},{4,5},{5,4},{6,7},{7,6},{8,9},{9,8},{10,11... | collective-permute-start | bytes 393224 | tf_op jit(solution)/shard_map/ppermute | solution.py:257
  100.1 3.6 %collective-permute-done.refs_1_.refs_2_ = f32[256,128]{1,0:T(8,128)S(1)} collective-permute-done((f32[256,128]{1,0:T(8,128)S(1)}, f32[256,128]{1,0:T(8,128)S(1)}, u32[]{:S(2)}, u32[]{:S(2)}) %collective-permute-start) | collective-permute-done | bytes 131104 | tf_op jit(solution)/shard_map/ppermute | solution.py:257
  103.7 2.6 %owner_out.1 = bf16[1024,1152]{1,0:T(8,128)(2,1)} custom-call(f32[256,128]{1,0:T(8,128)S(1)} %owner_in.1.refs_0_.refs_1_, f32[256,128]{1,0:T(8,128)S(1)} %collective-permute-done.refs_1_.refs_2_, bf16[256,128]{1,0:T(8,128)(2,1)S(1)} %get-tuple-element.22.label_ref.refs_2_.refs_3_, bf16[256,4096]{1,0:T(8,128)(2,1)S(1)} %bitcast.33, bf16[256,512]{1,0:T(8,128)(2,1)S(1)} %bitcast.35), custom_call_target="tpu_custom_call" | custom-call | tf_op jit(solution)/shard_map/owner_out/pallas_call | solution.py:322
  106.3 0.0 copy-start.5
  106.3 6.7 %all-to-all-start.1 = ((bf16[128,8,1152]{2,1,0:T(8,128)(2,1)}), bf16[128,8,1152]{2,1,0:T(8,128)(2,1)}, u32[]{:S(2)}, u32[]{:S(2)}) async-start(bf16[128,8,1152]{2,1,0:T(8,128)(2,1)} %bitcast.37), calls=%async_computation.1 | async-start | bytes 4718592 | tf_op jit(solution)/shard_map/all_to_all | solution.py:337
  113.1 24.8 %all-gather.4.cloned.1.call-done.rest_0_ = bf16[512,3072]{1,0:T(8,128)(2,1)} async-done(((bf16[128,3072]{1,0:T(8,128)(2,1)}), bf16[512,3072]{1,0:T(8,128)(2,1)}) %all-gather.4.cloned.1.call-update) | async-done | bytes 3145744 | tf_op jit(solution)/shard_map/all_gather | solution.py:295
  137.8 0.0 collective-permute-start.6
  137.9 4.0 %collective-permute-start.5 = (bf16[128,512]{1,0:T(8,128)(2,1)S(1)}, bf16[128,512]{1,0:T(8,128)(2,1)S(1)}, u32[]{:S(2)}, u32[]{:S(2)}) collective-permute-start(bf16[128,512]{1,0:T(8,128)(2,1)S(1)} %copy-done.5), channel_id=1, source_target_pairs={{0,1},{1,0},{2,3},{3,2},{4,5},{5,4},{6,7},{7,6},{8,9},{9,8},{10,11... | collective-permute-start | bytes 393224 | tf_op jit(solution)/shard_map/ppermute | solution.py:257
  141.9 0.2 collective-permute-start.7
  142.1 0.3 collective-permute-start.10
  142.4 0.2 collective-permute-start.8
  142.6 6.5 %collective-permute-done.5.cot2_ref = bf16[128,512]{1,0:T(8,128)(2,1)S(1)} collective-permute-done((bf16[128,512]{1,0:T(8,128)(2,1)S(1)}, bf16[128,512]{1,0:T(8,128)(2,1)S(1)}, u32[]{:S(2)}, u32[]{:S(2)}) %collective-permute-start.5) | collective-permute-done | bytes 131104 | tf_op jit(solution)/shard_map/ppermute | solution.py:257
  149.1 0.1 collective-permute-start.9
  149.2 0.1 pad_add_fusion.place_ref
  149.3 1.2 copy-done
  150.5 1.9 %copy-done.2 = bf16[512,3072]{1,0:T(8,128)(2,1)S(1)} copy-done((bf16[512,3072]{1,0:T(8,128)(2,1)S(1)}, bf16[512,3072]{1,0:T(8,128)(2,1)}, u32[]{:S(2)}) %copy-start.2) | copy-done | bytes 3145752
  152.4 4.6 %base_own.1 = (f32[2,128,512]{2,1,0:T(8,128)S(1)}, f32[128,4096]{1,0:T(8,128)S(1)}) custom-call(s32[4]{0:T(128)S(1)} %pad_add_fusion.place_ref, bf16[128,4096]{1,0:T(8,128)(2,1)S(1)} %copy-done, bf16[128,512]{1,0:T(8,128)(2,1)S(1)} %copy-done.5, bf16[128,512]{1,0:T(8,128)(2,1)S(1)} %collective-permute-done.5.cot2_ref, bf16[512,3072]{1,0:T(8,128)(2,1)S(1)} %copy-done.2, ...), custom_call_target="tpu_custom_call" | custom-call | tf_op jit(solution)/shard_map/base_own/pallas_call | solution.py:360
  157.1 0.0 copy-start.8
  157.1 5.3 %base_other.1 = (f32[2,128,512]{2,1,0:T(8,128)S(1)}, f32[128,4096]{1,0:T(8,128)S(1)}) custom-call(s32[4]{0:T(128)S(1)} %pad_add_fusion.place_ref, bf16[128,4096]{1,0:T(8,128)(2,1)S(1)} %copy-done, bf16[128,512]{1,0:T(8,128)(2,1)S(1)} %copy-done.5, bf16[128,512]{1,0:T(8,128)(2,1)S(1)} %collective-permute-done.5.cot2_ref, ...), custom_call_target="tpu_custom_call" | custom-call | tf_op jit(solution)/shard_map/base_other/pallas_call | solution.py:360
  162.4 1.3 copy-done.3
  163.8 0.8 copy-done.9
  164.6 3.8 %collective-permute-start.11 = (f32[128,512]{1,0:T(8,128)S(1)}, f32[128,512]{1,0:T(8,128)S(1)}, u32[]{:S(2)}, u32[]{:S(2)}) collective-permute-start(f32[128,512]{1,0:T(8,128)S(1)} %slice_bitcast_fusion), channel_id=1, source_target_pairs={{0,1},{1,0},{2,3},{3,2},{4,5},{5,4},{6,7},{7,6},{8,9},{9,8},{10,11... | collective-permute-start | bytes 786440 | tf_op jit(solution)/shard_map/ppermute | solution.py:257
  168.3 0.6 slice_bitcast_fusion.1
  169.0 0.1 copy.13.key_ref
  169.1 3.6 %gradients.1 = (f32[256,4096]{1,0:T(8,128)}, f32[256,512]{1,0:T(8,128)}) custom-call(bf16[1024,1280]{1,0:T(8,128)(2,1)S(1)} %bitcast.31, f32[256,128]{1,0:T(8,128)S(1)} %owner_in.1.refs_0_.refs_1_, f32[256,128]{1,0:T(8,128)S(1)} %copy-done.8, bf16[256,128]{1,0:T(8,128)(2,1)S(1)} %get-tuple-element.22.label_ref.refs_2_.refs_3_), custom_call_target="tpu_custom_call" | custom-call | tf_op jit(solution)/shard_map/gradients/pallas_call | solution.py:339
  172.7 0.0 copy-start.11
  172.7 3.6 %pick.1.found_ref = f32[512,1152]{1,0:T(8,128)S(1)} custom-call(s32[128,1]{1,0:T(8,128)S(1)} %copy.13.key_ref, bf16[1024,1152]{1,0:T(8,128)(2,1)} %bitcast.11.got_ref), custom_call_target="tpu_custom_call" | custom-call | tf_op jit(solution)/shard_map/pick/pallas_call | solution.py:381
  176.5 1.8 finish.1
  (31 shorter events, 0.1 us)
Async XLA Ops:
  7.2 48.2 %all-gather.6.cloned.1.call-start = ((), (), s32[]{:S(2)}) async-start(), calls=%async_computation.3 | async-start | bytes 1114112 | tf_op jit(solution)/shard_map/all_gather | solution.py:290
  12.7 81.8 %all-to-all-start = ((bf16[128,8,1280]{2,1,0:T(8,128)(2,1)}), bf16[128,8,1280]{2,1,0:T(8,128)(2,1)S(1)}, u32[]{:S(2)}, u32[]{:S(2)}) async-start(bf16[128,8,1280]{2,1,0:T(8,128)(2,1)} %bitcast.38), calls=%async_computation | async-start | bytes 5242880 | tf_op jit(solution)/shard_map/all_to_all | solution.py:288
  26.2 111.6 %all-gather.4.cloned.1.call-start = ((), (), s32[]{:S(2)}) async-start(), calls=%async_computation.2 | async-start | bytes 3932160 | tf_op jit(solution)/shard_map/all_gather | solution.py:295
  56.4 24.2 %copy-start.12 = (bf16[64,4096]{1,0:T(8,128)(2,1)}, bf16[64,4096]{1,0:T(8,128)(2,1)S(1)}, u32[]{:S(2)}) copy-start(bf16[64,4096]{1,0:T(8,128)(2,1)S(1)} %dynamic-slice_bitcast_fusion) | copy-start | bytes 1572868
  56.5 24.2 %collective-permute-start.1 = (bf16[64,4096]{1,0:T(8,128)(2,1)S(1)}, bf16[64,4096]{1,0:T(8,128)(2,1)S(1)}, u32[]{:S(2)}, u32[]{:S(2)}) collective-permute-start(bf16[64,4096]{1,0:T(8,128)(2,1)S(1)} %dynamic-slice_bitcast_fusion), channel_id=1, source_target_pairs={{0,32},{32,0},{1,33},{33,1},{2,34},{34,2},{3,35},{35,3},{4,36},{36... | collective-permute-start | bytes 1572872 | tf_op jit(solution)/shard_map/ppermute | solution.py:257
  80.7 0.8 copy-start.13
  82.4 13.0 %copy-start.6 = (bf16[4,64,512]{2,1,0:T(8,128)(2,1)S(1)}, bf16[4,64,512]{2,1,0:T(8,128)(2,1)}, u32[]{:S(2)}) copy-start(bf16[4,64,512]{2,1,0:T(8,128)(2,1)} %param.12) | copy-start | bytes 786436
  83.5 22.8 %collective-permute-start.2 = (bf16[128,1024]{1,0:T(8,128)(2,1)S(1)}, bf16[128,1024]{1,0:T(8,128)(2,1)}, u32[]{:S(2)}, u32[]{:S(2)}) collective-permute-start(bf16[128,1024]{1,0:T(8,128)(2,1)S(1)} %pad_maximum_fusion.1.rest_1_), channel_id=1, source_target_pairs={{0,64},{64,128},{128,192},{192,0},{1,65},{65,129},{129,193},{193,1... | collective-permute-start | bytes 786440 | tf_op jit(solution)/shard_map/ppermute | solution.py:253
  85.1 21.2 %collective-permute-start.3 = (bf16[128,1024]{1,0:T(8,128)(2,1)S(1)}, bf16[128,1024]{1,0:T(8,128)(2,1)}, u32[]{:S(2)}, u32[]{:S(2)}) collective-permute-start(bf16[128,1024]{1,0:T(8,128)(2,1)S(1)} %pad_maximum_fusion.1.rest_1_), channel_id=1, source_target_pairs={{0,128},{64,192},{128,0},{192,64},{1,129},{65,193},{129,1},{193,65... | collective-permute-start | bytes 786440 | tf_op jit(solution)/shard_map/ppermute | solution.py:253
  87.0 19.3 %collective-permute-start.4 = (bf16[128,1024]{1,0:T(8,128)(2,1)S(1)}, bf16[128,1024]{1,0:T(8,128)(2,1)}, u32[]{:S(2)}, u32[]{:S(2)}) collective-permute-start(bf16[128,1024]{1,0:T(8,128)(2,1)S(1)} %pad_maximum_fusion.1.rest_1_), channel_id=1, source_target_pairs={{0,192},{64,0},{128,64},{192,128},{1,193},{65,1},{129,65},{193,129... | collective-permute-start | bytes 786440 | tf_op jit(solution)/shard_map/ppermute | solution.py:253
  94.6 1.7 copy-start.1
  97.1 6.6 %collective-permute-start = (f32[256,128]{1,0:T(8,128)S(1)}, f32[256,128]{1,0:T(8,128)S(1)}, u32[]{:S(2)}, u32[]{:S(2)}) collective-permute-start(f32[256,128]{1,0:T(8,128)S(1)} %owner_in.1.refs_0_.refs_1_), channel_id=1, source_target_pairs={{0,1},{1,0},{2,3},{3,2},{4,5},{5,4},{6,7},{7,6},{8,9},{9,8},{10,11... | collective-permute-start | bytes 393224 | tf_op jit(solution)/shard_map/ppermute | solution.py:257
  103.7 2.6 %copy-start.7 = (f32[256,128]{1,0:T(8,128)}, f32[256,128]{1,0:T(8,128)S(1)}, u32[]{:S(2)}) copy-start(f32[256,128]{1,0:T(8,128)S(1)} %collective-permute-done.refs_1_.refs_2_) | copy-start | bytes 393220
  106.3 31.6 %copy-start.5 = (bf16[128,512]{1,0:T(8,128)(2,1)S(1)}, bf16[128,512]{1,0:T(8,128)(2,1)}, u32[]{:S(2)}) copy-start(bf16[128,512]{1,0:T(8,128)(2,1)} %cot_ref.5) | copy-start | bytes 393220
  106.3 66.4 %all-to-all-start.1 = ((bf16[128,8,1152]{2,1,0:T(8,128)(2,1)}), bf16[128,8,1152]{2,1,0:T(8,128)(2,1)}, u32[]{:S(2)}, u32[]{:S(2)}) async-start(bf16[128,8,1152]{2,1,0:T(8,128)(2,1)} %bitcast.37), calls=%async_computation.1 | async-start | bytes 4718592 | tf_op jit(solution)/shard_map/all_to_all | solution.py:337
  137.8 19.3 %collective-permute-start.6 = (bf16[512,3072]{1,0:T(8,128)(2,1)}, bf16[512,3072]{1,0:T(8,128)(2,1)}, u32[]{:S(2)}, u32[]{:S(2)}) collective-permute-start(bf16[512,3072]{1,0:T(8,128)(2,1)} %all-gather.4.cloned.1.call-done.rest_0_), channel_id=1, source_target_pairs={{0,2},{2,0},{1,3},{3,1},{4,6},{6,4},{5,7},{7,5},{8,10},{10,8},{9,1... | collective-permute-start | bytes 9437192 | tf_op jit(solution)/shard_map/ppermute | solution.py:257
  137.9 11.2 %collective-permute-start.5 = (bf16[128,512]{1,0:T(8,128)(2,1)S(1)}, bf16[128,512]{1,0:T(8,128)(2,1)S(1)}, u32[]{:S(2)}, u32[]{:S(2)}) collective-permute-start(bf16[128,512]{1,0:T(8,128)(2,1)S(1)} %copy-done.5), channel_id=1, source_target_pairs={{0,1},{1,0},{2,3},{3,2},{4,5},{5,4},{6,7},{7,6},{8,9},{9,8},{10,11... | collective-permute-start | bytes 393224 | tf_op jit(solution)/shard_map/ppermute | solution.py:257
  141.9 15.1 %collective-permute-start.7 = (bf16[128,1024]{1,0:T(8,128)(2,1)S(1)}, bf16[128,1024]{1,0:T(8,128)(2,1)}, u32[]{:S(2)}, u32[]{:S(2)}) collective-permute-start(bf16[128,1024]{1,0:T(8,128)(2,1)S(1)} %pad_maximum_fusion.1.rest_1_), channel_id=1, source_target_pairs={{0,2},{2,0},{1,3},{3,1},{4,6},{6,4},{5,7},{7,5},{8,10},{10,8},{9,1... | collective-permute-start | bytes 786440 | tf_op jit(solution)/shard_map/ppermute | solution.py:257
  142.1 15.0 %collective-permute-start.10 = (bf16[128,1024]{1,0:T(8,128)(2,1)}, bf16[128,1024]{1,0:T(8,128)(2,1)}, u32[]{:S(2)}, u32[]{:S(2)}) collective-permute-start(bf16[128,1024]{1,0:T(8,128)(2,1)} %collective-permute-done.4.rest_4_), channel_id=1, source_target_pairs={{0,2},{2,0},{1,3},{3,1},{4,6},{6,4},{5,7},{7,5},{8,10},{10,8},{9,1... | collective-permute-start | bytes 786440 | tf_op jit(solution)/shard_map/ppermute | solution.py:257
  142.4 14.6 %collective-permute-start.8 = (bf16[128,1024]{1,0:T(8,128)(2,1)}, bf16[128,1024]{1,0:T(8,128)(2,1)}, u32[]{:S(2)}, u32[]{:S(2)}) collective-permute-start(bf16[128,1024]{1,0:T(8,128)(2,1)} %collective-permute-done.2.rest_2_), channel_id=1, source_target_pairs={{0,2},{2,0},{1,3},{3,1},{4,6},{6,4},{5,7},{7,5},{8,10},{10,8},{9,1... | collective-permute-start | bytes 786440 | tf_op jit(solution)/shard_map/ppermute | solution.py:257
  149.1 8.0 %collective-permute-start.9 = (bf16[128,1024]{1,0:T(8,128)(2,1)}, bf16[128,1024]{1,0:T(8,128)(2,1)}, u32[]{:S(2)}, u32[]{:S(2)}) collective-permute-start(bf16[128,1024]{1,0:T(8,128)(2,1)} %collective-permute-done.3.rest_3_), channel_id=1, source_target_pairs={{0,2},{2,0},{1,3},{3,1},{4,6},{6,4},{5,7},{7,5},{8,10},{10,8},{9,1... | collective-permute-start | bytes 786440 | tf_op jit(solution)/shard_map/ppermute | solution.py:257
  149.3 1.2 copy-start
  150.5 1.9 %copy-start.2 = (bf16[512,3072]{1,0:T(8,128)(2,1)S(1)}, bf16[512,3072]{1,0:T(8,128)(2,1)}, u32[]{:S(2)}) copy-start(bf16[512,3072]{1,0:T(8,128)(2,1)} %all-gather.4.cloned.1.call-done.rest_0_) | copy-start | bytes 9437188
  157.1 12.0 %copy-start.8 = (f32[256,128]{1,0:T(8,128)S(1)}, f32[256,128]{1,0:T(8,128)}, u32[]{:S(2)}) copy-start(f32[256,128]{1,0:T(8,128)} %copy-done.7) | copy-start | bytes 393220
  162.4 1.4 copy-start.3
  163.8 0.8 copy-start.9
  164.6 11.8 %collective-permute-start.11 = (f32[128,512]{1,0:T(8,128)S(1)}, f32[128,512]{1,0:T(8,128)S(1)}, u32[]{:S(2)}, u32[]{:S(2)}) collective-permute-start(f32[128,512]{1,0:T(8,128)S(1)} %slice_bitcast_fusion), channel_id=1, source_target_pairs={{0,1},{1,0},{2,3},{3,2},{4,5},{5,4},{6,7},{7,6},{8,9},{9,8},{10,11... | collective-permute-start | bytes 786440 | tf_op jit(solution)/shard_map/ppermute | solution.py:257
  172.7 3.7 %copy-start.10 = (f32[2,128,512]{2,1,0:T(8,128)S(1)}, f32[2,128,512]{2,1,0:T(8,128)}, u32[]{:S(2)}) copy-start(f32[2,128,512]{2,1,0:T(8,128)} %copy-done.9) | copy-start | bytes 1572868
  172.7 3.7 %copy-start.4 = (f32[128,4096]{1,0:T(8,128)S(1)}, f32[128,4096]{1,0:T(8,128)}, u32[]{:S(2)}) copy-start(f32[128,4096]{1,0:T(8,128)} %copy-done.3) | copy-start | bytes 6291460
  172.7 3.7 %copy-start.11 = (f32[512]{0:T(512)S(1)}, f32[512]{0:T(512)}, u32[]{:S(2)}) copy-start(f32[512]{0:T(512)} %param.10) | copy-start | bytes 6148
Sparse Core Ops, SparseCore 0:
  9.8 45.4 all-gather.5
  82.5 55.2 all-gather.3

commit v5 on v4

--- a/solution.py
+++ b/solution.py
@@ -232,14 +232,18 @@
         grad_ref[:, cols] = total
 
 
-def pick_kernel(key_ref, got_ref, found_ref):
+def pick_kernel(key_ref, got_ref, found_ref, got, sems):
     rows = key_ref.shape[0]
+    count = sems.shape[0]
+    step = found_ref.shape[1] // count
+    tiles = [pl.ds(t * step, step) for t in range(count)]
+    copies = fetch([(got_ref.at[:, c], got.at[:, c]) for c in tiles], sems)
     key = jnp.concatenate([key_ref[...] + g for g in range(GROUPS)], axis=0)
-    pick = one(key == iota((GROUPS * rows, got_ref.shape[0]), 1))
-    step = 384
-    for t in range(found_ref.shape[1] // step):
+    pick = one(key == iota((GROUPS * rows, got.shape[0]), 1))
+    for t in range(count):
         cols = slice(t * step, (t + 1) * step)
-        found_ref[:, cols] = dot(pick, got_ref[:, cols])
+        copies[t].wait()
+        found_ref[:, cols] = dot(pick, got[:, cols])
 
 
 def finish_kernel(found_ref, base_ref, frozen_ref, bias_ref, grad_ref, proj_ref):
@@ -381,8 +385,12 @@
     found = pl.pallas_call(
         pick_kernel,
         out_shape=jax.ShapeDtypeStruct((GROUPS * rows_dev, tw + cw), f32),
-        in_specs=[VMEM, VMEM],
+        in_specs=[VMEM, HBM],
         out_specs=VMEM,
+        scratch_shapes=[
+            pltpu.VMEM((sent_rows, tw + cw), bf16),
+            pltpu.SemaphoreType.DMA((3,)),
+        ],
         compiler_params=PARAMS,
         name="pick",
     )(row_key[:, None], returned)

time: 186 us -> 186 us (level)
  no operation moved by 1% of the time
where the time goes in v5:
time: 186 us; the launch traced here: 185 us
  waiting for transfers between devices  92.5 us (50%)
  starting transfers between devices  39.4 us (21%)
  Pallas kernels  27.9 us (15%)
  between operations  14.3 us (8%)
  local copies, waits for them, and re-layouts  8.73 us (5%)
  other arithmetic  2.09 us (1%)
    ppermute x9, waiting for transfers between devices, swap(): return lax.ppermute(value, axis, [(0, 1), (1, 0)])  32.8 us
    all_gather x1, waiting for transfers between devices, on_device(): lax.all_gather(weight, ('z', 'c'), axis=0)  29.1 us
    all_gather x1, waiting for transfers between devices, on_device(): whole = lax.all_gather(slab[:, :cut], 'y', axis=0, tiled=True)  24.8 us
    all_to_all x1, starting transfers between devices, on_device(): got = lax.all_to_all(sent, SUB, split_axis=0, concat_axis=0, tiled=True)  13.5 us
    ppermute x9, starting transfers between devices, swap(): return lax.ppermute(value, axis, [(0, 1), (1, 0)])  13.1 us
    pallas_call x2, Pallas kernels, on_device(): pl.pallas_call(functools.partial(base_kernel, flip), out_shape=(jax.Shape...  9.94 us
    unnamed x28, local copies, waits for them, and re-layouts  6.92 us
    all_to_all x1, starting transfers between devices, on_device(): lax.all_to_all(to_return, SUB, split_axis=0, concat_axis=0, tiled=True)  6.74 us
  transfers between devices with their start and end apart: 16, of which 6 were waited for; matrix products, arithmetic and copies ran while one was open for 2% of the time, Pallas kernels for 14%

profile of v5, /device:TPU:32, one launch (start us, length us, event | category | flops | bytes accessed | tf_op | source)
XLA Modules:
  0.0 184.9 jit_solution(6489949617606372005)
XLA Ops:
  7.2 0.0 all-gather.6.cloned.1.call-start
  7.2 0.7 all-gather.6.cloned.1.call-update
  7.9 4.8 %pack.1 = (bf16[1024,1280]{1,0:T(8,128)(2,1)}, s32[1,512]{1,0:T(1,128)}) custom-call(s32[1,64]{1,0:T(1,128)} %bitcast.41, s32[1,512]{1,0:T(1,128)} %bitcast.40, bf16[128,4096]{1,0:T(8,128)(2,1)} %tok_ref.5, bf16[128,512]{1,0:T(8,128)(2,1)} %cot_ref.5), custom_call_target="tpu_custom_call" | custom-call | tf_op jit(solution)/shard_map/pack/pallas_call | solution.py:275
  12.7 13.5 %all-to-all-start = ((bf16[128,8,1280]{2,1,0:T(8,128)(2,1)}), bf16[128,8,1280]{2,1,0:T(8,128)(2,1)S(1)}, u32[]{:S(2)}, u32[]{:S(2)}) async-start(bf16[128,8,1280]{2,1,0:T(8,128)(2,1)} %bitcast.38), calls=%async_computation | async-start | bytes 5242880 | tf_op jit(solution)/shard_map/all_to_all | solution.py:292
  26.2 0.0 all-gather.4.cloned.1.call-start
  26.3 29.1 %all-gather.6.cloned.1.call-done = bf16[128,4096]{1,0:T(8,128)(2,1)} async-done(((bf16[8,4096]{1,0:T(8,128)(2,1)}), bf16[128,4096]{1,0:T(8,128)(2,1)}) %all-gather.6.cloned.1.call-update) | async-done | bytes 1048592 | tf_op jit(solution)/shard_map/all_gather | solution.py:294
  55.4 1.1 dynamic-slice_bitcast_fusion
  56.5 1.6 collective-permute-start.1
  58.0 22.6 %collective-permute-done.1 = bf16[64,4096]{1,0:T(8,128)(2,1)S(1)} collective-permute-done((bf16[64,4096]{1,0:T(8,128)(2,1)S(1)}, bf16[64,4096]{1,0:T(8,128)(2,1)S(1)}, u32[]{:S(2)}, u32[]{:S(2)}) %collective-permute-start.1) | collective-permute-done | bytes 524320 | tf_op jit(solution)/shard_map/ppermute | solution.py:261
  80.7 0.8 copy-done.13
  81.5 0.9 pad_maximum_fusion
  82.4 0.0 all-gather.4.cloned.1.call-update
  82.4 1.0 pad_maximum_fusion.1.rest_1_
  83.5 1.6 collective-permute-start.2
  85.1 1.9 %collective-permute-start.3 = (bf16[128,1024]{1,0:T(8,128)(2,1)S(1)}, bf16[128,1024]{1,0:T(8,128)(2,1)}, u32[]{:S(2)}, u32[]{:S(2)}) collective-permute-start(bf16[128,1024]{1,0:T(8,128)(2,1)S(1)} %pad_maximum_fusion.1.rest_1_), channel_id=1, source_target_pairs={{0,128},{64,192},{128,0},{192,64},{1,129},{65,193},{129,1},{193,65... | collective-permute-start | bytes 786440 | tf_op jit(solution)/shard_map/ppermute | solution.py:257
  87.0 2.4 %collective-permute-start.4 = (bf16[128,1024]{1,0:T(8,128)(2,1)S(1)}, bf16[128,1024]{1,0:T(8,128)(2,1)}, u32[]{:S(2)}, u32[]{:S(2)}) collective-permute-start(bf16[128,1024]{1,0:T(8,128)(2,1)S(1)} %pad_maximum_fusion.1.rest_1_), channel_id=1, source_target_pairs={{0,192},{64,0},{128,64},{192,128},{1,193},{65,1},{129,65},{193,129... | collective-permute-start | bytes 786440 | tf_op jit(solution)/shard_map/ppermute | solution.py:257
  89.4 5.2 %all-to-all-done = bf16[128,8,1280]{2,1,0:T(8,128)(2,1)S(1)} async-done(((bf16[128,8,1280]{2,1,0:T(8,128)(2,1)}), bf16[128,8,1280]{2,1,0:T(8,128)(2,1)S(1)}, u32[]{:S(2)}, u32[]{:S(2)}) %all-to-all-start) | async-done | bytes 2621472 | tf_op jit(solution)/shard_map/all_to_all | solution.py:292
  94.6 0.8 owner_rows.1
  95.4 0.8 copy-done.1
  96.3 0.9 owner_in.1.refs_0_.refs_1_
  97.1 2.9 %collective-permute-start = (f32[256,128]{1,0:T(8,128)S(1)}, f32[256,128]{1,0:T(8,128)S(1)}, u32[]{:S(2)}, u32[]{:S(2)}) collective-permute-start(f32[256,128]{1,0:T(8,128)S(1)} %owner_in.1.refs_0_.refs_1_), channel_id=1, source_target_pairs={{0,1},{1,0},{2,3},{3,2},{4,5},{5,4},{6,7},{7,6},{8,9},{9,8},{10,11... | collective-permute-start | bytes 393224 | tf_op jit(solution)/shard_map/ppermute | solution.py:261
  100.1 3.6 %collective-permute-done.refs_1_.refs_2_ = f32[256,128]{1,0:T(8,128)S(1)} collective-permute-done((f32[256,128]{1,0:T(8,128)S(1)}, f32[256,128]{1,0:T(8,128)S(1)}, u32[]{:S(2)}, u32[]{:S(2)}) %collective-permute-start) | collective-permute-done | bytes 131104 | tf_op jit(solution)/shard_map/ppermute | solution.py:261
  103.7 2.6 %owner_out.1 = bf16[1024,1152]{1,0:T(8,128)(2,1)} custom-call(f32[256,128]{1,0:T(8,128)S(1)} %owner_in.1.refs_0_.refs_1_, f32[256,128]{1,0:T(8,128)S(1)} %collective-permute-done.refs_1_.refs_2_, bf16[256,128]{1,0:T(8,128)(2,1)S(1)} %get-tuple-element.22.label_ref.refs_2_.refs_3_, bf16[256,4096]{1,0:T(8,128)(2,1)S(1)} %bitcast.33, bf16[256,512]{1,0:T(8,128)(2,1)S(1)} %bitcast.35), custom_call_target="tpu_custom_call" | custom-call | tf_op jit(solution)/shard_map/owner_out/pallas_call | solution.py:326
  106.3 0.0 copy-start.5
  106.3 6.7 %all-to-all-start.1 = ((bf16[128,8,1152]{2,1,0:T(8,128)(2,1)}), bf16[128,8,1152]{2,1,0:T(8,128)(2,1)}, u32[]{:S(2)}, u32[]{:S(2)}) async-start(bf16[128,8,1152]{2,1,0:T(8,128)(2,1)} %bitcast.37), calls=%async_computation.1 | async-start | bytes 4718592 | tf_op jit(solution)/shard_map/all_to_all | solution.py:341
  113.1 24.8 %all-gather.4.cloned.1.call-done.rest_0_ = bf16[512,3072]{1,0:T(8,128)(2,1)} async-done(((bf16[128,3072]{1,0:T(8,128)(2,1)}), bf16[512,3072]{1,0:T(8,128)(2,1)}) %all-gather.4.cloned.1.call-update) | async-done | bytes 3145744 | tf_op jit(solution)/shard_map/all_gather | solution.py:299
  137.8 0.0 collective-permute-start.6
  137.9 4.0 %collective-permute-start.5 = (bf16[128,512]{1,0:T(8,128)(2,1)S(1)}, bf16[128,512]{1,0:T(8,128)(2,1)S(1)}, u32[]{:S(2)}, u32[]{:S(2)}) collective-permute-start(bf16[128,512]{1,0:T(8,128)(2,1)S(1)} %copy-done.5), channel_id=1, source_target_pairs={{0,1},{1,0},{2,3},{3,2},{4,5},{5,4},{6,7},{7,6},{8,9},{9,8},{10,11... | collective-permute-start | bytes 393224 | tf_op jit(solution)/shard_map/ppermute | solution.py:261
  141.9 0.2 collective-permute-start.7
  142.1 0.3 collective-permute-start.10
  142.4 0.2 collective-permute-start.8
  142.6 6.5 %collective-permute-done.5.cot2_ref = bf16[128,512]{1,0:T(8,128)(2,1)S(1)} collective-permute-done((bf16[128,512]{1,0:T(8,128)(2,1)S(1)}, bf16[128,512]{1,0:T(8,128)(2,1)S(1)}, u32[]{:S(2)}, u32[]{:S(2)}) %collective-permute-start.5) | collective-permute-done | bytes 131104 | tf_op jit(solution)/shard_map/ppermute | solution.py:261
  149.1 0.1 collective-permute-start.9
  149.2 0.1 pad_add_fusion.place_ref
  149.3 1.2 copy-done
  150.5 1.9 %copy-done.2 = bf16[512,3072]{1,0:T(8,128)(2,1)S(1)} copy-done((bf16[512,3072]{1,0:T(8,128)(2,1)S(1)}, bf16[512,3072]{1,0:T(8,128)(2,1)}, u32[]{:S(2)}) %copy-start.2) | copy-done | bytes 3145752
  152.4 4.6 %base_own.1 = (f32[2,128,512]{2,1,0:T(8,128)S(1)}, f32[128,4096]{1,0:T(8,128)S(1)}) custom-call(s32[4]{0:T(128)S(1)} %pad_add_fusion.place_ref, bf16[128,4096]{1,0:T(8,128)(2,1)S(1)} %copy-done, bf16[128,512]{1,0:T(8,128)(2,1)S(1)} %copy-done.5, bf16[128,512]{1,0:T(8,128)(2,1)S(1)} %collective-permute-done.5.cot2_ref, bf16[512,3072]{1,0:T(8,128)(2,1)S(1)} %copy-done.2, ...), custom_call_target="tpu_custom_call" | custom-call | tf_op jit(solution)/shard_map/base_own/pallas_call | solution.py:364
  157.1 0.0 copy-start.8
  157.1 5.3 %base_other.1 = (f32[2,128,512]{2,1,0:T(8,128)S(1)}, f32[128,4096]{1,0:T(8,128)S(1)}) custom-call(s32[4]{0:T(128)S(1)} %pad_add_fusion.place_ref, bf16[128,4096]{1,0:T(8,128)(2,1)S(1)} %copy-done, bf16[128,512]{1,0:T(8,128)(2,1)S(1)} %copy-done.5, bf16[128,512]{1,0:T(8,128)(2,1)S(1)} %collective-permute-done.5.cot2_ref, ...), custom_call_target="tpu_custom_call" | custom-call | tf_op jit(solution)/shard_map/base_other/pallas_call | solution.py:364
  162.4 1.3 copy-done.3
  163.8 0.8 copy-done.9
  164.6 3.8 %collective-permute-start.11 = (f32[128,512]{1,0:T(8,128)S(1)}, f32[128,512]{1,0:T(8,128)S(1)}, u32[]{:S(2)}, u32[]{:S(2)}) collective-permute-start(f32[128,512]{1,0:T(8,128)S(1)} %slice_bitcast_fusion), channel_id=1, source_target_pairs={{0,1},{1,0},{2,3},{3,2},{4,5},{5,4},{6,7},{7,6},{8,9},{9,8},{10,11... | collective-permute-start | bytes 786440 | tf_op jit(solution)/shard_map/ppermute | solution.py:261
  168.3 0.6 slice_bitcast_fusion.1
  169.0 0.1 copy.13.key_ref
  169.1 3.6 %gradients.1 = (f32[256,4096]{1,0:T(8,128)}, f32[256,512]{1,0:T(8,128)}) custom-call(bf16[1024,1280]{1,0:T(8,128)(2,1)S(1)} %bitcast.31, f32[256,128]{1,0:T(8,128)S(1)} %owner_in.1.refs_0_.refs_1_, f32[256,128]{1,0:T(8,128)S(1)} %copy-done.8, bf16[256,128]{1,0:T(8,128)(2,1)S(1)} %get-tuple-element.22.label_ref.refs_2_.refs_3_), custom_call_target="tpu_custom_call" | custom-call | tf_op jit(solution)/shard_map/gradients/pallas_call | solution.py:343
  172.7 0.0 copy-start.11
  172.7 3.4 %pick.1.found_ref = f32[512,1152]{1,0:T(8,128)S(1)} custom-call(s32[128,1]{1,0:T(8,128)S(1)} %copy.13.key_ref, bf16[1024,1152]{1,0:T(8,128)(2,1)} %bitcast.11.got_ref), custom_call_target="tpu_custom_call" | custom-call | tf_op jit(solution)/shard_map/pick/pallas_call | solution.py:385
  176.3 1.8 finish.1
  (31 shorter events, 0.1 us)
Async XLA Ops:
  7.2 48.2 %all-gather.6.cloned.1.call-start = ((), (), s32[]{:S(2)}) async-start(), calls=%async_computation.3 | async-start | bytes 1114112 | tf_op jit(solution)/shard_map/all_gather | solution.py:294
  12.7 81.8 %all-to-all-start = ((bf16[128,8,1280]{2,1,0:T(8,128)(2,1)}), bf16[128,8,1280]{2,1,0:T(8,128)(2,1)S(1)}, u32[]{:S(2)}, u32[]{:S(2)}) async-start(bf16[128,8,1280]{2,1,0:T(8,128)(2,1)} %bitcast.38), calls=%async_computation | async-start | bytes 5242880 | tf_op jit(solution)/shard_map/all_to_all | solution.py:292
  26.2 111.6 %all-gather.4.cloned.1.call-start = ((), (), s32[]{:S(2)}) async-start(), calls=%async_computation.2 | async-start | bytes 3932160 | tf_op jit(solution)/shard_map/all_gather | solution.py:299
  56.4 24.2 %copy-start.12 = (bf16[64,4096]{1,0:T(8,128)(2,1)}, bf16[64,4096]{1,0:T(8,128)(2,1)S(1)}, u32[]{:S(2)}) copy-start(bf16[64,4096]{1,0:T(8,128)(2,1)S(1)} %dynamic-slice_bitcast_fusion) | copy-start | bytes 1572868
  56.5 24.2 %collective-permute-start.1 = (bf16[64,4096]{1,0:T(8,128)(2,1)S(1)}, bf16[64,4096]{1,0:T(8,128)(2,1)S(1)}, u32[]{:S(2)}, u32[]{:S(2)}) collective-permute-start(bf16[64,4096]{1,0:T(8,128)(2,1)S(1)} %dynamic-slice_bitcast_fusion), channel_id=1, source_target_pairs={{0,32},{32,0},{1,33},{33,1},{2,34},{34,2},{3,35},{35,3},{4,36},{36... | collective-permute-start | bytes 1572872 | tf_op jit(solution)/shard_map/ppermute | solution.py:261
  80.7 0.8 copy-start.13
  82.4 13.0 %copy-start.6 = (bf16[4,64,512]{2,1,0:T(8,128)(2,1)S(1)}, bf16[4,64,512]{2,1,0:T(8,128)(2,1)}, u32[]{:S(2)}) copy-start(bf16[4,64,512]{2,1,0:T(8,128)(2,1)} %param.12) | copy-start | bytes 786436
  83.5 22.8 %collective-permute-start.2 = (bf16[128,1024]{1,0:T(8,128)(2,1)S(1)}, bf16[128,1024]{1,0:T(8,128)(2,1)}, u32[]{:S(2)}, u32[]{:S(2)}) collective-permute-start(bf16[128,1024]{1,0:T(8,128)(2,1)S(1)} %pad_maximum_fusion.1.rest_1_), channel_id=1, source_target_pairs={{0,64},{64,128},{128,192},{192,0},{1,65},{65,129},{129,193},{193,1... | collective-permute-start | bytes 786440 | tf_op jit(solution)/shard_map/ppermute | solution.py:257
  85.1 21.2 %collective-permute-start.3 = (bf16[128,1024]{1,0:T(8,128)(2,1)S(1)}, bf16[128,1024]{1,0:T(8,128)(2,1)}, u32[]{:S(2)}, u32[]{:S(2)}) collective-permute-start(bf16[128,1024]{1,0:T(8,128)(2,1)S(1)} %pad_maximum_fusion.1.rest_1_), channel_id=1, source_target_pairs={{0,128},{64,192},{128,0},{192,64},{1,129},{65,193},{129,1},{193,65... | collective-permute-start | bytes 786440 | tf_op jit(solution)/shard_map/ppermute | solution.py:257
  87.0 19.3 %collective-permute-start.4 = (bf16[128,1024]{1,0:T(8,128)(2,1)S(1)}, bf16[128,1024]{1,0:T(8,128)(2,1)}, u32[]{:S(2)}, u32[]{:S(2)}) collective-permute-start(bf16[128,1024]{1,0:T(8,128)(2,1)S(1)} %pad_maximum_fusion.1.rest_1_), channel_id=1, source_target_pairs={{0,192},{64,0},{128,64},{192,128},{1,193},{65,1},{129,65},{193,129... | collective-permute-start | bytes 786440 | tf_op jit(solution)/shard_map/ppermute | solution.py:257
  94.6 1.7 copy-start.1
  97.1 6.6 %collective-permute-start = (f32[256,128]{1,0:T(8,128)S(1)}, f32[256,128]{1,0:T(8,128)S(1)}, u32[]{:S(2)}, u32[]{:S(2)}) collective-permute-start(f32[256,128]{1,0:T(8,128)S(1)} %owner_in.1.refs_0_.refs_1_), channel_id=1, source_target_pairs={{0,1},{1,0},{2,3},{3,2},{4,5},{5,4},{6,7},{7,6},{8,9},{9,8},{10,11... | collective-permute-start | bytes 393224 | tf_op jit(solution)/shard_map/ppermute | solution.py:261
  103.7 2.6 %copy-start.7 = (f32[256,128]{1,0:T(8,128)}, f32[256,128]{1,0:T(8,128)S(1)}, u32[]{:S(2)}) copy-start(f32[256,128]{1,0:T(8,128)S(1)} %collective-permute-done.refs_1_.refs_2_) | copy-start | bytes 393220
  106.3 31.6 %copy-start.5 = (bf16[128,512]{1,0:T(8,128)(2,1)S(1)}, bf16[128,512]{1,0:T(8,128)(2,1)}, u32[]{:S(2)}) copy-start(bf16[128,512]{1,0:T(8,128)(2,1)} %cot_ref.5) | copy-start | bytes 393220
  106.3 66.4 %all-to-all-start.1 = ((bf16[128,8,1152]{2,1,0:T(8,128)(2,1)}), bf16[128,8,1152]{2,1,0:T(8,128)(2,1)}, u32[]{:S(2)}, u32[]{:S(2)}) async-start(bf16[128,8,1152]{2,1,0:T(8,128)(2,1)} %bitcast.37), calls=%async_computation.1 | async-start | bytes 4718592 | tf_op jit(solution)/shard_map/all_to_all | solution.py:341
  137.8 19.3 %collective-permute-start.6 = (bf16[512,3072]{1,0:T(8,128)(2,1)}, bf16[512,3072]{1,0:T(8,128)(2,1)}, u32[]{:S(2)}, u32[]{:S(2)}) collective-permute-start(bf16[512,3072]{1,0:T(8,128)(2,1)} %all-gather.4.cloned.1.call-done.rest_0_), channel_id=1, source_target_pairs={{0,2},{2,0},{1,3},{3,1},{4,6},{6,4},{5,7},{7,5},{8,10},{10,8},{9,1... | collective-permute-start | bytes 9437192 | tf_op jit(solution)/shard_map/ppermute | solution.py:261
  137.9 11.2 %collective-permute-start.5 = (bf16[128,512]{1,0:T(8,128)(2,1)S(1)}, bf16[128,512]{1,0:T(8,128)(2,1)S(1)}, u32[]{:S(2)}, u32[]{:S(2)}) collective-permute-start(bf16[128,512]{1,0:T(8,128)(2,1)S(1)} %copy-done.5), channel_id=1, source_target_pairs={{0,1},{1,0},{2,3},{3,2},{4,5},{5,4},{6,7},{7,6},{8,9},{9,8},{10,11... | collective-permute-start | bytes 393224 | tf_op jit(solution)/shard_map/ppermute | solution.py:261
  141.9 15.1 %collective-permute-start.7 = (bf16[128,1024]{1,0:T(8,128)(2,1)S(1)}, bf16[128,1024]{1,0:T(8,128)(2,1)}, u32[]{:S(2)}, u32[]{:S(2)}) collective-permute-start(bf16[128,1024]{1,0:T(8,128)(2,1)S(1)} %pad_maximum_fusion.1.rest_1_), channel_id=1, source_target_pairs={{0,2},{2,0},{1,3},{3,1},{4,6},{6,4},{5,7},{7,5},{8,10},{10,8},{9,1... | collective-permute-start | bytes 786440 | tf_op jit(solution)/shard_map/ppermute | solution.py:261
  142.1 15.0 %collective-permute-start.10 = (bf16[128,1024]{1,0:T(8,128)(2,1)}, bf16[128,1024]{1,0:T(8,128)(2,1)}, u32[]{:S(2)}, u32[]{:S(2)}) collective-permute-start(bf16[128,1024]{1,0:T(8,128)(2,1)} %collective-permute-done.4.rest_4_), channel_id=1, source_target_pairs={{0,2},{2,0},{1,3},{3,1},{4,6},{6,4},{5,7},{7,5},{8,10},{10,8},{9,1... | collective-permute-start | bytes 786440 | tf_op jit(solution)/shard_map/ppermute | solution.py:261
  142.4 14.6 %collective-permute-start.8 = (bf16[128,1024]{1,0:T(8,128)(2,1)}, bf16[128,1024]{1,0:T(8,128)(2,1)}, u32[]{:S(2)}, u32[]{:S(2)}) collective-permute-start(bf16[128,1024]{1,0:T(8,128)(2,1)} %collective-permute-done.2.rest_2_), channel_id=1, source_target_pairs={{0,2},{2,0},{1,3},{3,1},{4,6},{6,4},{5,7},{7,5},{8,10},{10,8},{9,1... | collective-permute-start | bytes 786440 | tf_op jit(solution)/shard_map/ppermute | solution.py:261
  149.1 8.0 %collective-permute-start.9 = (bf16[128,1024]{1,0:T(8,128)(2,1)}, bf16[128,1024]{1,0:T(8,128)(2,1)}, u32[]{:S(2)}, u32[]{:S(2)}) collective-permute-start(bf16[128,1024]{1,0:T(8,128)(2,1)} %collective-permute-done.3.rest_3_), channel_id=1, source_target_pairs={{0,2},{2,0},{1,3},{3,1},{4,6},{6,4},{5,7},{7,5},{8,10},{10,8},{9,1... | collective-permute-start | bytes 786440 | tf_op jit(solution)/shard_map/ppermute | solution.py:261
  149.3 1.2 copy-start
  150.5 1.9 %copy-start.2 = (bf16[512,3072]{1,0:T(8,128)(2,1)S(1)}, bf16[512,3072]{1,0:T(8,128)(2,1)}, u32[]{:S(2)}) copy-start(bf16[512,3072]{1,0:T(8,128)(2,1)} %all-gather.4.cloned.1.call-done.rest_0_) | copy-start | bytes 9437188
  157.1 12.0 %copy-start.8 = (f32[256,128]{1,0:T(8,128)S(1)}, f32[256,128]{1,0:T(8,128)}, u32[]{:S(2)}) copy-start(f32[256,128]{1,0:T(8,128)} %copy-done.7) | copy-start | bytes 393220
  162.4 1.4 copy-start.3
  163.8 0.8 copy-start.9
  164.6 11.6 %collective-permute-start.11 = (f32[128,512]{1,0:T(8,128)S(1)}, f32[128,512]{1,0:T(8,128)S(1)}, u32[]{:S(2)}, u32[]{:S(2)}) collective-permute-start(f32[128,512]{1,0:T(8,128)S(1)} %slice_bitcast_fusion), channel_id=1, source_target_pairs={{0,1},{1,0},{2,3},{3,2},{4,5},{5,4},{6,7},{7,6},{8,9},{9,8},{10,11... | collective-permute-start | bytes 786440 | tf_op jit(solution)/shard_map/ppermute | solution.py:261
  172.7 3.5 %copy-start.10 = (f32[2,128,512]{2,1,0:T(8,128)S(1)}, f32[2,128,512]{2,1,0:T(8,128)}, u32[]{:S(2)}) copy-start(f32[2,128,512]{2,1,0:T(8,128)} %copy-done.9) | copy-start | bytes 1572868
  172.7 3.5 %copy-start.4 = (f32[128,4096]{1,0:T(8,128)S(1)}, f32[128,4096]{1,0:T(8,128)}, u32[]{:S(2)}) copy-start(f32[128,4096]{1,0:T(8,128)} %copy-done.3) | copy-start | bytes 6291460
  172.7 3.5 %copy-start.11 = (f32[512]{0:T(512)S(1)}, f32[512]{0:T(512)}, u32[]{:S(2)}) copy-start(f32[512]{0:T(512)} %param.10) | copy-start | bytes 6148
Sparse Core Ops, SparseCore 0:
  9.8 45.4 all-gather.5
  82.5 55.2 all-gather.3
